TPU v7x, 128 devices: a whole 4x4x4 slice. The times are simulated.
128 devices in a mesh: row: 8 (over x, core), col: 16 (over y, z).
Axes of the slice: x: 4, y: 4, z: 4, core: 2. Of those that a mesh axis runs over, the one named last changes fastest.
Arguments:
- features: bfloat16 [65536, 256], P(('row', 'col')), may hold values from -6 to 6
- weight: bfloat16 [256, 256], replicated, may hold values from -0.375 to 0.375
- cotangent: bfloat16 [65536, 256], P(('row', 'col')), may hold values from -6 to 6
- tile_values: bfloat16 [8, 16, 384, 128, 128], P('row', 'col'), may hold values from 0 to 0.15, as said below
- tile_rows: int32 [8, 16, 384], P('row', 'col'), may hold values from 0 to 63
- tile_cols: int32 [8, 16, 384], P('row', 'col'), may hold values from 0 to 31
- tile_count: int32 [8, 16], P('row', 'col'), may hold values from 96 to 384, as said below
Outputs:
- activated: bfloat16 [65536, 256], P(('row', 'col'))
- grad_features: bfloat16 [65536, 256], P(('row', 'col'))
- grad_weight: float32 [256, 256], replicated
Inputs may be any that keep to these rules, and one draw needn't show every extreme that they name: `tile_count`: some device in every draw has all 384 slots live. `tile_values`: each entry is zero or a positive edge weight.
All inputs are finite; a program needn't handle non-finite values.
Results may differ from a plain program's by a relative error of at most 0.006.
Values may be sent and summed in bfloat16 or wider, within the bound.
No kernel may reach another device: no remote copies, remote signals or barrier semaphores. Data moves between devices by JAX's collectives and lax.ppermute only.
A program may use at most 128 MiB of HBM per device.

v0:
```python
import jax
import jax.numpy as jnp
from jax import lax
from jax.sharding import PartitionSpec as P

GROUP = 48


def gelu_tanh(value):
    return jax.nn.gelu(value, approximate=True)


def aggregate(tile_vals, out_ids, in_ids, source, live_count, out_blocks, flipped, first_block):
    tile_size = tile_vals.shape[-1]
    feat_width = source.shape[1]
    per_group = GROUP
    group_total = tile_vals.shape[0] // per_group
    source_blocks = source.reshape(-1, tile_size, feat_width)
    pattern = "gba,gbf->gaf" if flipped else "gab,gbf->gaf"

    def one_group(group_idx, running):
        first_slot = group_idx * per_group
        vals_now = lax.dynamic_slice_in_dim(tile_vals, first_slot, per_group, 0)
        out_now = lax.dynamic_slice_in_dim(out_ids, first_slot, per_group, 0)
        in_now = lax.dynamic_slice_in_dim(in_ids, first_slot, per_group, 0)
        slot_ids = first_slot + jnp.arange(per_group, dtype=jnp.int32)
        picked = source_blocks[in_now]
        products = jnp.einsum(pattern, vals_now, picked, preferred_element_type=jnp.float32)
        target = out_now - first_block
        keep = (target >= 0) & (target < out_blocks) & (slot_ids < live_count)
        target = jnp.where(keep, target, out_blocks)
        return running.at[target].add(products, mode="drop")

    start = jnp.zeros((out_blocks, tile_size, feat_width), jnp.float32)
    running = lax.fori_loop(0, group_total, one_group, start)
    return running.reshape(out_blocks * tile_size, feat_width)


def per_device(features, weight, cotangent, tile_values, tile_rows, tile_cols, tile_count):
    tile_size = tile_values.shape[-1]
    shard_rows = features.shape[0]
    shard_blocks = shard_rows // tile_size
    row_blocks = shard_blocks * lax.axis_size("col")
    col_blocks = shard_blocks * lax.axis_size("row")
    tile_vals = tile_values[0, 0]
    row_ids = tile_rows[0, 0]
    col_ids = tile_cols[0, 0]
    live_count = tile_count[0, 0]
    gathered = lax.all_gather(features, "row", axis=0, tiled=True)
    partial_value = aggregate(
        tile_vals, row_ids, col_ids, gathered, live_count, row_blocks, False, 0
    )
    aggregated = lax.psum_scatter(partial_value, "col", scatter_dimension=0, tiled=True).astype(
        jnp.bfloat16
    )
    pre_act = jnp.dot(aggregated, weight, preferred_element_type=jnp.float32)
    activated, pullback = jax.vjp(gelu_tanh, pre_act)
    grad_pre = pullback(cotangent.astype(jnp.float32))[0].astype(jnp.bfloat16)
    mixed = lax.dot_general(
        grad_pre, weight, (((1,), (1,)), ((), ())), preferred_element_type=jnp.float32
    ).astype(jnp.bfloat16)
    row_slab = lax.all_gather(mixed, "col", axis=0, tiled=True)
    back_sums = aggregate(tile_vals, col_ids, row_ids, row_slab, live_count, col_blocks, True, 0)
    grad_features = lax.psum_scatter(back_sums, "row", scatter_dimension=0, tiled=True).astype(
        jnp.bfloat16
    )
    local_grad = lax.dot_general(
        aggregated, grad_pre, (((0,), (0,)), ((), ())), preferred_element_type=jnp.float32
    )
    grad_weight = lax.psum(local_grad, ("row", "col"))
    return (activated.astype(jnp.bfloat16), grad_features, grad_weight)


def solution(mesh):
    in_specs = (
        P(("row", "col"), None),
        P(),
        P(("row", "col"), None),
        P("row", "col", None, None, None),
        P("row", "col", None),
        P("row", "col", None),
        P("row", "col"),
    )
    out_specs = (P(("row", "col"), None), P(("row", "col"), None), P())
    return jax.shard_map(
        per_device, mesh=mesh, in_specs=in_specs, out_specs=out_specs, check_vma=False
    )
```

profile of v0, /device:TPU:32, one launch (start us, length us, event | category | flops | bytes accessed | tf_op | source)
XLA Modules:
  0.0 743.0 jit_solution(7264740897939900848)
XLA Ops:
  9.4 27.5 %all-gather.3.cloned.1.call-done = bf16[4096,256]{1,0:T(8,128)(2,1)} async-done(((bf16[512,256]{1,0:T(8,128)(2,1)}), bf16[4096,256]{1,0:T(8,128)(2,1)}) %all-gather.3.cloned.1.call-update) | async-done | bytes 2097168 | tf_op jit(solution)/shard_map/all_gather | solution.py:49
  41.2 175.2 %while.26 = (s32[]{:T(128)}, f32[64,128,256]{2,1,0:T(8,128)}, s32[384]{0:T(512)S(1)}, s32[]{:T(128)}, bf16[384,128,128]{2,1,0:T(8,128)(2,1)}, /*index=5*/s32[384...) while((s32[]{:T(128)}, f32[64,128,256]{2,1,0:T(8,128)}, ...), condition=%wide.region_2.3_spmd, body=%wide.region_0.2_spmd.sunk | while | flops 404227712 | bytes 36181480 | solution.py:35
  44.2 5.1 fusion.34
  49.3 14.8 %scatter_fusion = f32[64,128,256]{2,1,0:T(8,128)} fusion(f32[64,128,256]{2,1,0:T(8,128)} %get-tuple-element.400, s32[48]{0:T(128)S(1)} %get-tuple-element.377, f32[48,128,256]{2,1,0:T(8,128)} %fusion.34), kind=kCustom, calls=%fused_computation.2.clone.1 | custom fusion | flops 1572864 | bytes 18874560 | tf_op jit(solution)/shard_map/while/body/eval_jaxpr/scatter-add | solution.py:32
  67.2 5.1 fusion.34
  72.2 14.9 %scatter_fusion = f32[64,128,256]{2,1,0:T(8,128)} fusion(f32[64,128,256]{2,1,0:T(8,128)} %get-tuple-element.400, s32[48]{0:T(128)S(1)} %get-tuple-element.377, f32[48,128,256]{2,1,0:T(8,128)} %fusion.34), kind=kCustom, calls=%fused_computation.2.clone.1 | custom fusion | flops 1572864 | bytes 18874560 | tf_op jit(solution)/shard_map/while/body/eval_jaxpr/scatter-add | solution.py:32
  90.2 5.1 fusion.34
  95.3 14.6 %scatter_fusion = f32[64,128,256]{2,1,0:T(8,128)} fusion(f32[64,128,256]{2,1,0:T(8,128)} %get-tuple-element.400, s32[48]{0:T(128)S(1)} %get-tuple-element.377, f32[48,128,256]{2,1,0:T(8,128)} %fusion.34), kind=kCustom, calls=%fused_computation.2.clone.1 | custom fusion | flops 1572864 | bytes 18874560 | tf_op jit(solution)/shard_map/while/body/eval_jaxpr/scatter-add | solution.py:32
  113.0 5.1 fusion.34
  118.0 13.1 %scatter_fusion = f32[64,128,256]{2,1,0:T(8,128)} fusion(f32[64,128,256]{2,1,0:T(8,128)} %get-tuple-element.400, s32[48]{0:T(128)S(1)} %get-tuple-element.377, f32[48,128,256]{2,1,0:T(8,128)} %fusion.34), kind=kCustom, calls=%fused_computation.2.clone.1 | custom fusion | flops 1572864 | bytes 18874560 | tf_op jit(solution)/shard_map/while/body/eval_jaxpr/scatter-add | solution.py:32
  134.3 5.1 fusion.34
  139.3 13.1 %scatter_fusion = f32[64,128,256]{2,1,0:T(8,128)} fusion(f32[64,128,256]{2,1,0:T(8,128)} %get-tuple-element.400, s32[48]{0:T(128)S(1)} %get-tuple-element.377, f32[48,128,256]{2,1,0:T(8,128)} %fusion.34), kind=kCustom, calls=%fused_computation.2.clone.1 | custom fusion | flops 1572864 | bytes 18874560 | tf_op jit(solution)/shard_map/while/body/eval_jaxpr/scatter-add | solution.py:32
  155.5 5.1 fusion.34
  160.6 13.1 %scatter_fusion = f32[64,128,256]{2,1,0:T(8,128)} fusion(f32[64,128,256]{2,1,0:T(8,128)} %get-tuple-element.400, s32[48]{0:T(128)S(1)} %get-tuple-element.377, f32[48,128,256]{2,1,0:T(8,128)} %fusion.34), kind=kCustom, calls=%fused_computation.2.clone.1 | custom fusion | flops 1572864 | bytes 18874560 | tf_op jit(solution)/shard_map/while/body/eval_jaxpr/scatter-add | solution.py:32
  176.8 5.1 fusion.34
  181.9 13.1 %scatter_fusion = f32[64,128,256]{2,1,0:T(8,128)} fusion(f32[64,128,256]{2,1,0:T(8,128)} %get-tuple-element.400, s32[48]{0:T(128)S(1)} %get-tuple-element.377, f32[48,128,256]{2,1,0:T(8,128)} %fusion.34), kind=kCustom, calls=%fused_computation.2.clone.1 | custom fusion | flops 1572864 | bytes 18874560 | tf_op jit(solution)/shard_map/while/body/eval_jaxpr/scatter-add | solution.py:32
  198.1 5.1 fusion.34
  203.2 13.1 %scatter_fusion = f32[64,128,256]{2,1,0:T(8,128)} fusion(f32[64,128,256]{2,1,0:T(8,128)} %get-tuple-element.400, s32[48]{0:T(128)S(1)} %get-tuple-element.377, f32[48,128,256]{2,1,0:T(8,128)} %fusion.34), kind=kCustom, calls=%fused_computation.2.clone.1 | custom fusion | flops 1572864 | bytes 18874560 | tf_op jit(solution)/shard_map/while/body/eval_jaxpr/scatter-add | solution.py:32
  216.4 93.0 %reduce-scatter.3.cloned.1.call-done = f32[512,256]{1,0:T(8,128)} async-done(((f32[8192,256]{1,0:T(8,128)}), f32[512,256]{1,0:T(8,128)}) %reduce-scatter.3.cloned.1.call-update) | async-done | bytes 524304 | tf_op jit(solution)/shard_map/reduce_scatter | solution.py:53
  312.8 16.7 %copy.10 = bf16[1,1,384,128,128]{3,4,2,1,0:T(8,128)(2,1)} copy(bf16[1,1,384,128,128]{4,3,2,1,0:T(8,128)(2,1)} %bitcast.22) | data formatting | bytes 25165824 | tf_op args[3]
  329.4 34.3 %all-gather.5.cloned.1.call-done = bf16[8192,256]{1,0:T(8,128)(2,1)} async-done(((bf16[512,256]{1,0:T(8,128)(2,1)}), bf16[8192,256]{1,0:T(8,128)(2,1)}) %all-gather.5.cloned.1.call-update) | async-done | bytes 4194320 | tf_op jit(solution)/shard_map/all_gather | solution.py:62
  366.2 185.3 %while.27 = (s32[]{:T(128)}, f32[32,128,256]{2,1,0:T(8,128)}, s32[384]{0:T(512)S(1)}, s32[]{:T(128)}, bf16[384,128,128]{1,2,0:T(8,128)(2,1)}, /*index=5*/s32[384...) while((s32[]{:T(128)}, f32[32,128,256]{2,1,0:T(8,128)}, ...), condition=%wide.region_6.7_spmd, body=%wide.region_4.6_spmd.sunk | while | flops 404227712 | bytes 36181480 | solution.py:35
  374.9 14.7 %scatter_fusion.1 = f32[32,128,256]{2,1,0:T(8,128)} fusion(f32[32,128,256]{2,1,0:T(8,128)} %get-tuple-element.433, s32[48]{0:T(128)S(1)} %get-tuple-element.386, f32[48,128,256]{2,1,0:T(8,128)} %fusion.37), kind=kCustom, calls=%fused_computation.3.clone.1 | custom fusion | flops 1572864 | bytes 18874560 | tf_op jit(solution)/shard_map/while/body/eval_jaxpr/scatter-add | solution.py:32
  398.3 14.7 %scatter_fusion.1 = f32[32,128,256]{2,1,0:T(8,128)} fusion(f32[32,128,256]{2,1,0:T(8,128)} %get-tuple-element.433, s32[48]{0:T(128)S(1)} %get-tuple-element.386, f32[48,128,256]{2,1,0:T(8,128)} %fusion.37), kind=kCustom, calls=%fused_computation.3.clone.1 | custom fusion | flops 1572864 | bytes 18874560 | tf_op jit(solution)/shard_map/while/body/eval_jaxpr/scatter-add | solution.py:32
  421.6 14.4 %scatter_fusion.1 = f32[32,128,256]{2,1,0:T(8,128)} fusion(f32[32,128,256]{2,1,0:T(8,128)} %get-tuple-element.433, s32[48]{0:T(128)S(1)} %get-tuple-element.386, f32[48,128,256]{2,1,0:T(8,128)} %fusion.37), kind=kCustom, calls=%fused_computation.3.clone.1 | custom fusion | flops 1572864 | bytes 18874560 | tf_op jit(solution)/shard_map/while/body/eval_jaxpr/scatter-add | solution.py:32
  444.7 14.4 %scatter_fusion.1 = f32[32,128,256]{2,1,0:T(8,128)} fusion(f32[32,128,256]{2,1,0:T(8,128)} %get-tuple-element.433, s32[48]{0:T(128)S(1)} %get-tuple-element.386, f32[48,128,256]{2,1,0:T(8,128)} %fusion.37), kind=kCustom, calls=%fused_computation.3.clone.1 | custom fusion | flops 1572864 | bytes 18874560 | tf_op jit(solution)/shard_map/while/body/eval_jaxpr/scatter-add | solution.py:32
  467.8 14.4 %scatter_fusion.1 = f32[32,128,256]{2,1,0:T(8,128)} fusion(f32[32,128,256]{2,1,0:T(8,128)} %get-tuple-element.433, s32[48]{0:T(128)S(1)} %get-tuple-element.386, f32[48,128,256]{2,1,0:T(8,128)} %fusion.37), kind=kCustom, calls=%fused_computation.3.clone.1 | custom fusion | flops 1572864 | bytes 18874560 | tf_op jit(solution)/shard_map/while/body/eval_jaxpr/scatter-add | solution.py:32
  490.9 14.4 %scatter_fusion.1 = f32[32,128,256]{2,1,0:T(8,128)} fusion(f32[32,128,256]{2,1,0:T(8,128)} %get-tuple-element.433, s32[48]{0:T(128)S(1)} %get-tuple-element.386, f32[48,128,256]{2,1,0:T(8,128)} %fusion.37), kind=kCustom, calls=%fused_computation.3.clone.1 | custom fusion | flops 1572864 | bytes 18874560 | tf_op jit(solution)/shard_map/while/body/eval_jaxpr/scatter-add | solution.py:32
  514.0 14.4 %scatter_fusion.1 = f32[32,128,256]{2,1,0:T(8,128)} fusion(f32[32,128,256]{2,1,0:T(8,128)} %get-tuple-element.433, s32[48]{0:T(128)S(1)} %get-tuple-element.386, f32[48,128,256]{2,1,0:T(8,128)} %fusion.37), kind=kCustom, calls=%fused_computation.3.clone.1 | custom fusion | flops 1572864 | bytes 18874560 | tf_op jit(solution)/shard_map/while/body/eval_jaxpr/scatter-add | solution.py:32
  537.1 14.4 %scatter_fusion.1 = f32[32,128,256]{2,1,0:T(8,128)} fusion(f32[32,128,256]{2,1,0:T(8,128)} %get-tuple-element.433, s32[48]{0:T(128)S(1)} %get-tuple-element.386, f32[48,128,256]{2,1,0:T(8,128)} %fusion.37), kind=kCustom, calls=%fused_computation.3.clone.1 | custom fusion | flops 1572864 | bytes 18874560 | tf_op jit(solution)/shard_map/while/body/eval_jaxpr/scatter-add | solution.py:32
  553.6 36.2 %reduce-scatter.5.cloned.1.call-done = f32[512,256]{1,0:T(8,128)} async-done(((f32[4096,256]{1,0:T(8,128)}), f32[512,256]{1,0:T(8,128)}) %reduce-scatter.5.cloned.1.call-update) | async-done | bytes 524304 | tf_op jit(solution)/shard_map/reduce_scatter | solution.py:64
  591.6 143.2 %all-reduce.2.cloned.1.call-done = f32[256,256]{1,0:T(8,128)} async-done(((f32[256,256]{1,0:T(8,128)}), f32[256,256]{1,0:T(8,128)}) %all-reduce.2.cloned.1.call-update) | async-done | bytes 262160 | tf_op jit(solution)/shard_map/psum | solution.py:70
  (81 shorter events, 111.5 us)
Async XLA Ops:
  7.2 302.3 %copy-start = (bf16[256,256]{1,0:T(8,128)(2,1)S(1)}, bf16[256,256]{1,0:T(8,128)(2,1)}, u32[]{:S(2)}) copy-start(bf16[256,256]{1,0:T(8,128)(2,1)} %param.12) | copy-start | bytes 393220
  7.2 29.7 %all-gather.3.cloned.1.call-start = ((), (), s32[]{:S(2)}) async-start(), calls=%async_computation.2 | async-start | bytes 2359296 | tf_op jit(solution)/shard_map/all_gather | solution.py:49
  7.9 301.5 %reduce-scatter.3.cloned.1.call-start = ((), (), s32[]{:S(2)}) async-start(), calls=%async_computation.3 | async-start | bytes 8912896 | tf_op jit(solution)/shard_map/reduce_scatter | solution.py:53
  216.3 93.1 %copy-start.2 = (bf16[512,256]{1,0:T(8,128)(2,1)S(1)}, bf16[512,256]{1,0:T(8,128)(2,1)}, u32[]{:S(2)}) copy-start(bf16[512,256]{1,0:T(8,128)(2,1)} %param.13) | copy-start | bytes 786436
  216.4 147.4 %all-gather.5.cloned.1.call-start = ((), (), s32[]{:S(2)}) async-start(), calls=%async_computation.4 | async-start | bytes 4456448 | tf_op jit(solution)/shard_map/all_gather | solution.py:62
  312.7 277.1 %reduce-scatter.5.cloned.1.call-start = ((), (), s32[]{:S(2)}) async-start(), calls=%async_computation.5 | async-start | bytes 4718592 | tf_op jit(solution)/shard_map/reduce_scatter | solution.py:64
  551.6 1.0 copy-start.1
  551.6 183.2 %all-reduce.2.cloned.1.call-start = ((), (), s32[]{:S(2)}) async-start(), calls=%async_computation.6 | async-start | bytes 524288 | tf_op jit(solution)/shard_map/psum | solution.py:70
Sparse Core Ops, SparseCore 0:
  9.7 27.1 all-gather.2
  216.5 92.9 reduce-scatter.2
  312.9 50.8 all-gather.4
  551.7 38.0 reduce-scatter.4
  595.0 139.7 all-reduce.1
where the time goes:
time: 747 us; the launch traced here: 743 us
  waiting for transfers between devices  335 us (45%)
  other arithmetic  241 us (32%)
  matrix products  84.7 us (11%)
  local copies, waits for them, and re-layouts  68.3 us (9%)
  between operations  13.8 us (2%)
    scatter-add x16, other arithmetic, one_group(): return running.at[target].add(products, mode='drop')  226 us
    psum x1, waiting for transfers between devices, per_device(): grad_weight = lax.psum(local_grad, ('row', 'col'))  143 us
    reduce_scatter x1, waiting for transfers between devices, per_device(): lax.psum_scatter(partial_value, 'col', scatter_dimension=0, tiled=True)  93 us
    dot_general x16, matrix products, one_group(): jnp.einsum(pattern, vals_now, picked, preferred_element_type=jnp.float32)  80.4 us
    gather x16, local copies, waits for them, and re-layouts, one_group(): picked = source_blocks[in_now]  42.2 us
    reduce_scatter x1, waiting for transfers between devices, per_device(): lax.psum_scatter(back_sums, 'row', scatter_dimension=0, tiled=True)  36.2 us
    all_gather x1, waiting for transfers between devices, per_device(): row_slab = lax.all_gather(mixed, 'col', axis=0, tiled=True)  34.3 us
    all_gather x1, waiting for transfers between devices, per_device(): gathered = lax.all_gather(features, 'row', axis=0, tiled=True)  27.5 us
  transfers between devices with their start and end apart: 5, of which 5 were waited for; matrix products, arithmetic and copies ran while one was open for 3% of the time, Pallas kernels for 0%

commit v1 on v0

v1 whole, which is shorter than its diff:
```python
import math

import jax
import jax.numpy as jnp
from jax import lax
from jax.experimental import pallas as pl
from jax.experimental.pallas import tpu as pltpu
from jax.sharding import PartitionSpec as P

BF = jnp.bfloat16
F32 = jnp.float32
BLK = 128
UNIT = 2
UNROLL = 8
GROUP = UNIT * UNROLL
KEYS = 64
DUMMY = 32

ONE = ((0, 1), (1, 0), (2, 3), (3, 2))
TWO = ((1, 2), (2, 1), (3, 0), (0, 3))
FAR = ((0, 2), (2, 0), (1, 3), (3, 1))


def swap(value, axis, pairs):
    if axis == "z":
        return lax.ppermute(value, "col", [(y * 4 + a, y * 4 + b) for y in range(4) for a, b in pairs])
    if axis == "y":
        return lax.ppermute(value, "col", [(a * 4 + z, b * 4 + z) for z in range(4) for a, b in pairs])
    return lax.ppermute(value, "row", [(a * 2 + k, b * 2 + k) for k in range(2) for a, b in pairs])


def swap_core(value):
    return lax.ppermute(value, "row", [(2 * x + k, 2 * x + 1 - k) for x in range(4) for k in range(2)])


def distance(here, there):
    return jnp.where(here % 2 == 0, there - here, here - there) & 3


def pick(index, table):
    found = jnp.zeros_like(index)
    for place, entry in enumerate(table):
        found = jnp.where(index == place, entry, found)
    return found


ROLE = (6, 1, 0, 4, 7, 5, 2, 3)


def plan(keys, source, live, segments):
    total = keys.shape[0]
    room = -(-(total + KEYS * (UNIT - 1) + len(segments) * GROUP) // GROUP) * GROUP
    keys = jnp.where(live, keys, KEYS)
    all_keys = jnp.arange(KEYS, dtype=jnp.int32)
    segment_of = sum((all_keys >= first).astype(jnp.int32) for first, _ in segments) - 1
    count = jnp.sum((keys[:, None] == all_keys[None, :]).astype(jnp.int32), 0)
    padded = (count + UNIT - 1) // UNIT * UNIT
    before = (all_keys[:, None] < all_keys[None, :]) & (segment_of[:, None] == segment_of[None, :])
    offset = jnp.sum(jnp.where(before, padded[:, None], 0), 0)
    bounds = [jnp.zeros((), jnp.int32)]
    for index, (first, last) in enumerate(segments):
        size = jnp.sum(jnp.where(segment_of == index, padded, 0))
        offset = offset + jnp.where(segment_of == index, bounds[-1] * GROUP, 0)
        bounds.append(bounds[-1] + (size + GROUP - 1) // GROUP)
    slots = jnp.arange(total, dtype=jnp.int32)
    rank = jnp.sum(((keys[:, None] == keys[None, :]) & (slots[None, :] < slots[:, None])).astype(jnp.int32), 1)
    place = rank + jnp.sum(jnp.where(keys[:, None] == all_keys[None, :], offset[None, :], 0), 1)
    place = jnp.where(live, place, -1)
    local = keys
    for first, _ in segments[1:]:
        local = jnp.where(keys >= first, keys - first, local)
    spots = jnp.arange(room, dtype=jnp.int32)
    hit = place[None, :] == spots[:, None]
    order = jnp.sum(jnp.where(hit, slots[None, :], 0), 1)
    reads = jnp.sum(jnp.where(hit, source[None, :] + 1, 0), 1)
    hit_unit = place[None, :] == spots[::UNIT][:, None]
    found = jnp.sum(jnp.where(hit_unit, local[None, :] + 1, 0), 1)
    writes = jnp.where(found > 0, found - 1, DUMMY)
    return jnp.stack(bounds), order, reads, writes


def load(tiles, *after):
    parts = 8
    size = tiles.shape[0] // parts

    def kernel(tile_ref, *refs):
        out, done, sem = refs[len(after) :]
        copies = [
            pltpu.make_async_copy(tile_ref.at[pl.ds(k * size, size)], out.at[pl.ds(k * size, size)], sem.at[k])
            for k in range(parts)
        ]
        for copy in copies:
            copy.start()
        done[...] = jnp.zeros_like(done)
        for copy in copies:
            copy.wait()

    return pl.pallas_call(
        kernel,
        in_specs=[pl.BlockSpec(memory_space=pltpu.HBM)] + [pl.BlockSpec(memory_space=pl.ANY)] * len(after),
        out_specs=[pl.BlockSpec(memory_space=pltpu.VMEM)] * 2,
        out_shape=[pltpu.VMEM(tiles.shape, tiles.dtype), jax.ShapeDtypeStruct((8, 128), jnp.int32)],
        scratch_shapes=[pltpu.SemaphoreType.DMA((parts,))],
        compiler_params=pltpu.CompilerParams(vmem_limit_bytes=1 << 20),
        cost_estimate=pl.CostEstimate(flops=0, bytes_accessed=25 << 20, transcendentals=0),
        name="load_tiles",
    )(pltpu.with_memory_space_constraint(tiles, pltpu.HBM), *after)


def assemble(pieces):
    total = BLK + sum(piece.shape[0] for piece in pieces)

    def kernel(*refs):
        fill_slab(refs[-1], [(ref, 0, ref.shape[0]) for ref in refs[:-1]])

    vmem = pl.BlockSpec(memory_space=pltpu.VMEM)
    return pl.pallas_call(
        kernel,
        in_specs=[vmem] * len(pieces),
        out_specs=vmem,
        out_shape=pltpu.VMEM((total, pieces[0].shape[1]), BF),
        compiler_params=pltpu.CompilerParams(vmem_limit_bytes=8 << 20),
        name="assemble",
    )(*pieces)


def cut(one, three, *after):
    half = one.shape[0] // 2

    def kernel(one_ref, three_ref, *refs):
        first, second = refs[-2:]
        first[...] = one_ref[pl.ds(0, half)]
        second[...] = three_ref[pl.ds(half, half)]

    vmem = pl.BlockSpec(memory_space=pltpu.VMEM)
    return pl.pallas_call(
        kernel,
        in_specs=[vmem, vmem] + [pl.BlockSpec(memory_space=pl.ANY)] * len(after),
        out_specs=[vmem] * 2,
        out_shape=[shape(half)] * 2,
        compiler_params=pltpu.CompilerParams(vmem_limit_bytes=8 << 20),
        name="cut",
    )(one, three, *after)


def relay(values, after):
    n = len(values)

    def kernel(*refs):
        for k in range(n):
            refs[n + 1 + k][...] = refs[k][...]

    vmem = pl.BlockSpec(memory_space=pltpu.VMEM)
    return pl.pallas_call(
        kernel,
        in_specs=[vmem] * n + [pl.BlockSpec(memory_space=pl.ANY)],
        out_specs=[vmem] * n,
        out_shape=[shape(value.shape[0]) for value in values],
        compiler_params=pltpu.CompilerParams(vmem_limit_bytes=8 << 20),
        name="relay",
    )(*values, after)


def fill_slab(slab, pieces):
    slab[pl.ds(0, BLK)] = jnp.zeros((BLK, slab.shape[1]), BF)
    place = BLK
    for ref, row, rows in pieces:
        slab[pl.ds(place, rows)] = ref[pl.ds(row, rows)]
        place += rows


def aggregate(name, step, lists, pieces, tiles, outs, flipped, start=None, mark=False):
    whole = len(pieces) == 1
    n_pieces = len(pieces)
    total = pieces[0][2] if whole else BLK + sum(rows for _, _, rows in pieces)
    blocks = max(first + size for first, size, _ in outs)

    def kernel(bounds, order, reads, writes, *refs):
        source = refs[:n_pieces]
        held = refs[n_pieces]
        refs = refs[n_pieces + 1 :]
        if start is not None:
            start_ref, refs = refs[0], refs[1:]
        out_refs, refs = refs[: len(outs)], refs[len(outs) :]
        if mark:
            refs[0][...] = jnp.zeros_like(refs[0])
            refs = refs[1:]
        acc = refs[0]
        if whole:
            slab = source[0]
        else:
            slab = refs[1]
            fill_slab(slab, [(ref, row, rows) for ref, (_, row, rows) in zip(source, pieces)])

        @pl.loop(0, blocks)
        def _(block):
            rows = pl.ds(pl.multiple_of(block * BLK, BLK), BLK)
            acc[rows] = jnp.zeros((BLK, acc.shape[1]), F32) if start is None else start_ref[rows]

        @pl.loop(bounds[step], bounds[step + 1])
        def _(group):
            for unit in range(UNROLL):
                spots = [group * GROUP + unit * UNIT + k for k in range(UNIT)]
                matrix = [held[order[spot]] for spot in spots]
                read = [slab[pl.ds(pl.multiple_of(reads[spot] * BLK, BLK), BLK)] for spot in spots]
                to = pl.ds(pl.multiple_of(writes[group * UNROLL + unit] * BLK, BLK), BLK)
                if flipped:
                    dims = (((0,), (0,)), ((), ()))
                    value = lax.dot_general(
                        jnp.concatenate(matrix, 0), jnp.concatenate(read, 0), dims, preferred_element_type=F32
                    )
                else:
                    value = jnp.dot(jnp.concatenate(matrix, 1), jnp.concatenate(read, 0), preferred_element_type=F32)
                acc[to] += value

        for out, (block, size, _) in zip(out_refs, outs):

            @pl.loop(0, size)
            def _(k, out=out, block=block):
                rows = pl.ds(pl.multiple_of((block + k) * BLK, BLK), BLK)
                out[pl.ds(pl.multiple_of(k * BLK, BLK), BLK)] = acc[rows].astype(out.dtype)

    smem = pl.BlockSpec(memory_space=pltpu.SMEM)
    vmem = pl.BlockSpec(memory_space=pltpu.VMEM)
    width = pieces[0][0].shape[1]
    extra = [] if start is None else [start]
    scratch = [pltpu.VMEM(((DUMMY + 1) * BLK, width), F32)]
    if not whole:
        scratch.append(pltpu.VMEM((total, width), BF))
    return pl.pallas_call(
        kernel,
        in_specs=[smem] * 4 + [vmem] * (n_pieces + 1 + len(extra)),
        out_specs=[vmem] * (len(outs) + mark),
        out_shape=[jax.ShapeDtypeStruct((size * BLK, width), dtype) for _, size, dtype in outs]
        + [jax.ShapeDtypeStruct((8, 128), jnp.int32)] * mark,
        scratch_shapes=scratch,
        compiler_params=pltpu.CompilerParams(vmem_limit_bytes=24 << 20),
        cost_estimate=pl.CostEstimate(flops=3 * 10**9, bytes_accessed=12 << 20, transcendentals=0),
        name=name,
    )(*lists, *[array for array, _, _ in pieces], pltpu.with_memory_space_constraint(tiles, pltpu.VMEM), *extra)


def local(name, body, out_shape, *operands):
    vmem = pl.BlockSpec(memory_space=pltpu.VMEM)
    return pl.pallas_call(
        body,
        in_specs=[vmem] * len(operands),
        out_specs=[vmem] * len(out_shape),
        out_shape=out_shape,
        compiler_params=pltpu.CompilerParams(vmem_limit_bytes=24 << 20),
        name=name,
    )(*operands)


def shape(rows, dtype=BF, width=256):
    return jax.ShapeDtypeStruct((rows, width), dtype)


def second_phase(*refs):
    ins, outs = refs[:8], refs[8:]
    for k in range(2):
        kept, one, three, two = ins[4 * k : 4 * k + 4]
        total = (kept[...] + two[...].astype(F32)) + (one[...].astype(F32) + three[...].astype(F32))
        for away, out in enumerate(outs[4 * k : 4 * k + 4]):
            out[...] = total[256 * away : 256 * away + 256].astype(out.dtype)


SCALE = math.sqrt(2.0 / math.pi)


def dense(*refs):
    sums, (cotangent, weight, activated, message_a, message_b) = refs[:8], refs[8:]
    matrix = weight[...]
    halves = []
    for k in range(2):
        kept, one, three, two = sums[4 * k : 4 * k + 4]
        halves.append((kept[...] + two[...].astype(F32)) + (one[...].astype(F32) + three[...].astype(F32)))
    aggregated = jnp.concatenate(halves, 0).astype(BF)
    pre = jnp.dot(aggregated, matrix, preferred_element_type=F32)
    square = pre * pre
    curve = jnp.tanh(SCALE * (pre + 0.044715 * (pre * square)))
    activated[...] = (0.5 * pre * (1.0 + curve)).astype(BF)
    slope = 0.5 * (1.0 + curve) + 0.5 * pre * (1.0 - curve * curve) * (SCALE * (1.0 + 3.0 * 0.044715 * square))
    grad_pre = (cotangent[...].astype(F32) * slope).astype(BF)
    mixed = lax.dot_general(grad_pre, matrix, (((1,), (1,)), ((), ())), preferred_element_type=F32).astype(BF)
    grad = lax.dot_general(aggregated, grad_pre, (((0,), (0,)), ((), ())), preferred_element_type=F32).astype(BF)
    for k, message in enumerate((message_a, message_b)):
        for half in range(2):
            message[pl.ds(half * 192, BLK)] = mixed[(2 * k + half) * BLK : (2 * k + half + 1) * BLK]
            message[pl.ds(half * 192 + BLK, 64)] = grad[(2 * k + half) * 64 : (2 * k + half + 1) * 64]


def four(zero, one, two, three):
    return (zero.astype(F32) + two.astype(F32)) + (one.astype(F32) + three.astype(F32))


def gathered(own, one, three, two, out):
    for half in range(2):
        for slot, ref in enumerate((own, one, three, two)):
            out[pl.ds(half * 576 + slot * BLK, BLK)] = ref[pl.ds(192 * half, BLK)]
        parts = [ref[pl.ds(192 * half + BLK, 64)] for ref in (own, one, two, three)]
        out[pl.ds(half * 576 + 512, 64)] = four(*parts).astype(BF)


def sum_ring(*refs):
    out = refs[-1]
    for k in range(2):
        own, one, three, *two = refs[5 * k : 5 * k + 5]
        for half in range(2):
            rows = pl.ds(576 * half + 512, 64)
            total = four(own[rows], one[rows], two[half][pl.ds(512, 64)], three[rows])
            out[pl.ds((2 * k + half) * 64, 64)] = total


def last_phase(own, received, grad, grad_received, by_one, by_two, late_two, late_one, kept):
    total = own[...] + received[...].astype(F32)
    by_one[pl.ds(0, 512)] = total[0:512].astype(BF)
    by_two[pl.ds(0, 512)] = total[512:1024].astype(BF)
    late_two[...] = total[1024:1280].astype(BF)
    late_one[...] = total[1280:1536].astype(BF)
    kept[...] = total[1536:2048]
    both = (grad[...] + grad_received[...]).astype(BF)
    by_one[pl.ds(512, 256)] = both
    by_two[pl.ds(512, 256)] = both


def last_forward(late_two, by_one, late_one, by_two, out_two, out_one):
    out_two[pl.ds(0, 256)] = (late_two[...].astype(F32) + by_one[pl.ds(0, 256)].astype(F32)).astype(BF)
    out_two[pl.ds(256, 128)] = by_one[pl.ds(512, 128)]
    out_one[pl.ds(0, 256)] = (late_one[...].astype(F32) + by_two[pl.ds(0, 256)].astype(F32)).astype(BF)
    out_one[pl.ds(256, 128)] = by_two[pl.ds(640, 128)]


def last_sum(kept, by_one, by_two, late_two, late_one, own_message, features, weight):
    first = kept[pl.ds(0, 256)] + (by_one[pl.ds(256, 256)].astype(F32) + late_two[pl.ds(0, 256)].astype(F32))
    second = kept[pl.ds(256, 256)] + (by_two[pl.ds(256, 256)].astype(F32) + late_one[pl.ds(0, 256)].astype(F32))
    features[pl.ds(0, 256)] = first.astype(BF)
    features[pl.ds(256, 256)] = second.astype(BF)
    for half, late in enumerate((late_two, late_one)):
        rows = pl.ds(512 + 128 * half, 128)
        weight[pl.ds(128 * half, 128)] = four(own_message[rows], by_one[rows], late[pl.ds(256, 128)], by_two[rows])


def per_device(features, weight, cotangent, tile_values, tile_rows, tile_cols, tile_count):
    tiles = tile_values[0, 0]
    near_one, near_two = swap(features, "x", ONE), swap(features, "x", TWO)
    across = swap_core(features)
    rows, cols = tile_rows[0, 0], tile_cols[0, 0]
    live = jnp.arange(rows.shape[0], dtype=jnp.int32) < tile_count[0, 0]
    row, col = lax.axis_index("row"), lax.axis_index("col")
    x, core, y, z = row // 2, row % 2, col // 4, col % 4

    sub = rows % 4
    y_away, z_away = distance(y, rows // 16), distance(z, rows // 4 % 4)
    second = sub >= 2
    half = sub % 2
    ring_one, ring_two = jnp.where(second, y_away, z_away), jnp.where(second, z_away, y_away)
    within = ring_two * 2 + half
    base = pick(ring_one, (48, 16, 0, 24))
    forward_key = base + jnp.where(second, jnp.where(ring_one % 2 == 1, 16, 8), 0) + within
    x_away, other = distance(x, cols // 8), (cols // 4 % 2) ^ core
    slot = x_away ^ (x_away >> 1)
    forward_source = other * 16 + slot * 4 + cols % 4
    far = ring_one == 2
    near_slot = ring_one ^ (ring_one >> 1)
    inner = ring_two ^ (ring_two >> 1)
    backward_source = jnp.where(far, second * 8, second * 24 + near_slot * 8) + half * 4 + inner
    backward_role = pick(cols % 4 // 2 * 4 + x_away, ROLE)
    backward_key = jnp.where(far, 32, 0) + (1 - other) * 16 + backward_role * 2 + cols % 2

    forward = plan(forward_key, forward_source, live, ((0, 16), (16, 48), (48, 64)))

    far_first, far_second = cut(near_one, near_two, *forward)
    held_tiles, loaded = load(tiles, far_first)
    far_first, far_second = swap(far_first, "x", TWO), swap(far_second, "x", ONE)
    far_first, far_second = relay((far_first, far_second), loaded)
    across_near = [swap_core(near_one), swap_core(near_two)]
    across_far = [swap_core(far_first), swap_core(far_second)]
    held = [features, near_one, near_two, far_first, far_second, across, *across_near, *across_far]
    slab = assemble(held)
    pieces = [(slab, 0, slab.shape[0])]

    def ways(axis, one, three, two):
        return swap(one, axis, ONE), swap(three, axis, TWO), swap(two, axis, FAR)

    def out(*dtypes):
        return [(8 * k, 8, dtype) for k, dtype in enumerate(dtypes)]

    a_two, b_two = aggregate("forward_far", 0, forward, pieces, held_tiles, out(BF, BF), False)
    a_two, b_two = swap(a_two, "z", FAR), swap(b_two, "y", FAR)
    a_one, a_three, b_one, b_three = aggregate(
        "forward_near", 1, forward, pieces, held_tiles, out(BF, BF, BF, BF), False
    )
    a_one, a_three = swap(a_one, "z", ONE), swap(a_three, "z", TWO)
    b_one, b_three = swap(b_one, "y", ONE), swap(b_three, "y", TWO)
    a_own, b_own, after = aggregate("forward_own", 2, forward, pieces, held_tiles, out(F32, F32), False, None, True)
    backward = plan(
        backward_key + after[0, 0], backward_source + after[0, 0], live, ((0, 32), (32, 48), (48, 64))
    )
    second_shapes = [shape(256, F32), shape(256), shape(256), shape(256)]
    a_own, a_one, a_two, a_three, b_own, b_one, b_two, b_three = local(
        "second_phase", second_phase, second_shapes * 2,
        a_own, a_one, a_three, a_two, b_own, b_one, b_three, b_two,
    )
    a_sums = [a_own, *ways("y", a_one, a_three, a_two)]
    b_sums = [b_own, *ways("z", b_one, b_three, b_two)]
    activated, a_own, b_own = local(
        "dense", dense, [shape(512), shape(384), shape(384)], *a_sums, *b_sums, cotangent, weight
    )

    a_held = [a_own, *ways("y", a_own, a_own, a_own)]
    b_held = [b_own, *ways("z", b_own, b_own, b_own)]
    (a_own,) = local("gathered_a", gathered, [shape(1152)], *a_held)
    a_one, a_three = swap(a_own, "z", ONE), swap(a_own, "z", TWO)
    (b_own,) = local("gathered_b", gathered, [shape(1152)], *b_held)
    b_one, b_three = swap(b_own, "y", ONE), swap(b_own, "y", TWO)
    again, loaded = load(tiles, a_own, b_own)
    a_first, a_second = cut(a_one, a_three, loaded)
    b_first, b_second = cut(b_one, b_three, loaded)
    a_far = swap(a_first, "z", TWO), swap(a_second, "z", ONE)
    b_far = swap(b_first, "y", TWO), swap(b_second, "y", ONE)

    near = [
        (piece, row, 512) for piece in (a_own, a_one, a_three, b_own, b_one, b_three) for row in (0, 576)
    ]
    distant = [(piece, 0, 512) for piece in (*a_far, *b_far)]
    other_start, own_start = aggregate(
        "backward_near", 0, backward, near, again, [(0, 16, F32), (16, 16, F32)], True
    )
    (other_sum,) = aggregate("backward_other", 1, backward, distant, again, [(0, 16, BF)], True, other_start)
    received = swap_core(other_sum)
    (grad,) = local(
        "sum_ring", sum_ring, [shape(256, F32)], a_own, a_one, a_three, *a_far, b_own, b_one, b_three, *b_far
    )
    grad_received = swap_core(grad)
    (own_sum,) = aggregate("backward_own", 2, backward, distant, again, [(0, 16, F32)], True, own_start)
    by_one, by_two, late_two, late_one, kept = local(
        "last_phase", last_phase, [shape(768), shape(768), shape(256), shape(256), shape(512, F32)],
        own_sum, received, grad, grad_received,
    )
    got_one, got_two = swap(by_one, "x", ONE), swap(by_two, "x", TWO)
    late_two, late_one = local(
        "last_forward", last_forward, [shape(384), shape(384)], late_two, got_one, late_one, got_two
    )
    late_two, late_one = swap(late_two, "x", TWO), swap(late_one, "x", ONE)
    grad_features, grad_weight = local(
        "last_sum", last_sum, [shape(512), shape(256, F32)], kept, got_one, got_two, late_two, late_one, by_one
    )
    return activated, grad_features, grad_weight


def solution(mesh):
    in_specs = (
        P(("row", "col"), None),
        P(),
        P(("row", "col"), None),
        P("row", "col", None, None, None),
        P("row", "col", None),
        P("row", "col", None),
        P("row", "col"),
    )
    out_specs = (P(("row", "col"), None), P(("row", "col"), None), P())
    return jax.shard_map(
        per_device, mesh=mesh, in_specs=in_specs, out_specs=out_specs, check_vma=False
    )
```

time: 747 us -> 141 us (0.19)
  waiting for transfers between devices: 335 us -> 47.3 us
  other arithmetic: 241 us -> 5.87 us
  matrix products: 84.7 us -> 0 us
  local copies, waits for them, and re-layouts: 68.3 us -> 0.75 us
  starting transfers between devices: 0.2 us -> 45.5 us
  Pallas kernels: 0 us -> 34.5 us
  between operations: 13.8 us -> 5.79 us
    scatter-add x16 -> x0, other arithmetic: 226 us -> none  [one_group(): return running.at[target].add(products, mode='drop')]
    psum x1 -> x0, waiting for transfers between devices: 143 us -> none  [per_device(): grad_weight = lax.psum(local_grad, ('row', 'col'))]
    reduce_scatter x2 -> x0, waiting for transfers between devices: 129 us -> none  [the longest x1 93 us: per_device(): lax.psum_scatter(partial_value, 'col', scatter_dimension=0, tiled=True)]
    dot_general x19 -> x0, matrix products: 84.7 us -> none  [the longest x16 80.4 us: one_group(): jnp.einsum(pattern, vals_now, picked, preferred_element_type=jnp.float32)]
    all_gather x2 -> x0, waiting for transfers between devices: 61.8 us -> none  [the longest x1 34.3 us: per_device(): row_slab = lax.all_gather(mixed, 'col', axis=0, tiled=True)]
    ppermute x0 -> x41, waiting for transfers between devices: none -> 47.3 us  [the longest x8 18 us: swap(): lax.ppermute(value, 'row', [(a * 2 + k, b * 2 + k) for k in range(2) for...]
    ppermute x0 -> x41, starting transfers between devices: none -> 45.5 us  [the longest x13 20.4 us: swap(): lax.ppermute(value, 'col', [(a * 4 + z, b * 4 + z) for z in range(4) for...]
    gather x16 -> x0, local copies, waits for them, and re-layouts: 42.2 us -> none  [one_group(): picked = source_blocks[in_now]]
  transfers between devices with their start and end apart: 5 -> 41, of which waited for: 5 -> 18; matrix products, arithmetic and copies ran while one was open for 3% -> 5% of each run, Pallas kernels for 0% -> 19%
where the time goes in v1:
time: 141 us; the launch traced here: 140 us
  waiting for transfers between devices  47.3 us (34%)
  starting transfers between devices  45.5 us (32%)
  Pallas kernels  34.5 us (24%)
  other arithmetic  5.87 us (4%)
  between operations  5.79 us (4%)
    pallas_call x6, Pallas kernels, aggregate(): pl.pallas_call(kernel, in_specs=[smem] * 4 + [vmem] * (n_pieces + 1 + len...  21.8 us
    ppermute x13, starting transfers between devices, swap(): lax.ppermute(value, 'col', [(a * 4 + z, b * 4 + z) for z in range(4) for...  20.4 us
    ppermute x8, waiting for transfers between devices, swap(): lax.ppermute(value, 'row', [(a * 2 + k, b * 2 + k) for k in range(2) for...  18 us
    ppermute x13, waiting for transfers between devices, swap(): lax.ppermute(value, 'col', [(y * 4 + a, y * 4 + b) for y in range(4) for...  17.9 us
    ppermute x13, starting transfers between devices, swap(): lax.ppermute(value, 'col', [(y * 4 + a, y * 4 + b) for y in range(4) for...  14.8 us
    ppermute x13, waiting for transfers between devices, swap(): lax.ppermute(value, 'col', [(a * 4 + z, b * 4 + z) for z in range(4) for...  10.1 us
    pallas_call x2, Pallas kernels, load(): pl.pallas_call(kernel, in_specs=[pl.BlockSpec(memory_space=pltpu.HBM)] +...  9.44 us
    ppermute x8, starting transfers between devices, swap(): lax.ppermute(value, 'row', [(a * 2 + k, b * 2 + k) for k in range(2) for...  8.36 us
  transfers between devices with their start and end apart: 41, of which 18 were waited for; matrix products, arithmetic and copies ran while one was open for 5% of the time, Pallas kernels for 19%

profile of v1, /device:TPU:32, one launch (start us, length us, event | category | flops | bytes accessed | tf_op | source)
XLA Modules:
  0.0 139.7 jit_solution(7214588098031066222)
XLA Ops:
  0.6 2.8 %collective-permute-start.1 = (bf16[512,256]{1,0:T(8,128)(2,1)}, bf16[512,256]{1,0:T(8,128)(2,1)S(1)}, u32[]{:S(2)}, u32[]{:S(2)}) collective-permute-start(bf16[512,256]{1,0:T(8,128)(2,1)} %refs_0_.1), channel_id=1, source_target_pairs={{32,64},{64,32},{96,0},{0,96},{48,80},{80,48},{112,16},{16,112},{3... | collective-permute-start | bytes 786440 | tf_op jit(solution)/shard_map/ppermute | solution.py:29
  13.7 4.7 %load_tiles.2 = (bf16[384,128,128]{2,1,0:T(8,128)(2,1)S(1)}, s32[8,128]{1,0:T(8,128)S(1)}) custom-call(bf16[384,128,128]{2,1,0:T(8,128)(2,1)} %bitcast.13, bf16[256,256]{1,0:T(8,128)(2,1)S(1)} %get-tuple-element.46.refs_0_), custom_call_target="tpu_custom_call" | custom-call | bytes 26214400 | tf_op jit(solution)/shard_map/load_tiles/pallas_call | solution.py:98
  20.5 2.9 %forward_far.1 = (bf16[1024,256]{1,0:T(8,128)(2,1)S(1)}, bf16[1024,256]{1,0:T(8,128)(2,1)S(1)}) custom-call(s32[4]{0:T(128)S(1)} %fusion.38.refs_0_.bounds, s32[496]{0:T(512)S(1)} %get-tuple-element.92.refs_1_.order, s32[496]{0:T(512)S(1)} %get-tuple-element.91.refs_2_.reads, s32[248]{0:T(256)S(1)} %compare_select_fusion.4.refs_3_.writes, ...), custom_call_target="tpu_custom_call" | custom-call | flops 3000000000 | bytes 12582912 | tf_op jit(solution)/shard_map/forward_far/pallas_call | solution.py:230
  23.4 3.4 %collective-permute-start.11 = (bf16[1024,256]{1,0:T(8,128)(2,1)S(1)}, bf16[1024,256]{1,0:T(8,128)(2,1)S(1)}, u32[]{:S(2)}, u32[]{:S(2)}) collective-permute-start(bf16[1024,256]{1,0:T(8,128)(2,1)S(1)} %get-tuple-element.55), channel_id=1, source_target_pairs={{0,2},{2,0},{1,3},{3,1},{4,6},{6,4},{5,7},{7,5},{8,10},{10,8},{9,1... | collective-permute-start | bytes 1572872 | tf_op jit(solution)/shard_map/ppermute | solution.py:26
  26.8 2.9 %collective-permute-start.14 = (bf16[1024,256]{1,0:T(8,128)(2,1)S(1)}, bf16[1024,256]{1,0:T(8,128)(2,1)S(1)}, u32[]{:S(2)}, u32[]{:S(2)}) collective-permute-start(bf16[1024,256]{1,0:T(8,128)(2,1)S(1)} %get-tuple-element.59), channel_id=1, source_target_pairs={{0,8},{8,0},{4,12},{12,4},{1,9},{9,1},{5,13},{13,5},{2,10},{10,2},... | collective-permute-start | bytes 1572872 | tf_op jit(solution)/shard_map/ppermute | solution.py:28
  29.7 4.9 %forward_near.1 = (bf16[1024,256]{1,0:T(8,128)(2,1)S(1)}, bf16[1024,256]{1,0:T(8,128)(2,1)S(1)}, bf16[1024,256]{1,0:T(8,128)(2,1)S(1)}, bf16[1024,256]{1,0:T(8,128)(2,1)S(1)}) custom-call(s32[4]{0:T(128)S(1)} %fusion.38.refs_0_.bounds, s32[496]{0:T(512)S(1)} %get-tuple-element.92.refs_1_.order, s32[496]{0:T(512)S(1)} %get-tuple-element.91.refs_2_.reads, ...), custom_call_target="tpu_custom_call" | custom-call | flops 3000000000 | bytes 12582912 | tf_op jit(solution)/shard_map/forward_near/pallas_call | solution.py:230
  36.5 3.3 %collective-permute-done.11.refs_3_ = bf16[1024,256]{1,0:T(8,128)(2,1)S(1)} collective-permute-done((bf16[1024,256]{1,0:T(8,128)(2,1)S(1)}, bf16[1024,256]{1,0:T(8,128)(2,1)S(1)}, u32[]{:S(2)}, u32[]{:S(2)}) %collective-permute-start.11) | collective-permute-done | bytes 524320 | tf_op jit(solution)/shard_map/ppermute | solution.py:26
  39.8 3.1 %collective-permute-start.13 = (bf16[1024,256]{1,0:T(8,128)(2,1)S(1)}, bf16[1024,256]{1,0:T(8,128)(2,1)S(1)}, u32[]{:S(2)}, u32[]{:S(2)}) collective-permute-start(bf16[1024,256]{1,0:T(8,128)(2,1)S(1)} %get-tuple-element.58), channel_id=1, source_target_pairs={{4,8},{8,4},{12,0},{0,12},{5,9},{9,5},{13,1},{1,13},{6,10},{10,6},... | collective-permute-start | bytes 1572872 | tf_op jit(solution)/shard_map/ppermute | solution.py:28
  42.9 2.6 %forward_own.1 = (f32[1024,256]{1,0:T(8,128)S(1)}, f32[1024,256]{1,0:T(8,128)S(1)}, s32[8,128]{1,0:T(8,128)S(1)}) custom-call(s32[4]{0:T(128)S(1)} %fusion.38.refs_0_.bounds, s32[496]{0:T(512)S(1)} %get-tuple-element.92.refs_1_.order, s32[496]{0:T(512)S(1)} %get-tuple-element.91.refs_2_.reads, s32[248]{0:T(256)S(1)} %compare_select_fusion.4.refs_3_.writes, ...), custom_call_target="tpu_custom_call" | custom-call | flops 3000000000 | bytes 12582912 | tf_op jit(solution)/shard_map/forward_own/pallas_call | solution.py:230
  46.0 4.4 %collective-permute-done.9.refs_1_ = bf16[1024,256]{1,0:T(8,128)(2,1)S(1)} collective-permute-done((bf16[1024,256]{1,0:T(8,128)(2,1)S(1)}, bf16[1024,256]{1,0:T(8,128)(2,1)S(1)}, u32[]{:S(2)}, u32[]{:S(2)}) %collective-permute-start.9) | collective-permute-done | bytes 524320 | tf_op jit(solution)/shard_map/ppermute | solution.py:26
  50.5 2.9 %collective-permute-done.12.refs_5_ = bf16[1024,256]{1,0:T(8,128)(2,1)S(1)} collective-permute-done((bf16[1024,256]{1,0:T(8,128)(2,1)S(1)}, bf16[1024,256]{1,0:T(8,128)(2,1)S(1)}, u32[]{:S(2)}, u32[]{:S(2)}) %collective-permute-start.12) | collective-permute-done | bytes 524320 | tf_op jit(solution)/shard_map/ppermute | solution.py:28
  55.9 2.2 %collective-permute-start.16 = (bf16[256,256]{1,0:T(8,128)(2,1)S(1)}, bf16[256,256]{1,0:T(8,128)(2,1)S(1)}, u32[]{:S(2)}, u32[]{:S(2)}) collective-permute-start(bf16[256,256]{1,0:T(8,128)(2,1)S(1)} %get-tuple-element.62), channel_id=1, source_target_pairs={{4,8},{8,4},{12,0},{0,12},{5,9},{9,5},{13,1},{1,13},{6,10},{10,6},... | collective-permute-start | bytes 393224 | tf_op jit(solution)/shard_map/ppermute | solution.py:28
  58.1 1.5 %collective-permute-start.17 = (bf16[256,256]{1,0:T(8,128)(2,1)S(1)}, bf16[256,256]{1,0:T(8,128)(2,1)S(1)}, u32[]{:S(2)}, u32[]{:S(2)}) collective-permute-start(bf16[256,256]{1,0:T(8,128)(2,1)S(1)} %get-tuple-element.63), channel_id=1, source_target_pairs={{0,8},{8,0},{4,12},{12,4},{1,9},{9,1},{5,13},{13,5},{2,10},{10,2},... | collective-permute-start | bytes 393224 | tf_op jit(solution)/shard_map/ppermute | solution.py:28
  60.4 2.2 %collective-permute-start.19 = (bf16[256,256]{1,0:T(8,128)(2,1)S(1)}, bf16[256,256]{1,0:T(8,128)(2,1)S(1)}, u32[]{:S(2)}, u32[]{:S(2)}) collective-permute-start(bf16[256,256]{1,0:T(8,128)(2,1)S(1)} %get-tuple-element.66), channel_id=1, source_target_pairs={{1,2},{2,1},{3,0},{0,3},{5,6},{6,5},{7,4},{4,7},{9,10},{10,9},{11,... | collective-permute-start | bytes 393224 | tf_op jit(solution)/shard_map/ppermute | solution.py:26
  66.0 3.1 %collective-permute-done.20.refs_7_ = bf16[256,256]{1,0:T(8,128)(2,1)S(1)} collective-permute-done((bf16[256,256]{1,0:T(8,128)(2,1)S(1)}, bf16[256,256]{1,0:T(8,128)(2,1)S(1)}, u32[]{:S(2)}, u32[]{:S(2)}) %collective-permute-start.20) | collective-permute-done | bytes 131104 | tf_op jit(solution)/shard_map/ppermute | solution.py:26
  70.4 1.4 collective-permute-start.28
  71.7 2.0 %collective-permute-start.23 = (bf16[384,256]{1,0:T(8,128)(2,1)S(1)}, bf16[384,256]{1,0:T(8,128)(2,1)S(1)}, u32[]{:S(2)}, u32[]{:S(2)}) collective-permute-start(bf16[384,256]{1,0:T(8,128)(2,1)S(1)} %get-tuple-element.70.own), channel_id=1, source_target_pairs={{0,8},{8,0},{4,12},{12,4},{1,9},{9,1},{5,13},{13,5},{2,10},{10,2},... | collective-permute-start | bytes 589832 | tf_op jit(solution)/shard_map/ppermute | solution.py:28
  75.2 1.5 %collective-permute-start.27 = (bf16[384,256]{1,0:T(8,128)(2,1)S(1)}, bf16[384,256]{1,0:T(8,128)(2,1)S(1)}, u32[]{:S(2)}, u32[]{:S(2)}) collective-permute-start(bf16[384,256]{1,0:T(8,128)(2,1)S(1)} %get-tuple-element.71.own), channel_id=1, source_target_pairs={{1,2},{2,1},{3,0},{0,3},{5,6},{6,5},{7,4},{4,7},{9,10},{10,9},{11,... | collective-permute-start | bytes 589832 | tf_op jit(solution)/shard_map/ppermute | solution.py:26
  76.7 2.4 %collective-permute-done.28.two = bf16[384,256]{1,0:T(8,128)(2,1)S(1)} collective-permute-done((bf16[384,256]{1,0:T(8,128)(2,1)S(1)}, bf16[384,256]{1,0:T(8,128)(2,1)S(1)}, u32[]{:S(2)}, u32[]{:S(2)}) %collective-permute-start.28) | collective-permute-done | bytes 196640 | tf_op jit(solution)/shard_map/ppermute | solution.py:26
  81.1 3.8 %collective-permute-done.26.one = bf16[384,256]{1,0:T(8,128)(2,1)S(1)} collective-permute-done((bf16[384,256]{1,0:T(8,128)(2,1)S(1)}, bf16[384,256]{1,0:T(8,128)(2,1)S(1)}, u32[]{:S(2)}, u32[]{:S(2)}) %collective-permute-start.26) | collective-permute-done | bytes 196640 | tf_op jit(solution)/shard_map/ppermute | solution.py:26
  84.9 5.0 %collective-permute-start.32 = (bf16[1152,256]{1,0:T(8,128)(2,1)S(1)}, bf16[1152,256]{1,0:T(8,128)(2,1)S(1)}, u32[]{:S(2)}, u32[]{:S(2)}) collective-permute-start(bf16[1152,256]{1,0:T(8,128)(2,1)S(1)} %gathered_b.1.refs_1_.refs_6_.refs_7_.refs_5_), channel_id=1, source_target_pairs={{4,8},{8,4},{12,0},{0,12},{5,9},{9,5},{13,1},{1,13},{6,10},{10,6},... | collective-permute-start | bytes 1769480 | tf_op jit(solution)/shard_map/ppermute | solution.py:28
  91.3 4.7 %load_tiles.3 = (bf16[384,128,128]{2,1,0:T(8,128)(2,1)S(1)}, s32[8,128]{1,0:T(8,128)S(1)}) custom-call(bf16[384,128,128]{2,1,0:T(8,128)(2,1)} %bitcast.14, bf16[1152,256]{1,0:T(8,128)(2,1)S(1)} %gathered_a.1.refs_0_.refs_1_, bf16[1152,256]{1,0:T(8,128)(2,1)S(1)} %gathered_b.1.refs_1_.refs_6_.refs_7_.refs_5_), custom_call_target="tpu_custom_call" | custom-call | bytes 26214400 | tf_op jit(solution)/shard_map/load_tiles/pallas_call | solution.py:98
  96.0 4.9 %collective-permute-done.32.three_ref.refs_10_.refs_11_.refs_7_ = bf16[1152,256]{1,0:T(8,128)(2,1)S(1)} collective-permute-done((bf16[1152,256]{1,0:T(8,128)(2,1)S(1)}, bf16[1152,256]{1,0:T(8,128)(2,1)S(1)}, u32[]{:S(2)}, u32[]{:S(2)}) %collective-permute-start.32) | collective-permute-done | bytes 589856 | tf_op jit(solution)/shard_map/ppermute | solution.py:28
  100.9 2.0 %collective-permute-done.31.one_ref.refs_8_.refs_9_.refs_6_ = bf16[1152,256]{1,0:T(8,128)(2,1)S(1)} collective-permute-done((bf16[1152,256]{1,0:T(8,128)(2,1)S(1)}, bf16[1152,256]{1,0:T(8,128)(2,1)S(1)}, u32[]{:S(2)}, u32[]{:S(2)}) %collective-permute-start.31) | collective-permute-done | bytes 589856 | tf_op jit(solution)/shard_map/ppermute | solution.py:28
  102.9 1.3 collective-permute-start.33
  106.1 6.7 %backward_near.1 = (f32[2048,256]{1,0:T(8,128)S(1)}, f32[2048,256]{1,0:T(8,128)S(1)}) custom-call(s32[4]{0:T(128)S(1)} %fusion.40.bounds, s32[496]{0:T(512)S(1)} %get-tuple-element.90.order, s32[496]{0:T(512)S(1)} %get-tuple-element.89.reads, s32[248]{0:T(256)S(1)} %compare_select_fusion.2.writes, bf16[1152,256]{1,0:T(8,128)(2,1)S(1)} %gathered_a.1.refs_0_.refs_1_, ...), custom_call_target="tpu_custom_call" | custom-call | flops 3000000000 | bytes 12582912 | tf_op jit(solution)/shard_map/backward_near/pallas_call | solution.py:230
  112.8 2.4 %backward_other.1 = bf16[2048,256]{1,0:T(8,128)(2,1)S(1)} custom-call(s32[4]{0:T(128)S(1)} %fusion.40.bounds, s32[496]{0:T(512)S(1)} %get-tuple-element.90.order, s32[496]{0:T(512)S(1)} %get-tuple-element.89.reads, s32[248]{0:T(256)S(1)} %compare_select_fusion.2.writes, bf16[576,256]{1,0:T(8,128)(2,1)S(1)} %collective-permute-done.29.refs_0_.refs_3_, ...), custom_call_target="tpu_custom_call" | custom-call | flops 3000000000 | bytes 12582912 | tf_op jit(solution)/shard_map/backward_other/pallas_call | solution.py:230
  115.9 2.4 %backward_own.1.own = f32[2048,256]{1,0:T(8,128)S(1)} custom-call(s32[4]{0:T(128)S(1)} %fusion.40.bounds, s32[496]{0:T(512)S(1)} %get-tuple-element.90.order, s32[496]{0:T(512)S(1)} %get-tuple-element.89.reads, s32[248]{0:T(256)S(1)} %compare_select_fusion.2.writes, bf16[576,256]{1,0:T(8,128)(2,1)S(1)} %collective-permute-done.29.refs_0_.refs_3_, ...), custom_call_target="tpu_custom_call" | custom-call | flops 3000000000 | bytes 12582912 | tf_op jit(solution)/shard_map/backward_own/pallas_call | solution.py:230
  118.6 2.1 %collective-permute-start.38 = (bf16[768,256]{1,0:T(8,128)(2,1)S(1)}, bf16[768,256]{1,0:T(8,128)(2,1)S(1)}, u32[]{:S(2)}, u32[]{:S(2)}) collective-permute-start(bf16[768,256]{1,0:T(8,128)(2,1)S(1)} %get-tuple-element.82), channel_id=1, source_target_pairs={{32,64},{64,32},{96,0},{0,96},{48,80},{80,48},{112,16},{16,112},{3... | collective-permute-start | bytes 1179656 | tf_op jit(solution)/shard_map/ppermute | solution.py:29
  120.6 10.3 %collective-permute-done.38.by_two = bf16[768,256]{1,0:T(8,128)(2,1)S(1)} collective-permute-done((bf16[768,256]{1,0:T(8,128)(2,1)S(1)}, bf16[768,256]{1,0:T(8,128)(2,1)S(1)}, u32[]{:S(2)}, u32[]{:S(2)}) %collective-permute-start.38) | collective-permute-done | bytes 393248 | tf_op jit(solution)/shard_map/ppermute | solution.py:29
  131.5 1.6 %collective-permute-start.39 = (bf16[384,256]{1,0:T(8,128)(2,1)S(1)}, bf16[384,256]{1,0:T(8,128)(2,1)S(1)}, u32[]{:S(2)}, u32[]{:S(2)}) collective-permute-start(bf16[384,256]{1,0:T(8,128)(2,1)S(1)} %get-tuple-element.85), channel_id=1, source_target_pairs={{32,64},{64,32},{96,0},{0,96},{48,80},{80,48},{112,16},{16,112},{3... | collective-permute-start | bytes 589832 | tf_op jit(solution)/shard_map/ppermute | solution.py:29
  133.1 5.4 %collective-permute-done.39.late_two = bf16[384,256]{1,0:T(8,128)(2,1)S(1)} collective-permute-done((bf16[384,256]{1,0:T(8,128)(2,1)S(1)}, bf16[384,256]{1,0:T(8,128)(2,1)S(1)}, u32[]{:S(2)}, u32[]{:S(2)}) %collective-permute-start.39) | collective-permute-done | bytes 196640 | tf_op jit(solution)/shard_map/ppermute | solution.py:29
  (108 shorter events, 27.2 us)
Async XLA Ops:
  0.6 9.5 %collective-permute-start.1 = (bf16[512,256]{1,0:T(8,128)(2,1)}, bf16[512,256]{1,0:T(8,128)(2,1)S(1)}, u32[]{:S(2)}, u32[]{:S(2)}) collective-permute-start(bf16[512,256]{1,0:T(8,128)(2,1)} %refs_0_.1), channel_id=1, source_target_pairs={{32,64},{64,32},{96,0},{0,96},{48,80},{80,48},{112,16},{16,112},{3... | collective-permute-start | bytes 786440 | tf_op jit(solution)/shard_map/ppermute | solution.py:29
  3.5 8.0 %collective-permute-start = (bf16[512,256]{1,0:T(8,128)(2,1)}, bf16[512,256]{1,0:T(8,128)(2,1)S(1)}, u32[]{:S(2)}, u32[]{:S(2)}) collective-permute-start(bf16[512,256]{1,0:T(8,128)(2,1)} %refs_0_.1), channel_id=1, source_target_pairs={{0,32},{32,0},{64,96},{96,64},{16,48},{48,16},{80,112},{112,80},{1... | collective-permute-start | bytes 786440 | tf_op jit(solution)/shard_map/ppermute | solution.py:29
  11.5 6.9 %collective-permute-start.3 = (bf16[256,256]{1,0:T(8,128)(2,1)S(1)}, bf16[256,256]{1,0:T(8,128)(2,1)S(1)}, u32[]{:S(2)}, u32[]{:S(2)}) collective-permute-start(bf16[256,256]{1,0:T(8,128)(2,1)S(1)} %get-tuple-element.47), channel_id=1, source_target_pairs={{0,32},{32,0},{64,96},{96,64},{16,48},{48,16},{80,112},{112,80},{1... | collective-permute-start | bytes 393224 | tf_op jit(solution)/shard_map/ppermute | solution.py:29
  12.0 6.5 %collective-permute-start.2 = (bf16[256,256]{1,0:T(8,128)(2,1)S(1)}, bf16[256,256]{1,0:T(8,128)(2,1)S(1)}, u32[]{:S(2)}, u32[]{:S(2)}) collective-permute-start(bf16[256,256]{1,0:T(8,128)(2,1)S(1)} %get-tuple-element.46.refs_0_), channel_id=1, source_target_pairs={{32,64},{64,32},{96,0},{0,96},{48,80},{80,48},{112,16},{16,112},{3... | collective-permute-start | bytes 393224 | tf_op jit(solution)/shard_map/ppermute | solution.py:29
  13.1 6.0 %collective-permute-start.4 = (bf16[512,256]{1,0:T(8,128)(2,1)}, bf16[512,256]{1,0:T(8,128)(2,1)S(1)}, u32[]{:S(2)}, u32[]{:S(2)}) collective-permute-start(bf16[512,256]{1,0:T(8,128)(2,1)} %refs_0_.1), channel_id=1, source_target_pairs={{0,16},{16,0},{32,48},{48,32},{64,80},{80,64},{96,112},{112,96},{1... | collective-permute-start | bytes 786440 | tf_op jit(solution)/shard_map/ppermute | solution.py:33
  13.1 6.0 %collective-permute-start.6 = (bf16[512,256]{1,0:T(8,128)(2,1)S(1)}, bf16[512,256]{1,0:T(8,128)(2,1)S(1)}, u32[]{:S(2)}, u32[]{:S(2)}) collective-permute-start(bf16[512,256]{1,0:T(8,128)(2,1)S(1)} %collective-permute-done.1.three_ref.refs_2_), channel_id=1, source_target_pairs={{0,16},{16,0},{32,48},{48,32},{64,80},{80,64},{96,112},{112,96},{1... | collective-permute-start | bytes 786440 | tf_op jit(solution)/shard_map/ppermute | solution.py:33
  23.4 16.4 %collective-permute-start.11 = (bf16[1024,256]{1,0:T(8,128)(2,1)S(1)}, bf16[1024,256]{1,0:T(8,128)(2,1)S(1)}, u32[]{:S(2)}, u32[]{:S(2)}) collective-permute-start(bf16[1024,256]{1,0:T(8,128)(2,1)S(1)} %get-tuple-element.55), channel_id=1, source_target_pairs={{0,2},{2,0},{1,3},{3,1},{4,6},{6,4},{5,7},{7,5},{8,10},{10,8},{9,1... | collective-permute-start | bytes 1572872 | tf_op jit(solution)/shard_map/ppermute | solution.py:26
  26.8 19.2 %collective-permute-start.14 = (bf16[1024,256]{1,0:T(8,128)(2,1)S(1)}, bf16[1024,256]{1,0:T(8,128)(2,1)S(1)}, u32[]{:S(2)}, u32[]{:S(2)}) collective-permute-start(bf16[1024,256]{1,0:T(8,128)(2,1)S(1)} %get-tuple-element.59), channel_id=1, source_target_pairs={{0,8},{8,0},{4,12},{12,4},{1,9},{9,1},{5,13},{13,5},{2,10},{10,2},... | collective-permute-start | bytes 1572872 | tf_op jit(solution)/shard_map/ppermute | solution.py:28
  34.6 15.9 %collective-permute-start.9 = (bf16[1024,256]{1,0:T(8,128)(2,1)S(1)}, bf16[1024,256]{1,0:T(8,128)(2,1)S(1)}, u32[]{:S(2)}, u32[]{:S(2)}) collective-permute-start(bf16[1024,256]{1,0:T(8,128)(2,1)S(1)} %get-tuple-element.53), channel_id=1, source_target_pairs={{0,1},{1,0},{2,3},{3,2},{4,5},{5,4},{6,7},{7,6},{8,9},{9,8},{10,11... | collective-permute-start | bytes 1572872 | tf_op jit(solution)/shard_map/ppermute | solution.py:26
  35.3 15.1 %collective-permute-start.10 = (bf16[1024,256]{1,0:T(8,128)(2,1)S(1)}, bf16[1024,256]{1,0:T(8,128)(2,1)S(1)}, u32[]{:S(2)}, u32[]{:S(2)}) collective-permute-start(bf16[1024,256]{1,0:T(8,128)(2,1)S(1)} %get-tuple-element.54), channel_id=1, source_target_pairs={{1,2},{2,1},{3,0},{0,3},{5,6},{6,5},{7,4},{4,7},{9,10},{10,9},{11,... | collective-permute-start | bytes 1572872 | tf_op jit(solution)/shard_map/ppermute | solution.py:26
  36.4 16.9 %collective-permute-start.12 = (bf16[1024,256]{1,0:T(8,128)(2,1)S(1)}, bf16[1024,256]{1,0:T(8,128)(2,1)S(1)}, u32[]{:S(2)}, u32[]{:S(2)}) collective-permute-start(bf16[1024,256]{1,0:T(8,128)(2,1)S(1)} %get-tuple-element.57), channel_id=1, source_target_pairs={{0,4},{4,0},{8,12},{12,8},{1,5},{5,1},{9,13},{13,9},{2,6},{6,2},{1... | collective-permute-start | bytes 1572872 | tf_op jit(solution)/shard_map/ppermute | solution.py:28
  39.8 13.9 %collective-permute-start.13 = (bf16[1024,256]{1,0:T(8,128)(2,1)S(1)}, bf16[1024,256]{1,0:T(8,128)(2,1)S(1)}, u32[]{:S(2)}, u32[]{:S(2)}) collective-permute-start(bf16[1024,256]{1,0:T(8,128)(2,1)S(1)} %get-tuple-element.58), channel_id=1, source_target_pairs={{4,8},{8,4},{12,0},{0,12},{5,9},{9,5},{13,1},{1,13},{6,10},{10,6},... | collective-permute-start | bytes 1572872 | tf_op jit(solution)/shard_map/ppermute | solution.py:28
  54.1 8.5 %collective-permute-start.15 = (bf16[256,256]{1,0:T(8,128)(2,1)S(1)}, bf16[256,256]{1,0:T(8,128)(2,1)S(1)}, u32[]{:S(2)}, u32[]{:S(2)}) collective-permute-start(bf16[256,256]{1,0:T(8,128)(2,1)S(1)} %get-tuple-element.61), channel_id=1, source_target_pairs={{0,4},{4,0},{8,12},{12,8},{1,5},{5,1},{9,13},{13,9},{2,6},{6,2},{1... | collective-permute-start | bytes 393224 | tf_op jit(solution)/shard_map/ppermute | solution.py:28
  55.9 10.1 %collective-permute-start.16 = (bf16[256,256]{1,0:T(8,128)(2,1)S(1)}, bf16[256,256]{1,0:T(8,128)(2,1)S(1)}, u32[]{:S(2)}, u32[]{:S(2)}) collective-permute-start(bf16[256,256]{1,0:T(8,128)(2,1)S(1)} %get-tuple-element.62), channel_id=1, source_target_pairs={{4,8},{8,4},{12,0},{0,12},{5,9},{9,5},{13,1},{1,13},{6,10},{10,6},... | collective-permute-start | bytes 393224 | tf_op jit(solution)/shard_map/ppermute | solution.py:28
  58.1 7.9 %collective-permute-start.17 = (bf16[256,256]{1,0:T(8,128)(2,1)S(1)}, bf16[256,256]{1,0:T(8,128)(2,1)S(1)}, u32[]{:S(2)}, u32[]{:S(2)}) collective-permute-start(bf16[256,256]{1,0:T(8,128)(2,1)S(1)} %get-tuple-element.63), channel_id=1, source_target_pairs={{0,8},{8,0},{4,12},{12,4},{1,9},{9,1},{5,13},{13,5},{2,10},{10,2},... | collective-permute-start | bytes 393224 | tf_op jit(solution)/shard_map/ppermute | solution.py:28
  59.6 6.4 %collective-permute-start.18 = (bf16[256,256]{1,0:T(8,128)(2,1)S(1)}, bf16[256,256]{1,0:T(8,128)(2,1)S(1)}, u32[]{:S(2)}, u32[]{:S(2)}) collective-permute-start(bf16[256,256]{1,0:T(8,128)(2,1)S(1)} %get-tuple-element.65), channel_id=1, source_target_pairs={{0,1},{1,0},{2,3},{3,2},{4,5},{5,4},{6,7},{7,6},{8,9},{9,8},{10,11... | collective-permute-start | bytes 393224 | tf_op jit(solution)/shard_map/ppermute | solution.py:26
  62.6 6.5 %collective-permute-start.20 = (bf16[256,256]{1,0:T(8,128)(2,1)S(1)}, bf16[256,256]{1,0:T(8,128)(2,1)S(1)}, u32[]{:S(2)}, u32[]{:S(2)}) collective-permute-start(bf16[256,256]{1,0:T(8,128)(2,1)S(1)} %get-tuple-element.67), channel_id=1, source_target_pairs={{0,2},{2,0},{1,3},{3,1},{4,6},{6,4},{5,7},{7,5},{8,10},{10,8},{9,1... | collective-permute-start | bytes 393224 | tf_op jit(solution)/shard_map/ppermute | solution.py:26
  70.4 8.8 %collective-permute-start.28 = (bf16[384,256]{1,0:T(8,128)(2,1)S(1)}, bf16[384,256]{1,0:T(8,128)(2,1)S(1)}, u32[]{:S(2)}, u32[]{:S(2)}) collective-permute-start(bf16[384,256]{1,0:T(8,128)(2,1)S(1)} %get-tuple-element.71.own), channel_id=1, source_target_pairs={{0,2},{2,0},{1,3},{3,1},{4,6},{6,4},{5,7},{7,5},{8,10},{10,8},{9,1... | collective-permute-start | bytes 589832 | tf_op jit(solution)/shard_map/ppermute | solution.py:26
  71.7 18.1 %collective-permute-start.23 = (bf16[384,256]{1,0:T(8,128)(2,1)S(1)}, bf16[384,256]{1,0:T(8,128)(2,1)S(1)}, u32[]{:S(2)}, u32[]{:S(2)}) collective-permute-start(bf16[384,256]{1,0:T(8,128)(2,1)S(1)} %get-tuple-element.70.own), channel_id=1, source_target_pairs={{0,8},{8,0},{4,12},{12,4},{1,9},{9,1},{5,13},{13,5},{2,10},{10,2},... | collective-permute-start | bytes 589832 | tf_op jit(solution)/shard_map/ppermute | solution.py:28
  73.7 16.2 %collective-permute-start.22 = (bf16[384,256]{1,0:T(8,128)(2,1)S(1)}, bf16[384,256]{1,0:T(8,128)(2,1)S(1)}, u32[]{:S(2)}, u32[]{:S(2)}) collective-permute-start(bf16[384,256]{1,0:T(8,128)(2,1)S(1)} %get-tuple-element.70.own), channel_id=1, source_target_pairs={{4,8},{8,4},{12,0},{0,12},{5,9},{9,5},{13,1},{1,13},{6,10},{10,6},... | collective-permute-start | bytes 589832 | tf_op jit(solution)/shard_map/ppermute | solution.py:28
  74.6 15.3 %collective-permute-start.21 = (bf16[384,256]{1,0:T(8,128)(2,1)S(1)}, bf16[384,256]{1,0:T(8,128)(2,1)S(1)}, u32[]{:S(2)}, u32[]{:S(2)}) collective-permute-start(bf16[384,256]{1,0:T(8,128)(2,1)S(1)} %get-tuple-element.70.own), channel_id=1, source_target_pairs={{0,4},{4,0},{8,12},{12,8},{1,5},{5,1},{9,13},{13,9},{2,6},{6,2},{1... | collective-permute-start | bytes 589832 | tf_op jit(solution)/shard_map/ppermute | solution.py:28
  84.9 16.0 %collective-permute-start.32 = (bf16[1152,256]{1,0:T(8,128)(2,1)S(1)}, bf16[1152,256]{1,0:T(8,128)(2,1)S(1)}, u32[]{:S(2)}, u32[]{:S(2)}) collective-permute-start(bf16[1152,256]{1,0:T(8,128)(2,1)S(1)} %gathered_b.1.refs_1_.refs_6_.refs_7_.refs_5_), channel_id=1, source_target_pairs={{4,8},{8,4},{12,0},{0,12},{5,9},{9,5},{13,1},{1,13},{6,10},{10,6},... | collective-permute-start | bytes 1769480 | tf_op jit(solution)/shard_map/ppermute | solution.py:28
  89.9 13.0 %collective-permute-start.31 = (bf16[1152,256]{1,0:T(8,128)(2,1)S(1)}, bf16[1152,256]{1,0:T(8,128)(2,1)S(1)}, u32[]{:S(2)}, u32[]{:S(2)}) collective-permute-start(bf16[1152,256]{1,0:T(8,128)(2,1)S(1)} %gathered_b.1.refs_1_.refs_6_.refs_7_.refs_5_), channel_id=1, source_target_pairs={{0,4},{4,0},{8,12},{12,8},{1,5},{5,1},{9,13},{13,9},{2,6},{6,2},{1... | collective-permute-start | bytes 1769480 | tf_op jit(solution)/shard_map/ppermute | solution.py:28
  90.0 14.3 %collective-permute-start.25 = (bf16[1152,256]{1,0:T(8,128)(2,1)S(1)}, bf16[1152,256]{1,0:T(8,128)(2,1)S(1)}, u32[]{:S(2)}, u32[]{:S(2)}) collective-permute-start(bf16[1152,256]{1,0:T(8,128)(2,1)S(1)} %gathered_a.1.refs_0_.refs_1_), channel_id=1, source_target_pairs={{1,2},{2,1},{3,0},{0,3},{5,6},{6,5},{7,4},{4,7},{9,10},{10,9},{11,... | collective-permute-start | bytes 1769480 | tf_op jit(solution)/shard_map/ppermute | solution.py:26
  90.0 14.2 %collective-permute-start.24 = (bf16[1152,256]{1,0:T(8,128)(2,1)S(1)}, bf16[1152,256]{1,0:T(8,128)(2,1)S(1)}, u32[]{:S(2)}, u32[]{:S(2)}) collective-permute-start(bf16[1152,256]{1,0:T(8,128)(2,1)S(1)} %gathered_a.1.refs_0_.refs_1_), channel_id=1, source_target_pairs={{0,1},{1,0},{2,3},{3,2},{4,5},{5,4},{6,7},{7,6},{8,9},{9,8},{10,11... | collective-permute-start | bytes 1769480 | tf_op jit(solution)/shard_map/ppermute | solution.py:26
  102.9 9.8 %collective-permute-start.33 = (bf16[576,256]{1,0:T(8,128)(2,1)S(1)}, bf16[576,256]{1,0:T(8,128)(2,1)S(1)}, u32[]{:S(2)}, u32[]{:S(2)}) collective-permute-start(bf16[576,256]{1,0:T(8,128)(2,1)S(1)} %get-tuple-element.75), channel_id=1, source_target_pairs={{4,8},{8,4},{12,0},{0,12},{5,9},{9,5},{13,1},{1,13},{6,10},{10,6},... | collective-permute-start | bytes 884744 | tf_op jit(solution)/shard_map/ppermute | solution.py:28
  104.2 8.5 %collective-permute-start.34 = (bf16[576,256]{1,0:T(8,128)(2,1)S(1)}, bf16[576,256]{1,0:T(8,128)(2,1)S(1)}, u32[]{:S(2)}, u32[]{:S(2)}) collective-permute-start(bf16[576,256]{1,0:T(8,128)(2,1)S(1)} %get-tuple-element.76), channel_id=1, source_target_pairs={{0,4},{4,0},{8,12},{12,8},{1,5},{5,1},{9,13},{13,9},{2,6},{6,2},{1... | collective-permute-start | bytes 884744 | tf_op jit(solution)/shard_map/ppermute | solution.py:28
  104.3 8.4 %collective-permute-start.29 = (bf16[576,256]{1,0:T(8,128)(2,1)S(1)}, bf16[576,256]{1,0:T(8,128)(2,1)S(1)}, u32[]{:S(2)}, u32[]{:S(2)}) collective-permute-start(bf16[576,256]{1,0:T(8,128)(2,1)S(1)} %get-tuple-element.73), channel_id=1, source_target_pairs={{1,2},{2,1},{3,0},{0,3},{5,6},{6,5},{7,4},{4,7},{9,10},{10,9},{11,... | collective-permute-start | bytes 884744 | tf_op jit(solution)/shard_map/ppermute | solution.py:26
  105.2 7.5 %collective-permute-start.30 = (bf16[576,256]{1,0:T(8,128)(2,1)S(1)}, bf16[576,256]{1,0:T(8,128)(2,1)S(1)}, u32[]{:S(2)}, u32[]{:S(2)}) collective-permute-start(bf16[576,256]{1,0:T(8,128)(2,1)S(1)} %get-tuple-element.74), channel_id=1, source_target_pairs={{0,1},{1,0},{2,3},{3,2},{4,5},{5,4},{6,7},{7,6},{8,9},{9,8},{10,11... | collective-permute-start | bytes 884744 | tf_op jit(solution)/shard_map/ppermute | solution.py:26
  118.6 12.4 %collective-permute-start.38 = (bf16[768,256]{1,0:T(8,128)(2,1)S(1)}, bf16[768,256]{1,0:T(8,128)(2,1)S(1)}, u32[]{:S(2)}, u32[]{:S(2)}) collective-permute-start(bf16[768,256]{1,0:T(8,128)(2,1)S(1)} %get-tuple-element.82), channel_id=1, source_target_pairs={{32,64},{64,32},{96,0},{0,96},{48,80},{80,48},{112,16},{16,112},{3... | collective-permute-start | bytes 1179656 | tf_op jit(solution)/shard_map/ppermute | solution.py:29
  120.6 10.8 %collective-permute-start.37 = (bf16[768,256]{1,0:T(8,128)(2,1)S(1)}, bf16[768,256]{1,0:T(8,128)(2,1)S(1)}, u32[]{:S(2)}, u32[]{:S(2)}) collective-permute-start(bf16[768,256]{1,0:T(8,128)(2,1)S(1)} %get-tuple-element.81.own_message), channel_id=1, source_target_pairs={{0,32},{32,0},{64,96},{96,64},{16,48},{48,16},{80,112},{112,80},{1... | collective-permute-start | bytes 1179656 | tf_op jit(solution)/shard_map/ppermute | solution.py:29
  131.5 7.0 %collective-permute-start.39 = (bf16[384,256]{1,0:T(8,128)(2,1)S(1)}, bf16[384,256]{1,0:T(8,128)(2,1)S(1)}, u32[]{:S(2)}, u32[]{:S(2)}) collective-permute-start(bf16[384,256]{1,0:T(8,128)(2,1)S(1)} %get-tuple-element.85), channel_id=1, source_target_pairs={{32,64},{64,32},{96,0},{0,96},{48,80},{80,48},{112,16},{16,112},{3... | collective-permute-start | bytes 589832 | tf_op jit(solution)/shard_map/ppermute | solution.py:29
  (12 other events, 75.0 us)

commit v2 on v1

--- a/solution.py
+++ b/solution.py
@@ -34,7 +34,7 @@
 
 
 def distance(here, there):
-    return jnp.where(here % 2 == 0, there - here, here - there) & 3
+    return ((1 - 2 * (here & 1)) * (there - here)) & 3
 
 
 def pick(index, table):
@@ -47,36 +47,90 @@
 ROLE = (6, 1, 0, 4, 7, 5, 2, 3)
 
 
-def plan(keys, source, live, segments):
-    total = keys.shape[0]
-    room = -(-(total + KEYS * (UNIT - 1) + len(segments) * GROUP) // GROUP) * GROUP
-    keys = jnp.where(live, keys, KEYS)
-    all_keys = jnp.arange(KEYS, dtype=jnp.int32)
-    segment_of = sum((all_keys >= first).astype(jnp.int32) for first, _ in segments) - 1
-    count = jnp.sum((keys[:, None] == all_keys[None, :]).astype(jnp.int32), 0)
-    padded = (count + UNIT - 1) // UNIT * UNIT
-    before = (all_keys[:, None] < all_keys[None, :]) & (segment_of[:, None] == segment_of[None, :])
-    offset = jnp.sum(jnp.where(before, padded[:, None], 0), 0)
-    bounds = [jnp.zeros((), jnp.int32)]
-    for index, (first, last) in enumerate(segments):
-        size = jnp.sum(jnp.where(segment_of == index, padded, 0))
-        offset = offset + jnp.where(segment_of == index, bounds[-1] * GROUP, 0)
-        bounds.append(bounds[-1] + (size + GROUP - 1) // GROUP)
-    slots = jnp.arange(total, dtype=jnp.int32)
-    rank = jnp.sum(((keys[:, None] == keys[None, :]) & (slots[None, :] < slots[:, None])).astype(jnp.int32), 1)
-    place = rank + jnp.sum(jnp.where(keys[:, None] == all_keys[None, :], offset[None, :], 0), 1)
-    place = jnp.where(live, place, -1)
+FORWARD = ((0, 8), (8, 16), (16, 32), (32, 48), (48, 64))
+BACKWARD = ((0, 32), (32, 48), (48, 64))
+ROOM = 640
+
+
+def sort_tiles(out, keys, source, live, segments):
+    total = keys.shape[1]
+
+    def iota(rows, lanes, axis):
+        return lax.broadcasted_iota(jnp.int32, (rows, lanes), axis).astype(F32)
+
+    def column(value):
+        return jnp.transpose(jnp.broadcast_to(value, (128, total)))
+
+    def segment_of(key):
+        return sum((key >= first).astype(F32) for first, _ in segments) - 1.0
+
     local = keys
     for first, _ in segments[1:]:
         local = jnp.where(keys >= first, keys - first, local)
-    spots = jnp.arange(room, dtype=jnp.int32)
-    hit = place[None, :] == spots[:, None]
-    order = jnp.sum(jnp.where(hit, slots[None, :], 0), 1)
-    reads = jnp.sum(jnp.where(hit, source[None, :] + 1, 0), 1)
-    hit_unit = place[None, :] == spots[::UNIT][:, None]
-    found = jnp.sum(jnp.where(hit_unit, local[None, :] + 1, 0), 1)
-    writes = jnp.where(found > 0, found - 1, DUMMY)
-    return jnp.stack(bounds), order, reads, writes
+    slots = lax.broadcasted_iota(jnp.int32, (1, total), 1)
+    payload = (slots + 512 * (source + 1) + 65536 * (local + 1)).astype(F32)
+    keys = jnp.where(live, keys, KEYS).astype(F32)
+    key_column = column(keys)
+    lane = iota(1, 128, 1)
+    count = jnp.sum(jnp.where(key_column == lane, 1.0, 0.0), 0, keepdims=True)
+    padded = jnp.where(lane < KEYS, ((count.astype(jnp.int32) + 1) >> 1 << 1).astype(F32), 0.0)
+    bounds = [jnp.zeros((1, 1), F32)]
+    for index in range(len(segments)):
+        size = jnp.sum(jnp.where(segment_of(lane) == index, padded, 0.0), 1, keepdims=True).astype(jnp.int32)
+        bounds.append(bounds[-1] + ((size + GROUP - 1) // GROUP).astype(F32))
+    key, before = iota(KEYS, 128, 0), iota(KEYS, 128, 1)
+    counted = (before < key) & (segment_of(before) == segment_of(key))
+    offset = jnp.sum(jnp.where(counted, padded, 0.0), 1, keepdims=True)
+    for index in range(len(segments)):
+        offset += jnp.where(segment_of(key[:, :1]) == index, GROUP * bounds[index], 0.0)
+    same = jnp.concatenate([key_column] * (total // 128), 1) == keys
+    rank = jnp.sum(jnp.where(same & (iota(total, total, 0) < iota(total, total, 1)), 1.0, 0.0), 0, keepdims=True)
+    start = jnp.sum(jnp.where(iota(KEYS, total, 0) == keys, offset, 0.0), 0, keepdims=True)
+    place_column = column(jnp.where(live, rank + start, -1.0))
+    payload_column = column(payload)
+    for block in range(ROOM // 128):
+        here = pl.ds(block * 128, 128)
+        found = jnp.sum(jnp.where(place_column == lane + 128.0 * block, payload_column, 0.0), 0, keepdims=True)
+        found = found.astype(jnp.int32)
+        out[0:1, here] = found & 511
+        out[1:2, here] = (found >> 9) & 127
+        out[2:3, here] = jnp.where(found == 0, DUMMY, (found >> 16) - 1)
+        out[3:4, here] = sum(jnp.where(lane >= index, bounds[index] - bounds[index - 1], 0.0) for index in range(1, len(bounds))).astype(jnp.int32)
+
+
+def plan(position, count, rows, cols):
+    def kernel(position_ref, count_ref, rows_ref, cols_ref, forward, backward):
+        x, core, y, z = [position_ref[k] for k in range(4)]
+        rows, cols = rows_ref[...], cols_ref[...]
+        live = lax.broadcasted_iota(jnp.int32, rows.shape, 1) < count_ref[0, 0]
+        y_away, z_away = distance(y, rows >> 4), distance(z, (rows >> 2) & 3)
+        second = (rows & 2) != 0
+        half = rows & 1
+        ring_one, ring_two = jnp.where(second, y_away, z_away), jnp.where(second, z_away, y_away)
+        base = jnp.where(second, pick(ring_one, (56, 16, 8, 24)), pick(ring_one, (48, 32, 0, 40)))
+        x_away, other = distance(x, cols >> 3), ((cols >> 2) & 1) ^ core
+        slot = x_away ^ (x_away >> 1)
+        source = other * 16 + slot * 4 + (cols & 3)
+        sort_tiles(forward, base + ring_two * 2 + half, source, live, FORWARD)
+        far = ring_one == 2
+        near_slot = ring_one ^ (ring_one >> 1)
+        inner = ring_two ^ (ring_two >> 1)
+        source = jnp.where(second, jnp.where(far, 8, 24 + near_slot * 8), jnp.where(far, 0, near_slot * 8))
+        source += half * 4 + inner
+        role = pick(((cols >> 1) & 1) * 4 + x_away, ROLE)
+        keys = jnp.where(far, 32, 0) + (1 - other) * 16 + role * 2 + (cols & 1)
+        sort_tiles(backward, keys, source, live, BACKWARD)
+
+    smem = pl.BlockSpec(memory_space=pltpu.SMEM)
+    vmem = pl.BlockSpec(memory_space=pltpu.VMEM)
+    return pl.pallas_call(
+        kernel,
+        in_specs=[smem, smem, vmem, vmem],
+        out_specs=[vmem] * 2,
+        out_shape=[jax.ShapeDtypeStruct((4, ROOM), jnp.int32)] * 2,
+        compiler_params=pltpu.CompilerParams(vmem_limit_bytes=8 << 20),
+        name="plan",
+    )(position, count, rows, cols)
 
 
 def load(tiles, *after):
@@ -169,22 +223,19 @@
         place += rows
 
 
-def aggregate(name, step, lists, pieces, tiles, outs, flipped, start=None, mark=False):
+def aggregate(name, step, lists, pieces, tiles, outs, flipped, start=None):
     whole = len(pieces) == 1
     n_pieces = len(pieces)
     total = pieces[0][2] if whole else BLK + sum(rows for _, _, rows in pieces)
     blocks = max(first + size for first, size, _ in outs)
 
-    def kernel(bounds, order, reads, writes, *refs):
+    def kernel(listed, *refs):
         source = refs[:n_pieces]
         held = refs[n_pieces]
         refs = refs[n_pieces + 1 :]
         if start is not None:
             start_ref, refs = refs[0], refs[1:]
         out_refs, refs = refs[: len(outs)], refs[len(outs) :]
-        if mark:
-            refs[0][...] = jnp.zeros_like(refs[0])
-            refs = refs[1:]
         acc = refs[0]
         if whole:
             slab = source[0]
@@ -197,13 +248,13 @@
             rows = pl.ds(pl.multiple_of(block * BLK, BLK), BLK)
             acc[rows] = jnp.zeros((BLK, acc.shape[1]), F32) if start is None else start_ref[rows]
 
-        @pl.loop(bounds[step], bounds[step + 1])
+        @pl.loop(listed[3, step], listed[3, step + 1])
         def _(group):
             for unit in range(UNROLL):
                 spots = [group * GROUP + unit * UNIT + k for k in range(UNIT)]
-                matrix = [held[order[spot]] for spot in spots]
-                read = [slab[pl.ds(pl.multiple_of(reads[spot] * BLK, BLK), BLK)] for spot in spots]
-                to = pl.ds(pl.multiple_of(writes[group * UNROLL + unit] * BLK, BLK), BLK)
+                matrix = [held[listed[0, spot]] for spot in spots]
+                read = [slab[pl.ds(pl.multiple_of(listed[1, spot] * BLK, BLK), BLK)] for spot in spots]
+                to = pl.ds(pl.multiple_of(listed[2, spots[0]] * BLK, BLK), BLK)
                 if flipped:
                     dims = (((0,), (0,)), ((), ()))
                     value = lax.dot_general(
@@ -229,15 +280,14 @@
         scratch.append(pltpu.VMEM((total, width), BF))
     return pl.pallas_call(
         kernel,
-        in_specs=[smem] * 4 + [vmem] * (n_pieces + 1 + len(extra)),
-        out_specs=[vmem] * (len(outs) + mark),
-        out_shape=[jax.ShapeDtypeStruct((size * BLK, width), dtype) for _, size, dtype in outs]
-        + [jax.ShapeDtypeStruct((8, 128), jnp.int32)] * mark,
+        in_specs=[smem] + [vmem] * (n_pieces + 1 + len(extra)),
+        out_specs=[vmem] * len(outs),
+        out_shape=[jax.ShapeDtypeStruct((size * BLK, width), dtype) for _, size, dtype in outs],
         scratch_shapes=scratch,
         compiler_params=pltpu.CompilerParams(vmem_limit_bytes=24 << 20),
-        cost_estimate=pl.CostEstimate(flops=3 * 10**9, bytes_accessed=12 << 20, transcendentals=0),
+        cost_estimate=pl.CostEstimate(flops=10**6, bytes_accessed=1 << 17, transcendentals=0),
         name=name,
-    )(*lists, *[array for array, _, _ in pieces], pltpu.with_memory_space_constraint(tiles, pltpu.VMEM), *extra)
+    )(lists, *[array for array, _, _ in pieces], pltpu.with_memory_space_constraint(tiles, pltpu.VMEM), *extra)
 
 
 def local(name, body, out_shape, *operands):
@@ -345,38 +395,15 @@
     tiles = tile_values[0, 0]
     near_one, near_two = swap(features, "x", ONE), swap(features, "x", TWO)
     across = swap_core(features)
-    rows, cols = tile_rows[0, 0], tile_cols[0, 0]
-    live = jnp.arange(rows.shape[0], dtype=jnp.int32) < tile_count[0, 0]
     row, col = lax.axis_index("row"), lax.axis_index("col")
-    x, core, y, z = row // 2, row % 2, col // 4, col % 4
-
-    sub = rows % 4
-    y_away, z_away = distance(y, rows // 16), distance(z, rows // 4 % 4)
-    second = sub >= 2
-    half = sub % 2
-    ring_one, ring_two = jnp.where(second, y_away, z_away), jnp.where(second, z_away, y_away)
-    within = ring_two * 2 + half
-    base = pick(ring_one, (48, 16, 0, 24))
-    forward_key = base + jnp.where(second, jnp.where(ring_one % 2 == 1, 16, 8), 0) + within
-    x_away, other = distance(x, cols // 8), (cols // 4 % 2) ^ core
-    slot = x_away ^ (x_away >> 1)
-    forward_source = other * 16 + slot * 4 + cols % 4
-    far = ring_one == 2
-    near_slot = ring_one ^ (ring_one >> 1)
-    inner = ring_two ^ (ring_two >> 1)
-    backward_source = jnp.where(far, second * 8, second * 24 + near_slot * 8) + half * 4 + inner
-    backward_role = pick(cols % 4 // 2 * 4 + x_away, ROLE)
-    backward_key = jnp.where(far, 32, 0) + (1 - other) * 16 + backward_role * 2 + cols % 2
-
-    forward = plan(forward_key, forward_source, live, ((0, 16), (16, 48), (48, 64)))
-
-    far_first, far_second = cut(near_one, near_two, *forward)
-    held_tiles, loaded = load(tiles, far_first)
-    far_first, far_second = swap(far_first, "x", TWO), swap(far_second, "x", ONE)
-    far_first, far_second = relay((far_first, far_second), loaded)
+    position = jnp.stack([row // 2, row % 2, col // 4, col % 4]).astype(jnp.int32)
+    forward, backward = plan(position, tile_count, tile_rows[0], tile_cols[0])
+
+    far_away = swap(features, "x", FAR)
+    held_tiles, loaded = load(tiles, forward, backward)
+    (far_away,) = relay((far_away,), loaded)
     across_near = [swap_core(near_one), swap_core(near_two)]
-    across_far = [swap_core(far_first), swap_core(far_second)]
-    held = [features, near_one, near_two, far_first, far_second, across, *across_near, *across_far]
+    held = [features, near_one, near_two, far_away, across, *across_near, swap_core(far_away)]
     slab = assemble(held)
     pieces = [(slab, 0, slab.shape[0])]
 
@@ -386,17 +413,15 @@
     def out(*dtypes):
         return [(8 * k, 8, dtype) for k, dtype in enumerate(dtypes)]
 
-    a_two, b_two = aggregate("forward_far", 0, forward, pieces, held_tiles, out(BF, BF), False)
-    a_two, b_two = swap(a_two, "z", FAR), swap(b_two, "y", FAR)
-    a_one, a_three, b_one, b_three = aggregate(
-        "forward_near", 1, forward, pieces, held_tiles, out(BF, BF, BF, BF), False
-    )
+    (a_two,) = aggregate("forward_far_a", 0, forward, pieces, held_tiles, out(BF), False)
+    a_two = swap(a_two, "z", FAR)
+    (b_two,) = aggregate("forward_far_b", 1, forward, pieces, held_tiles, out(BF), False)
+    b_two = swap(b_two, "y", FAR)
+    b_one, b_three = aggregate("forward_near_b", 2, forward, pieces, held_tiles, out(BF, BF), False)
+    b_one, b_three = swap(b_one, "y", ONE), swap(b_three, "y", TWO)
+    a_one, a_three = aggregate("forward_near_a", 3, forward, pieces, held_tiles, out(BF, BF), False)
     a_one, a_three = swap(a_one, "z", ONE), swap(a_three, "z", TWO)
-    b_one, b_three = swap(b_one, "y", ONE), swap(b_three, "y", TWO)
-    a_own, b_own, after = aggregate("forward_own", 2, forward, pieces, held_tiles, out(F32, F32), False, None, True)
-    backward = plan(
-        backward_key + after[0, 0], backward_source + after[0, 0], live, ((0, 32), (32, 48), (48, 64))
-    )
+    a_own, b_own = aggregate("forward_own", 4, forward, pieces, held_tiles, out(F32, F32), False)
     second_shapes = [shape(256, F32), shape(256), shape(256), shape(256)]
     a_own, a_one, a_two, a_three, b_own, b_one, b_two, b_three = local(
         "second_phase", second_phase, second_shapes * 2,

time: 141 us -> 136 us (0.965)
  other arithmetic: 5.87 us -> 0.08 us
  starting transfers between devices: 45.5 us -> 50.8 us
  between operations: 5.79 us -> 1.57 us
    ppermute x13, waiting for transfers between devices: 17.9 us -> 4.9 us  [swap(): lax.ppermute(value, 'col', [(y * 4 + a, y * 4 + b) for y in range(4) for...]
    ppermute x13, waiting for transfers between devices: 10.1 us -> 22.1 us  [swap(): lax.ppermute(value, 'col', [(a * 4 + z, b * 4 + z) for z in range(4) for...]
    ppermute x13, starting transfers between devices: 14.8 us -> 20.5 us  [swap(): lax.ppermute(value, 'col', [(y * 4 + a, y * 4 + b) for y in range(4) for...]
    reduce_sum x14 -> x0, other arithmetic: 3.53 us -> none  [the longest x2 1.52 us: plan(): size = jnp.sum(jnp.where(segment_of == index, padded, 0))]
    ppermute x8 -> x7, starting transfers between devices: 8.36 us -> 11.5 us  [swap(): lax.ppermute(value, 'row', [(a * 2 + k, b * 2 + k) for k in range(2) for...]
    ppermute x13, starting transfers between devices: 20.4 us -> 17.4 us  [swap(): lax.ppermute(value, 'col', [(a * 4 + z, b * 4 + z) for z in range(4) for...]
    ppermute x8 -> x7, waiting for transfers between devices: 18 us -> 19.7 us  [swap(): lax.ppermute(value, 'row', [(a * 2 + k, b * 2 + k) for k in range(2) for...]
    pallas_call x6 -> x9, Pallas kernels: 21.8 us -> 20.8 us  [the longest x8 19.5 us: aggregate(): pl.pallas_call(kernel, in_specs=[smem] + [vmem] * (n_pieces + 1 + len(ext...]
  transfers between devices with their start and end apart: 41 -> 39, of which waited for: 18 -> 18; matrix products, arithmetic and copies ran while one was open for 5% -> 0% of each run, Pallas kernels for 19% -> 20%
where the time goes in v2:
time: 136 us
  starting transfers between devices  50.8 us (37%)
  waiting for transfers between devices  48.7 us (36%)
  Pallas kernels  33.5 us (25%)
  between operations  1.57 us (1%)
  local copies, waits for them, and re-layouts  1.38 us (1%)
    ppermute x13, waiting for transfers between devices, swap(): lax.ppermute(value, 'col', [(a * 4 + z, b * 4 + z) for z in range(4) for...  22.1 us
    ppermute x13, starting transfers between devices, swap(): lax.ppermute(value, 'col', [(y * 4 + a, y * 4 + b) for y in range(4) for...  20.5 us
    ppermute x7, waiting for transfers between devices, swap(): lax.ppermute(value, 'row', [(a * 2 + k, b * 2 + k) for k in range(2) for...  19.7 us
    pallas_call x8, Pallas kernels, aggregate(): pl.pallas_call(kernel, in_specs=[smem] + [vmem] * (n_pieces + 1 + len(ext...  19.5 us
    ppermute x13, starting transfers between devices, swap(): lax.ppermute(value, 'col', [(a * 4 + z, b * 4 + z) for z in range(4) for...  17.4 us
    ppermute x7, starting transfers between devices, swap(): lax.ppermute(value, 'row', [(a * 2 + k, b * 2 + k) for k in range(2) for...  11.5 us
    pallas_call x2, Pallas kernels, load(): pl.pallas_call(kernel, in_specs=[pl.BlockSpec(memory_space=pltpu.HBM)] +...  9.44 us
    ppermute x13, waiting for transfers between devices, swap(): lax.ppermute(value, 'col', [(y * 4 + a, y * 4 + b) for y in range(4) for...  4.9 us
  transfers between devices with their start and end apart: 39, of which 18 were waited for; matrix products, arithmetic and copies ran while one was open for 0% of the time, Pallas kernels for 20%

profile of v2, /device:TPU:32, one launch (start us, length us, event | category | flops | bytes accessed | tf_op | source)
XLA Modules:
  0.0 136.0 jit_solution(6391191349993874126)
XLA Ops:
  0.6 2.8 %collective-permute-start.1 = (bf16[512,256]{1,0:T(8,128)(2,1)}, bf16[512,256]{1,0:T(8,128)(2,1)S(1)}, u32[]{:S(2)}, u32[]{:S(2)}) collective-permute-start(bf16[512,256]{1,0:T(8,128)(2,1)} %refs_0_.1), channel_id=1, source_target_pairs={{32,64},{64,32},{96,0},{0,96},{48,80},{80,48},{112,16},{16,112},{3... | collective-permute-start | bytes 786440 | tf_op jit(solution)/shard_map/ppermute | solution.py:29
  3.7 1.7 %collective-permute-start.2 = (bf16[512,256]{1,0:T(8,128)(2,1)}, bf16[512,256]{1,0:T(8,128)(2,1)S(1)}, u32[]{:S(2)}, u32[]{:S(2)}) collective-permute-start(bf16[512,256]{1,0:T(8,128)(2,1)} %refs_0_.1), channel_id=1, source_target_pairs={{0,64},{64,0},{32,96},{96,32},{16,80},{80,16},{48,112},{112,48},{1... | collective-permute-start | bytes 786440 | tf_op jit(solution)/shard_map/ppermute | solution.py:29
  8.8 4.7 %load_tiles.2 = (bf16[384,128,128]{2,1,0:T(8,128)(2,1)S(1)}, s32[8,128]{1,0:T(8,128)S(1)}) custom-call(bf16[384,128,128]{2,1,0:T(8,128)(2,1)} %bitcast.9, s32[4,640]{1,0:T(4,128)S(1)} %get-tuple-element.41.refs_0_.listed, s32[4,640]{1,0:T(4,128)S(1)} %get-tuple-element.42.refs_1_.listed), custom_call_target="tpu_custom_call" | custom-call | bytes 26214400 | tf_op jit(solution)/shard_map/load_tiles/pallas_call | solution.py:152
  14.2 2.7 %collective-permute-done.2.refs_0_ = bf16[512,256]{1,0:T(8,128)(2,1)S(1)} collective-permute-done((bf16[512,256]{1,0:T(8,128)(2,1)}, bf16[512,256]{1,0:T(8,128)(2,1)S(1)}, u32[]{:S(2)}, u32[]{:S(2)}) %collective-permute-start.2) | collective-permute-done | bytes 262176 | tf_op jit(solution)/shard_map/ppermute | solution.py:29
  18.8 1.5 %forward_far_a.1 = bf16[1024,256]{1,0:T(8,128)(2,1)S(1)} custom-call(s32[4,640]{1,0:T(4,128)S(1)} %get-tuple-element.41.refs_0_.listed, bf16[4224,256]{1,0:T(8,128)(2,1)S(1)} %assemble.1.refs_0_, bf16[384,128,128]{2,1,0:T(8,128)(2,1)S(1)} %get-tuple-element.44.refs_1_), custom_call_target="tpu_custom_call" | custom-call | flops 1000000 | bytes 131072 | tf_op jit(solution)/shard_map/forward_far_a/pallas_call | solution.py:281
  20.3 3.4 %collective-permute-start.9 = (bf16[1024,256]{1,0:T(8,128)(2,1)S(1)}, bf16[1024,256]{1,0:T(8,128)(2,1)S(1)}, u32[]{:S(2)}, u32[]{:S(2)}) collective-permute-start(bf16[1024,256]{1,0:T(8,128)(2,1)S(1)} %forward_far_a.1), channel_id=1, source_target_pairs={{0,2},{2,0},{1,3},{3,1},{4,6},{6,4},{5,7},{7,5},{8,10},{10,8},{9,1... | collective-permute-start | bytes 1572872 | tf_op jit(solution)/shard_map/ppermute | solution.py:26
  23.7 1.5 %forward_far_b.1 = bf16[1024,256]{1,0:T(8,128)(2,1)S(1)} custom-call(s32[4,640]{1,0:T(4,128)S(1)} %get-tuple-element.41.refs_0_.listed, bf16[4224,256]{1,0:T(8,128)(2,1)S(1)} %assemble.1.refs_0_, bf16[384,128,128]{2,1,0:T(8,128)(2,1)S(1)} %get-tuple-element.44.refs_1_), custom_call_target="tpu_custom_call" | custom-call | flops 1000000 | bytes 131072 | tf_op jit(solution)/shard_map/forward_far_b/pallas_call | solution.py:281
  25.2 3.3 %collective-permute-start.12 = (bf16[1024,256]{1,0:T(8,128)(2,1)S(1)}, bf16[1024,256]{1,0:T(8,128)(2,1)S(1)}, u32[]{:S(2)}, u32[]{:S(2)}) collective-permute-start(bf16[1024,256]{1,0:T(8,128)(2,1)S(1)} %forward_far_b.1), channel_id=1, source_target_pairs={{0,8},{8,0},{4,12},{12,4},{1,9},{9,1},{5,13},{13,5},{2,10},{10,2},... | collective-permute-start | bytes 1572872 | tf_op jit(solution)/shard_map/ppermute | solution.py:28
  28.5 2.4 %forward_near_b.1 = (bf16[1024,256]{1,0:T(8,128)(2,1)S(1)}, bf16[1024,256]{1,0:T(8,128)(2,1)S(1)}) custom-call(s32[4,640]{1,0:T(4,128)S(1)} %get-tuple-element.41.refs_0_.listed, bf16[4224,256]{1,0:T(8,128)(2,1)S(1)} %assemble.1.refs_0_, bf16[384,128,128]{2,1,0:T(8,128)(2,1)S(1)} %get-tuple-element.44.refs_1_), custom_call_target="tpu_custom_call" | custom-call | flops 1000000 | bytes 131072 | tf_op jit(solution)/shard_map/forward_near_b/pallas_call | solution.py:281
  32.9 2.4 %forward_near_a.1 = (bf16[1024,256]{1,0:T(8,128)(2,1)S(1)}, bf16[1024,256]{1,0:T(8,128)(2,1)S(1)}) custom-call(s32[4,640]{1,0:T(4,128)S(1)} %get-tuple-element.41.refs_0_.listed, bf16[4224,256]{1,0:T(8,128)(2,1)S(1)} %assemble.1.refs_0_, bf16[384,128,128]{2,1,0:T(8,128)(2,1)S(1)} %get-tuple-element.44.refs_1_), custom_call_target="tpu_custom_call" | custom-call | flops 1000000 | bytes 131072 | tf_op jit(solution)/shard_map/forward_near_a/pallas_call | solution.py:281
  35.3 2.0 %collective-permute-start.7 = (bf16[1024,256]{1,0:T(8,128)(2,1)S(1)}, bf16[1024,256]{1,0:T(8,128)(2,1)S(1)}, u32[]{:S(2)}, u32[]{:S(2)}) collective-permute-start(bf16[1024,256]{1,0:T(8,128)(2,1)S(1)} %get-tuple-element.46), channel_id=1, source_target_pairs={{0,1},{1,0},{2,3},{3,2},{4,5},{5,4},{6,7},{7,6},{8,9},{9,8},{10,11... | collective-permute-start | bytes 1572872 | tf_op jit(solution)/shard_map/ppermute | solution.py:26
  37.8 2.4 %forward_own.1 = (f32[1024,256]{1,0:T(8,128)S(1)}, f32[1024,256]{1,0:T(8,128)S(1)}) custom-call(s32[4,640]{1,0:T(4,128)S(1)} %get-tuple-element.41.refs_0_.listed, bf16[4224,256]{1,0:T(8,128)(2,1)S(1)} %assemble.1.refs_0_, bf16[384,128,128]{2,1,0:T(8,128)(2,1)S(1)} %get-tuple-element.44.refs_1_), custom_call_target="tpu_custom_call" | custom-call | flops 1000000 | bytes 131072 | tf_op jit(solution)/shard_map/forward_own/pallas_call | solution.py:281
  41.7 10.8 %collective-permute-done.10.refs_5_ = bf16[1024,256]{1,0:T(8,128)(2,1)S(1)} collective-permute-done((bf16[1024,256]{1,0:T(8,128)(2,1)S(1)}, bf16[1024,256]{1,0:T(8,128)(2,1)S(1)}, u32[]{:S(2)}, u32[]{:S(2)}) %collective-permute-start.10) | collective-permute-done | bytes 524320 | tf_op jit(solution)/shard_map/ppermute | solution.py:28
  53.7 2.0 %collective-permute-start.14 = (bf16[256,256]{1,0:T(8,128)(2,1)S(1)}, bf16[256,256]{1,0:T(8,128)(2,1)S(1)}, u32[]{:S(2)}, u32[]{:S(2)}) collective-permute-start(bf16[256,256]{1,0:T(8,128)(2,1)S(1)} %get-tuple-element.53), channel_id=1, source_target_pairs={{4,8},{8,4},{12,0},{0,12},{5,9},{9,5},{13,1},{1,13},{6,10},{10,6},... | collective-permute-start | bytes 393224 | tf_op jit(solution)/shard_map/ppermute | solution.py:28
  59.5 1.8 %collective-permute-start.18 = (bf16[256,256]{1,0:T(8,128)(2,1)S(1)}, bf16[256,256]{1,0:T(8,128)(2,1)S(1)}, u32[]{:S(2)}, u32[]{:S(2)}) collective-permute-start(bf16[256,256]{1,0:T(8,128)(2,1)S(1)} %get-tuple-element.58), channel_id=1, source_target_pairs={{0,2},{2,0},{1,3},{3,1},{4,6},{6,4},{5,7},{7,5},{8,10},{10,8},{9,1... | collective-permute-start | bytes 393224 | tf_op jit(solution)/shard_map/ppermute | solution.py:26
  61.5 1.8 %collective-permute-done.15.refs_3_ = bf16[256,256]{1,0:T(8,128)(2,1)S(1)} collective-permute-done((bf16[256,256]{1,0:T(8,128)(2,1)S(1)}, bf16[256,256]{1,0:T(8,128)(2,1)S(1)}, u32[]{:S(2)}, u32[]{:S(2)}) %collective-permute-start.15) | collective-permute-done | bytes 131104 | tf_op jit(solution)/shard_map/ppermute | solution.py:28
  67.2 2.0 %collective-permute-start.26 = (bf16[384,256]{1,0:T(8,128)(2,1)S(1)}, bf16[384,256]{1,0:T(8,128)(2,1)S(1)}, u32[]{:S(2)}, u32[]{:S(2)}) collective-permute-start(bf16[384,256]{1,0:T(8,128)(2,1)S(1)} %get-tuple-element.61.own), channel_id=1, source_target_pairs={{0,2},{2,0},{1,3},{3,1},{4,6},{6,4},{5,7},{7,5},{8,10},{10,8},{9,1... | collective-permute-start | bytes 589832 | tf_op jit(solution)/shard_map/ppermute | solution.py:26
  71.9 2.2 %collective-permute-start.21 = (bf16[384,256]{1,0:T(8,128)(2,1)S(1)}, bf16[384,256]{1,0:T(8,128)(2,1)S(1)}, u32[]{:S(2)}, u32[]{:S(2)}) collective-permute-start(bf16[384,256]{1,0:T(8,128)(2,1)S(1)} %get-tuple-element.60.own), channel_id=1, source_target_pairs={{0,8},{8,0},{4,12},{12,4},{1,9},{9,1},{5,13},{13,5},{2,10},{10,2},... | collective-permute-start | bytes 589832 | tf_op jit(solution)/shard_map/ppermute | solution.py:28
  78.2 1.9 %collective-permute-start.30 = (bf16[1152,256]{1,0:T(8,128)(2,1)S(1)}, bf16[1152,256]{1,0:T(8,128)(2,1)S(1)}, u32[]{:S(2)}, u32[]{:S(2)}) collective-permute-start(bf16[1152,256]{1,0:T(8,128)(2,1)S(1)} %gathered_b.1.refs_1_.refs_6_.refs_7_.refs_5_), channel_id=1, source_target_pairs={{4,8},{8,4},{12,0},{0,12},{5,9},{9,5},{13,1},{1,13},{6,10},{10,6},... | collective-permute-start | bytes 1769480 | tf_op jit(solution)/shard_map/ppermute | solution.py:28
  80.1 3.7 %collective-permute-done.20.three = bf16[384,256]{1,0:T(8,128)(2,1)S(1)} collective-permute-done((bf16[384,256]{1,0:T(8,128)(2,1)S(1)}, bf16[384,256]{1,0:T(8,128)(2,1)S(1)}, u32[]{:S(2)}, u32[]{:S(2)}) %collective-permute-start.20) | collective-permute-done | bytes 196640 | tf_op jit(solution)/shard_map/ppermute | solution.py:28
  85.7 4.7 %load_tiles.3 = (bf16[384,128,128]{2,1,0:T(8,128)(2,1)S(1)}, s32[8,128]{1,0:T(8,128)S(1)}) custom-call(bf16[384,128,128]{2,1,0:T(8,128)(2,1)} %bitcast.10, bf16[1152,256]{1,0:T(8,128)(2,1)S(1)} %gathered_a.1.refs_0_.refs_1_, bf16[1152,256]{1,0:T(8,128)(2,1)S(1)} %gathered_b.1.refs_1_.refs_6_.refs_7_.refs_5_), custom_call_target="tpu_custom_call" | custom-call | bytes 26214400 | tf_op jit(solution)/shard_map/load_tiles/pallas_call | solution.py:152
  90.4 4.1 %collective-permute-done.30.three_ref.refs_10_.refs_11_.refs_7_ = bf16[1152,256]{1,0:T(8,128)(2,1)S(1)} collective-permute-done((bf16[1152,256]{1,0:T(8,128)(2,1)S(1)}, bf16[1152,256]{1,0:T(8,128)(2,1)S(1)}, u32[]{:S(2)}, u32[]{:S(2)}) %collective-permute-start.30) | collective-permute-done | bytes 589856 | tf_op jit(solution)/shard_map/ppermute | solution.py:28
  94.5 2.1 %collective-permute-start.31 = (bf16[576,256]{1,0:T(8,128)(2,1)S(1)}, bf16[576,256]{1,0:T(8,128)(2,1)S(1)}, u32[]{:S(2)}, u32[]{:S(2)}) collective-permute-start(bf16[576,256]{1,0:T(8,128)(2,1)S(1)} %get-tuple-element.65), channel_id=1, source_target_pairs={{4,8},{8,4},{12,0},{0,12},{5,9},{9,5},{13,1},{1,13},{6,10},{10,6},... | collective-permute-start | bytes 884744 | tf_op jit(solution)/shard_map/ppermute | solution.py:28
  96.7 1.6 %collective-permute-start.27 = (bf16[576,256]{1,0:T(8,128)(2,1)S(1)}, bf16[576,256]{1,0:T(8,128)(2,1)S(1)}, u32[]{:S(2)}, u32[]{:S(2)}) collective-permute-start(bf16[576,256]{1,0:T(8,128)(2,1)S(1)} %get-tuple-element.63), channel_id=1, source_target_pairs={{1,2},{2,1},{3,0},{0,3},{5,6},{6,5},{7,4},{4,7},{9,10},{10,9},{11,... | collective-permute-start | bytes 884744 | tf_op jit(solution)/shard_map/ppermute | solution.py:26
  98.3 2.3 %collective-permute-start.28 = (bf16[576,256]{1,0:T(8,128)(2,1)S(1)}, bf16[576,256]{1,0:T(8,128)(2,1)S(1)}, u32[]{:S(2)}, u32[]{:S(2)}) collective-permute-start(bf16[576,256]{1,0:T(8,128)(2,1)S(1)} %get-tuple-element.64), channel_id=1, source_target_pairs={{0,1},{1,0},{2,3},{3,2},{4,5},{5,4},{6,7},{7,6},{8,9},{9,8},{10,11... | collective-permute-start | bytes 884744 | tf_op jit(solution)/shard_map/ppermute | solution.py:26
  100.6 5.2 %backward_near.1 = (f32[2048,256]{1,0:T(8,128)S(1)}, f32[2048,256]{1,0:T(8,128)S(1)}) custom-call(s32[4,640]{1,0:T(4,128)S(1)} %get-tuple-element.42.refs_1_.listed, bf16[1152,256]{1,0:T(8,128)(2,1)S(1)} %gathered_a.1.refs_0_.refs_1_, bf16[1152,256]{1,0:T(8,128)(2,1)S(1)} %gathered_a.1.refs_0_.refs_1_, ...), custom_call_target="tpu_custom_call" | custom-call | flops 1000000 | bytes 131072 | tf_op jit(solution)/shard_map/backward_near/pallas_call | solution.py:281
  105.9 2.2 %backward_other.1 = bf16[2048,256]{1,0:T(8,128)(2,1)S(1)} custom-call(s32[4,640]{1,0:T(4,128)S(1)} %get-tuple-element.42.refs_1_.listed, bf16[576,256]{1,0:T(8,128)(2,1)S(1)} %collective-permute-done.27.refs_0_.refs_3_, bf16[576,256]{1,0:T(8,128)(2,1)S(1)} %collective-permute-done.28.refs_1_.refs_4_, ...), custom_call_target="tpu_custom_call" | custom-call | flops 1000000 | bytes 131072 | tf_op jit(solution)/shard_map/backward_other/pallas_call | solution.py:281
  108.8 1.9 %backward_own.1.own = f32[2048,256]{1,0:T(8,128)S(1)} custom-call(s32[4,640]{1,0:T(4,128)S(1)} %get-tuple-element.42.refs_1_.listed, bf16[576,256]{1,0:T(8,128)(2,1)S(1)} %collective-permute-done.27.refs_0_.refs_3_, bf16[576,256]{1,0:T(8,128)(2,1)S(1)} %collective-permute-done.28.refs_1_.refs_4_, ...), custom_call_target="tpu_custom_call" | custom-call | flops 1000000 | bytes 131072 | tf_op jit(solution)/shard_map/backward_own/pallas_call | solution.py:281
  111.4 5.2 %collective-permute-start.36 = (bf16[768,256]{1,0:T(8,128)(2,1)S(1)}, bf16[768,256]{1,0:T(8,128)(2,1)S(1)}, u32[]{:S(2)}, u32[]{:S(2)}) collective-permute-start(bf16[768,256]{1,0:T(8,128)(2,1)S(1)} %get-tuple-element.72), channel_id=1, source_target_pairs={{32,64},{64,32},{96,0},{0,96},{48,80},{80,48},{112,16},{16,112},{3... | collective-permute-start | bytes 1179656 | tf_op jit(solution)/shard_map/ppermute | solution.py:29
  116.6 9.5 %collective-permute-done.36.by_two = bf16[768,256]{1,0:T(8,128)(2,1)S(1)} collective-permute-done((bf16[768,256]{1,0:T(8,128)(2,1)S(1)}, bf16[768,256]{1,0:T(8,128)(2,1)S(1)}, u32[]{:S(2)}, u32[]{:S(2)}) %collective-permute-start.36) | collective-permute-done | bytes 393248 | tf_op jit(solution)/shard_map/ppermute | solution.py:29
  127.6 1.6 %collective-permute-start.37 = (bf16[384,256]{1,0:T(8,128)(2,1)S(1)}, bf16[384,256]{1,0:T(8,128)(2,1)S(1)}, u32[]{:S(2)}, u32[]{:S(2)}) collective-permute-start(bf16[384,256]{1,0:T(8,128)(2,1)S(1)} %get-tuple-element.75), channel_id=1, source_target_pairs={{32,64},{64,32},{96,0},{0,96},{48,80},{80,48},{112,16},{16,112},{3... | collective-permute-start | bytes 589832 | tf_op jit(solution)/shard_map/ppermute | solution.py:29
  129.2 5.6 %collective-permute-done.37.late_two = bf16[384,256]{1,0:T(8,128)(2,1)S(1)} collective-permute-done((bf16[384,256]{1,0:T(8,128)(2,1)S(1)}, bf16[384,256]{1,0:T(8,128)(2,1)S(1)}, u32[]{:S(2)}, u32[]{:S(2)}) %collective-permute-start.37) | collective-permute-done | bytes 196640 | tf_op jit(solution)/shard_map/ppermute | solution.py:29
  (80 shorter events, 31.4 us)
Async XLA Ops:
  0.6 12.9 %collective-permute-start.1 = (bf16[512,256]{1,0:T(8,128)(2,1)}, bf16[512,256]{1,0:T(8,128)(2,1)S(1)}, u32[]{:S(2)}, u32[]{:S(2)}) collective-permute-start(bf16[512,256]{1,0:T(8,128)(2,1)} %refs_0_.1), channel_id=1, source_target_pairs={{32,64},{64,32},{96,0},{0,96},{48,80},{80,48},{112,16},{16,112},{3... | collective-permute-start | bytes 786440 | tf_op jit(solution)/shard_map/ppermute | solution.py:29
  3.5 10.7 %collective-permute-start = (bf16[512,256]{1,0:T(8,128)(2,1)}, bf16[512,256]{1,0:T(8,128)(2,1)S(1)}, u32[]{:S(2)}, u32[]{:S(2)}) collective-permute-start(bf16[512,256]{1,0:T(8,128)(2,1)} %refs_0_.1), channel_id=1, source_target_pairs={{0,32},{32,0},{64,96},{96,64},{16,48},{48,16},{80,112},{112,80},{1... | collective-permute-start | bytes 786440 | tf_op jit(solution)/shard_map/ppermute | solution.py:29
  3.7 13.3 %collective-permute-start.2 = (bf16[512,256]{1,0:T(8,128)(2,1)}, bf16[512,256]{1,0:T(8,128)(2,1)S(1)}, u32[]{:S(2)}, u32[]{:S(2)}) collective-permute-start(bf16[512,256]{1,0:T(8,128)(2,1)} %refs_0_.1), channel_id=1, source_target_pairs={{0,64},{64,0},{32,96},{96,32},{16,80},{80,16},{48,112},{112,48},{1... | collective-permute-start | bytes 786440 | tf_op jit(solution)/shard_map/ppermute | solution.py:29
  5.4 11.7 %collective-permute-start.3 = (bf16[512,256]{1,0:T(8,128)(2,1)}, bf16[512,256]{1,0:T(8,128)(2,1)S(1)}, u32[]{:S(2)}, u32[]{:S(2)}) collective-permute-start(bf16[512,256]{1,0:T(8,128)(2,1)} %refs_0_.1), channel_id=1, source_target_pairs={{0,16},{16,0},{32,48},{48,32},{64,80},{80,64},{96,112},{112,96},{1... | collective-permute-start | bytes 786440 | tf_op jit(solution)/shard_map/ppermute | solution.py:33
  20.3 17.0 %collective-permute-start.9 = (bf16[1024,256]{1,0:T(8,128)(2,1)S(1)}, bf16[1024,256]{1,0:T(8,128)(2,1)S(1)}, u32[]{:S(2)}, u32[]{:S(2)}) collective-permute-start(bf16[1024,256]{1,0:T(8,128)(2,1)S(1)} %forward_far_a.1), channel_id=1, source_target_pairs={{0,2},{2,0},{1,3},{3,1},{4,6},{6,4},{5,7},{7,5},{8,10},{10,8},{9,1... | collective-permute-start | bytes 1572872 | tf_op jit(solution)/shard_map/ppermute | solution.py:26
  25.2 16.4 %collective-permute-start.12 = (bf16[1024,256]{1,0:T(8,128)(2,1)S(1)}, bf16[1024,256]{1,0:T(8,128)(2,1)S(1)}, u32[]{:S(2)}, u32[]{:S(2)}) collective-permute-start(bf16[1024,256]{1,0:T(8,128)(2,1)S(1)} %forward_far_b.1), channel_id=1, source_target_pairs={{0,8},{8,0},{4,12},{12,4},{1,9},{9,1},{5,13},{13,5},{2,10},{10,2},... | collective-permute-start | bytes 1572872 | tf_op jit(solution)/shard_map/ppermute | solution.py:28
  30.9 21.6 %collective-permute-start.10 = (bf16[1024,256]{1,0:T(8,128)(2,1)S(1)}, bf16[1024,256]{1,0:T(8,128)(2,1)S(1)}, u32[]{:S(2)}, u32[]{:S(2)}) collective-permute-start(bf16[1024,256]{1,0:T(8,128)(2,1)S(1)} %get-tuple-element.49), channel_id=1, source_target_pairs={{0,4},{4,0},{8,12},{12,8},{1,5},{5,1},{9,13},{13,9},{2,6},{6,2},{1... | collective-permute-start | bytes 1572872 | tf_op jit(solution)/shard_map/ppermute | solution.py:28
  32.3 20.1 %collective-permute-start.11 = (bf16[1024,256]{1,0:T(8,128)(2,1)S(1)}, bf16[1024,256]{1,0:T(8,128)(2,1)S(1)}, u32[]{:S(2)}, u32[]{:S(2)}) collective-permute-start(bf16[1024,256]{1,0:T(8,128)(2,1)S(1)} %get-tuple-element.50), channel_id=1, source_target_pairs={{4,8},{8,4},{12,0},{0,12},{5,9},{9,5},{13,1},{1,13},{6,10},{10,6},... | collective-permute-start | bytes 1572872 | tf_op jit(solution)/shard_map/ppermute | solution.py:28
  35.3 17.2 %collective-permute-start.7 = (bf16[1024,256]{1,0:T(8,128)(2,1)S(1)}, bf16[1024,256]{1,0:T(8,128)(2,1)S(1)}, u32[]{:S(2)}, u32[]{:S(2)}) collective-permute-start(bf16[1024,256]{1,0:T(8,128)(2,1)S(1)} %get-tuple-element.46), channel_id=1, source_target_pairs={{0,1},{1,0},{2,3},{3,2},{4,5},{5,4},{6,7},{7,6},{8,9},{9,8},{10,11... | collective-permute-start | bytes 1572872 | tf_op jit(solution)/shard_map/ppermute | solution.py:26
  37.3 15.2 %collective-permute-start.8 = (bf16[1024,256]{1,0:T(8,128)(2,1)S(1)}, bf16[1024,256]{1,0:T(8,128)(2,1)S(1)}, u32[]{:S(2)}, u32[]{:S(2)}) collective-permute-start(bf16[1024,256]{1,0:T(8,128)(2,1)S(1)} %get-tuple-element.47), channel_id=1, source_target_pairs={{1,2},{2,1},{3,0},{0,3},{5,6},{6,5},{7,4},{4,7},{9,10},{10,9},{11,... | collective-permute-start | bytes 1572872 | tf_op jit(solution)/shard_map/ppermute | solution.py:26
  53.0 6.5 %collective-permute-start.13 = (bf16[256,256]{1,0:T(8,128)(2,1)S(1)}, bf16[256,256]{1,0:T(8,128)(2,1)S(1)}, u32[]{:S(2)}, u32[]{:S(2)}) collective-permute-start(bf16[256,256]{1,0:T(8,128)(2,1)S(1)} %get-tuple-element.52), channel_id=1, source_target_pairs={{0,4},{4,0},{8,12},{12,8},{1,5},{5,1},{9,13},{13,9},{2,6},{6,2},{1... | collective-permute-start | bytes 393224 | tf_op jit(solution)/shard_map/ppermute | solution.py:28
  53.7 7.8 %collective-permute-start.14 = (bf16[256,256]{1,0:T(8,128)(2,1)S(1)}, bf16[256,256]{1,0:T(8,128)(2,1)S(1)}, u32[]{:S(2)}, u32[]{:S(2)}) collective-permute-start(bf16[256,256]{1,0:T(8,128)(2,1)S(1)} %get-tuple-element.53), channel_id=1, source_target_pairs={{4,8},{8,4},{12,0},{0,12},{5,9},{9,5},{13,1},{1,13},{6,10},{10,6},... | collective-permute-start | bytes 393224 | tf_op jit(solution)/shard_map/ppermute | solution.py:28
  55.8 7.6 %collective-permute-start.15 = (bf16[256,256]{1,0:T(8,128)(2,1)S(1)}, bf16[256,256]{1,0:T(8,128)(2,1)S(1)}, u32[]{:S(2)}, u32[]{:S(2)}) collective-permute-start(bf16[256,256]{1,0:T(8,128)(2,1)S(1)} %get-tuple-element.54), channel_id=1, source_target_pairs={{0,8},{8,0},{4,12},{12,4},{1,9},{9,1},{5,13},{13,5},{2,10},{10,2},... | collective-permute-start | bytes 393224 | tf_op jit(solution)/shard_map/ppermute | solution.py:28
  58.2 6.7 %collective-permute-start.17 = (bf16[256,256]{1,0:T(8,128)(2,1)S(1)}, bf16[256,256]{1,0:T(8,128)(2,1)S(1)}, u32[]{:S(2)}, u32[]{:S(2)}) collective-permute-start(bf16[256,256]{1,0:T(8,128)(2,1)S(1)} %get-tuple-element.57), channel_id=1, source_target_pairs={{1,2},{2,1},{3,0},{0,3},{5,6},{6,5},{7,4},{4,7},{9,10},{10,9},{11,... | collective-permute-start | bytes 393224 | tf_op jit(solution)/shard_map/ppermute | solution.py:26
  59.5 6.5 %collective-permute-start.18 = (bf16[256,256]{1,0:T(8,128)(2,1)S(1)}, bf16[256,256]{1,0:T(8,128)(2,1)S(1)}, u32[]{:S(2)}, u32[]{:S(2)}) collective-permute-start(bf16[256,256]{1,0:T(8,128)(2,1)S(1)} %get-tuple-element.58), channel_id=1, source_target_pairs={{0,2},{2,0},{1,3},{3,1},{4,6},{6,4},{5,7},{7,5},{8,10},{10,8},{9,1... | collective-permute-start | bytes 393224 | tf_op jit(solution)/shard_map/ppermute | solution.py:26
  67.2 8.6 %collective-permute-start.26 = (bf16[384,256]{1,0:T(8,128)(2,1)S(1)}, bf16[384,256]{1,0:T(8,128)(2,1)S(1)}, u32[]{:S(2)}, u32[]{:S(2)}) collective-permute-start(bf16[384,256]{1,0:T(8,128)(2,1)S(1)} %get-tuple-element.61.own), channel_id=1, source_target_pairs={{0,2},{2,0},{1,3},{3,1},{4,6},{6,4},{5,7},{7,5},{8,10},{10,8},{9,1... | collective-permute-start | bytes 589832 | tf_op jit(solution)/shard_map/ppermute | solution.py:26
  69.2 8.0 %collective-permute-start.25 = (bf16[384,256]{1,0:T(8,128)(2,1)S(1)}, bf16[384,256]{1,0:T(8,128)(2,1)S(1)}, u32[]{:S(2)}, u32[]{:S(2)}) collective-permute-start(bf16[384,256]{1,0:T(8,128)(2,1)S(1)} %get-tuple-element.61.own), channel_id=1, source_target_pairs={{1,2},{2,1},{3,0},{0,3},{5,6},{6,5},{7,4},{4,7},{9,10},{10,9},{11,... | collective-permute-start | bytes 589832 | tf_op jit(solution)/shard_map/ppermute | solution.py:26
  70.5 7.6 %collective-permute-start.24 = (bf16[384,256]{1,0:T(8,128)(2,1)S(1)}, bf16[384,256]{1,0:T(8,128)(2,1)S(1)}, u32[]{:S(2)}, u32[]{:S(2)}) collective-permute-start(bf16[384,256]{1,0:T(8,128)(2,1)S(1)} %get-tuple-element.61.own), channel_id=1, source_target_pairs={{0,1},{1,0},{2,3},{3,2},{4,5},{5,4},{6,7},{7,6},{8,9},{9,8},{10,11... | collective-permute-start | bytes 589832 | tf_op jit(solution)/shard_map/ppermute | solution.py:26
  71.9 8.2 %collective-permute-start.21 = (bf16[384,256]{1,0:T(8,128)(2,1)S(1)}, bf16[384,256]{1,0:T(8,128)(2,1)S(1)}, u32[]{:S(2)}, u32[]{:S(2)}) collective-permute-start(bf16[384,256]{1,0:T(8,128)(2,1)S(1)} %get-tuple-element.60.own), channel_id=1, source_target_pairs={{0,8},{8,0},{4,12},{12,4},{1,9},{9,1},{5,13},{13,5},{2,10},{10,2},... | collective-permute-start | bytes 589832 | tf_op jit(solution)/shard_map/ppermute | solution.py:28
  74.1 9.7 %collective-permute-start.20 = (bf16[384,256]{1,0:T(8,128)(2,1)S(1)}, bf16[384,256]{1,0:T(8,128)(2,1)S(1)}, u32[]{:S(2)}, u32[]{:S(2)}) collective-permute-start(bf16[384,256]{1,0:T(8,128)(2,1)S(1)} %get-tuple-element.60.own), channel_id=1, source_target_pairs={{4,8},{8,4},{12,0},{0,12},{5,9},{9,5},{13,1},{1,13},{6,10},{10,6},... | collective-permute-start | bytes 589832 | tf_op jit(solution)/shard_map/ppermute | solution.py:28
  75.8 8.0 %collective-permute-start.19 = (bf16[384,256]{1,0:T(8,128)(2,1)S(1)}, bf16[384,256]{1,0:T(8,128)(2,1)S(1)}, u32[]{:S(2)}, u32[]{:S(2)}) collective-permute-start(bf16[384,256]{1,0:T(8,128)(2,1)S(1)} %get-tuple-element.60.own), channel_id=1, source_target_pairs={{0,4},{4,0},{8,12},{12,8},{1,5},{5,1},{9,13},{13,9},{2,6},{6,2},{1... | collective-permute-start | bytes 589832 | tf_op jit(solution)/shard_map/ppermute | solution.py:28
  78.2 16.3 %collective-permute-start.30 = (bf16[1152,256]{1,0:T(8,128)(2,1)S(1)}, bf16[1152,256]{1,0:T(8,128)(2,1)S(1)}, u32[]{:S(2)}, u32[]{:S(2)}) collective-permute-start(bf16[1152,256]{1,0:T(8,128)(2,1)S(1)} %gathered_b.1.refs_1_.refs_6_.refs_7_.refs_5_), channel_id=1, source_target_pairs={{4,8},{8,4},{12,0},{0,12},{5,9},{9,5},{13,1},{1,13},{6,10},{10,6},... | collective-permute-start | bytes 1769480 | tf_op jit(solution)/shard_map/ppermute | solution.py:28
  80.1 14.4 %collective-permute-start.29 = (bf16[1152,256]{1,0:T(8,128)(2,1)S(1)}, bf16[1152,256]{1,0:T(8,128)(2,1)S(1)}, u32[]{:S(2)}, u32[]{:S(2)}) collective-permute-start(bf16[1152,256]{1,0:T(8,128)(2,1)S(1)} %gathered_b.1.refs_1_.refs_6_.refs_7_.refs_5_), channel_id=1, source_target_pairs={{0,4},{4,0},{8,12},{12,8},{1,5},{5,1},{9,13},{13,9},{2,6},{6,2},{1... | collective-permute-start | bytes 1769480 | tf_op jit(solution)/shard_map/ppermute | solution.py:28
  83.9 12.7 %collective-permute-start.23 = (bf16[1152,256]{1,0:T(8,128)(2,1)S(1)}, bf16[1152,256]{1,0:T(8,128)(2,1)S(1)}, u32[]{:S(2)}, u32[]{:S(2)}) collective-permute-start(bf16[1152,256]{1,0:T(8,128)(2,1)S(1)} %gathered_a.1.refs_0_.refs_1_), channel_id=1, source_target_pairs={{1,2},{2,1},{3,0},{0,3},{5,6},{6,5},{7,4},{4,7},{9,10},{10,9},{11,... | collective-permute-start | bytes 1769480 | tf_op jit(solution)/shard_map/ppermute | solution.py:26
  84.7 11.9 %collective-permute-start.22 = (bf16[1152,256]{1,0:T(8,128)(2,1)S(1)}, bf16[1152,256]{1,0:T(8,128)(2,1)S(1)}, u32[]{:S(2)}, u32[]{:S(2)}) collective-permute-start(bf16[1152,256]{1,0:T(8,128)(2,1)S(1)} %gathered_a.1.refs_0_.refs_1_), channel_id=1, source_target_pairs={{0,1},{1,0},{2,3},{3,2},{4,5},{5,4},{6,7},{7,6},{8,9},{9,8},{10,11... | collective-permute-start | bytes 1769480 | tf_op jit(solution)/shard_map/ppermute | solution.py:26
  94.5 11.4 %collective-permute-start.31 = (bf16[576,256]{1,0:T(8,128)(2,1)S(1)}, bf16[576,256]{1,0:T(8,128)(2,1)S(1)}, u32[]{:S(2)}, u32[]{:S(2)}) collective-permute-start(bf16[576,256]{1,0:T(8,128)(2,1)S(1)} %get-tuple-element.65), channel_id=1, source_target_pairs={{4,8},{8,4},{12,0},{0,12},{5,9},{9,5},{13,1},{1,13},{6,10},{10,6},... | collective-permute-start | bytes 884744 | tf_op jit(solution)/shard_map/ppermute | solution.py:28
  96.6 9.3 %collective-permute-start.32 = (bf16[576,256]{1,0:T(8,128)(2,1)S(1)}, bf16[576,256]{1,0:T(8,128)(2,1)S(1)}, u32[]{:S(2)}, u32[]{:S(2)}) collective-permute-start(bf16[576,256]{1,0:T(8,128)(2,1)S(1)} %get-tuple-element.66), channel_id=1, source_target_pairs={{0,4},{4,0},{8,12},{12,8},{1,5},{5,1},{9,13},{13,9},{2,6},{6,2},{1... | collective-permute-start | bytes 884744 | tf_op jit(solution)/shard_map/ppermute | solution.py:28
  96.7 9.2 %collective-permute-start.27 = (bf16[576,256]{1,0:T(8,128)(2,1)S(1)}, bf16[576,256]{1,0:T(8,128)(2,1)S(1)}, u32[]{:S(2)}, u32[]{:S(2)}) collective-permute-start(bf16[576,256]{1,0:T(8,128)(2,1)S(1)} %get-tuple-element.63), channel_id=1, source_target_pairs={{1,2},{2,1},{3,0},{0,3},{5,6},{6,5},{7,4},{4,7},{9,10},{10,9},{11,... | collective-permute-start | bytes 884744 | tf_op jit(solution)/shard_map/ppermute | solution.py:26
  98.3 7.6 %collective-permute-start.28 = (bf16[576,256]{1,0:T(8,128)(2,1)S(1)}, bf16[576,256]{1,0:T(8,128)(2,1)S(1)}, u32[]{:S(2)}, u32[]{:S(2)}) collective-permute-start(bf16[576,256]{1,0:T(8,128)(2,1)S(1)} %get-tuple-element.64), channel_id=1, source_target_pairs={{0,1},{1,0},{2,3},{3,2},{4,5},{5,4},{6,7},{7,6},{8,9},{9,8},{10,11... | collective-permute-start | bytes 884744 | tf_op jit(solution)/shard_map/ppermute | solution.py:26
  111.4 14.7 %collective-permute-start.36 = (bf16[768,256]{1,0:T(8,128)(2,1)S(1)}, bf16[768,256]{1,0:T(8,128)(2,1)S(1)}, u32[]{:S(2)}, u32[]{:S(2)}) collective-permute-start(bf16[768,256]{1,0:T(8,128)(2,1)S(1)} %get-tuple-element.72), channel_id=1, source_target_pairs={{32,64},{64,32},{96,0},{0,96},{48,80},{80,48},{112,16},{16,112},{3... | collective-permute-start | bytes 1179656 | tf_op jit(solution)/shard_map/ppermute | solution.py:29
  116.6 11.0 %collective-permute-start.35 = (bf16[768,256]{1,0:T(8,128)(2,1)S(1)}, bf16[768,256]{1,0:T(8,128)(2,1)S(1)}, u32[]{:S(2)}, u32[]{:S(2)}) collective-permute-start(bf16[768,256]{1,0:T(8,128)(2,1)S(1)} %get-tuple-element.71.own_message), channel_id=1, source_target_pairs={{0,32},{32,0},{64,96},{96,64},{16,48},{48,16},{80,112},{112,80},{1... | collective-permute-start | bytes 1179656 | tf_op jit(solution)/shard_map/ppermute | solution.py:29
  127.6 7.2 %collective-permute-start.37 = (bf16[384,256]{1,0:T(8,128)(2,1)S(1)}, bf16[384,256]{1,0:T(8,128)(2,1)S(1)}, u32[]{:S(2)}, u32[]{:S(2)}) collective-permute-start(bf16[384,256]{1,0:T(8,128)(2,1)S(1)} %get-tuple-element.75), channel_id=1, source_target_pairs={{32,64},{64,32},{96,0},{0,96},{48,80},{80,48},{112,16},{16,112},{3... | collective-permute-start | bytes 589832 | tf_op jit(solution)/shard_map/ppermute | solution.py:29
  (12 other events, 64.5 us)

commit v3 on v2

--- a/solution.py
+++ b/solution.py
@@ -13,8 +13,6 @@
 UNIT = 2
 UNROLL = 8
 GROUP = UNIT * UNROLL
-KEYS = 64
-DUMMY = 32
 
 ONE = ((0, 1), (1, 0), (2, 3), (3, 2))
 TWO = ((1, 2), (2, 1), (3, 0), (0, 3))
@@ -44,16 +42,13 @@
     return found
 
 
-ROLE = (6, 1, 0, 4, 7, 5, 2, 3)
-
-
-FORWARD = ((0, 8), (8, 16), (16, 32), (32, 48), (48, 64))
-BACKWARD = ((0, 32), (32, 48), (48, 64))
+FORWARD = ((0, 16), (16, 32), (32, 48), (48, 64))
+BACKWARD = ((0, 32), (32, 64), (64, 80), (80, 96))
 ROOM = 640
 
 
 def sort_tiles(out, keys, source, live, segments):
-    total = keys.shape[1]
+    total, n_keys = keys.shape[1], segments[-1][1]
 
     def iota(rows, lanes, axis):
         return lax.broadcasted_iota(jnp.int32, (rows, lanes), axis).astype(F32)
@@ -69,23 +64,23 @@
         local = jnp.where(keys >= first, keys - first, local)
     slots = lax.broadcasted_iota(jnp.int32, (1, total), 1)
     payload = (slots + 512 * (source + 1) + 65536 * (local + 1)).astype(F32)
-    keys = jnp.where(live, keys, KEYS).astype(F32)
+    keys = jnp.where(live, keys, n_keys).astype(F32)
     key_column = column(keys)
     lane = iota(1, 128, 1)
     count = jnp.sum(jnp.where(key_column == lane, 1.0, 0.0), 0, keepdims=True)
-    padded = jnp.where(lane < KEYS, ((count.astype(jnp.int32) + 1) >> 1 << 1).astype(F32), 0.0)
+    padded = jnp.where(lane < n_keys, ((count.astype(jnp.int32) + 1) >> 1 << 1).astype(F32), 0.0)
     bounds = [jnp.zeros((1, 1), F32)]
     for index in range(len(segments)):
         size = jnp.sum(jnp.where(segment_of(lane) == index, padded, 0.0), 1, keepdims=True).astype(jnp.int32)
         bounds.append(bounds[-1] + ((size + GROUP - 1) // GROUP).astype(F32))
-    key, before = iota(KEYS, 128, 0), iota(KEYS, 128, 1)
+    key, before = iota(n_keys, 128, 0), iota(n_keys, 128, 1)
     counted = (before < key) & (segment_of(before) == segment_of(key))
     offset = jnp.sum(jnp.where(counted, padded, 0.0), 1, keepdims=True)
     for index in range(len(segments)):
         offset += jnp.where(segment_of(key[:, :1]) == index, GROUP * bounds[index], 0.0)
     same = jnp.concatenate([key_column] * (total // 128), 1) == keys
     rank = jnp.sum(jnp.where(same & (iota(total, total, 0) < iota(total, total, 1)), 1.0, 0.0), 0, keepdims=True)
-    start = jnp.sum(jnp.where(iota(KEYS, total, 0) == keys, offset, 0.0), 0, keepdims=True)
+    start = jnp.sum(jnp.where(iota(n_keys, total, 0) == keys, offset, 0.0), 0, keepdims=True)
     place_column = column(jnp.where(live, rank + start, -1.0))
     payload_column = column(payload)
     for block in range(ROOM // 128):
@@ -94,7 +89,7 @@
         found = found.astype(jnp.int32)
         out[0:1, here] = found & 511
         out[1:2, here] = (found >> 9) & 127
-        out[2:3, here] = jnp.where(found == 0, DUMMY, (found >> 16) - 1)
+        out[2:3, here] = jnp.where(found == 0, 0, (found >> 16) - 1)
         out[3:4, here] = sum(jnp.where(lane >= index, bounds[index] - bounds[index - 1], 0.0) for index in range(1, len(bounds))).astype(jnp.int32)
 
 
@@ -113,12 +108,11 @@
         source = other * 16 + slot * 4 + (cols & 3)
         sort_tiles(forward, base + ring_two * 2 + half, source, live, FORWARD)
         far = ring_one == 2
-        near_slot = ring_one ^ (ring_one >> 1)
+        near = ring_one % 2 == 1
         inner = ring_two ^ (ring_two >> 1)
-        source = jnp.where(second, jnp.where(far, 8, 24 + near_slot * 8), jnp.where(far, 0, near_slot * 8))
+        source = jnp.where(near, jnp.where(second, 16, 0) + (ring_one >> 1) * 8, jnp.where(second, 8, 0))
         source += half * 4 + inner
-        role = pick(((cols >> 1) & 1) * 4 + x_away, ROLE)
-        keys = jnp.where(far, 32, 0) + (1 - other) * 16 + role * 2 + (cols & 1)
+        keys = jnp.where(far, 64, jnp.where(near, 32, 0)) + (1 - other) * 16 + x_away * 4 + (cols & 3)
         sort_tiles(backward, keys, source, live, BACKWARD)
 
     smem = pl.BlockSpec(memory_space=pltpu.SMEM)
@@ -223,11 +217,12 @@
         place += rows
 
 
-def aggregate(name, step, lists, pieces, tiles, outs, flipped, start=None):
+def aggregate(name, step, lists, pieces, tiles, outs, flipped, start=None, after=()):
     whole = len(pieces) == 1
     n_pieces = len(pieces)
     total = pieces[0][2] if whole else BLK + sum(rows for _, _, rows in pieces)
     blocks = max(first + size for first, size, _ in outs)
+    direct = len(outs) == 1 and outs[0][2] == F32
 
     def kernel(listed, *refs):
         source = refs[:n_pieces]
@@ -235,18 +230,22 @@
         refs = refs[n_pieces + 1 :]
         if start is not None:
             start_ref, refs = refs[0], refs[1:]
+        refs = refs[len(after) :]
         out_refs, refs = refs[: len(outs)], refs[len(outs) :]
-        acc = refs[0]
+        acc = out_refs[0] if direct else refs[0]
         if whole:
             slab = source[0]
         else:
-            slab = refs[1]
+            slab = refs[-1]
             fill_slab(slab, [(ref, row, rows) for ref, (_, row, rows) in zip(source, pieces)])
 
         @pl.loop(0, blocks)
         def _(block):
             rows = pl.ds(pl.multiple_of(block * BLK, BLK), BLK)
-            acc[rows] = jnp.zeros((BLK, acc.shape[1]), F32) if start is None else start_ref[rows]
+            if start is None:
+                acc[rows] = jnp.zeros((BLK, acc.shape[1]), F32)
+            else:
+                acc[rows] = start_ref[pl.ds(pl.multiple_of((block + start[1]) * BLK, BLK), BLK)]
 
         @pl.loop(listed[3, step], listed[3, step + 1])
         def _(group):
@@ -264,7 +263,7 @@
                     value = jnp.dot(jnp.concatenate(matrix, 1), jnp.concatenate(read, 0), preferred_element_type=F32)
                 acc[to] += value
 
-        for out, (block, size, _) in zip(out_refs, outs):
+        for out, (block, size, _) in zip(() if direct else out_refs, outs):
 
             @pl.loop(0, size)
             def _(k, out=out, block=block):
@@ -274,20 +273,20 @@
     smem = pl.BlockSpec(memory_space=pltpu.SMEM)
     vmem = pl.BlockSpec(memory_space=pltpu.VMEM)
     width = pieces[0][0].shape[1]
-    extra = [] if start is None else [start]
-    scratch = [pltpu.VMEM(((DUMMY + 1) * BLK, width), F32)]
+    extra = [] if start is None else [start[0]]
+    scratch = [] if direct else [pltpu.VMEM((blocks * BLK, width), F32)]
     if not whole:
         scratch.append(pltpu.VMEM((total, width), BF))
     return pl.pallas_call(
         kernel,
-        in_specs=[smem] + [vmem] * (n_pieces + 1 + len(extra)),
+        in_specs=[smem] + [vmem] * (n_pieces + 1 + len(extra)) + [pl.BlockSpec(memory_space=pl.ANY)] * len(after),
         out_specs=[vmem] * len(outs),
         out_shape=[jax.ShapeDtypeStruct((size * BLK, width), dtype) for _, size, dtype in outs],
         scratch_shapes=scratch,
         compiler_params=pltpu.CompilerParams(vmem_limit_bytes=24 << 20),
         cost_estimate=pl.CostEstimate(flops=10**6, bytes_accessed=1 << 17, transcendentals=0),
         name=name,
-    )(lists, *[array for array, _, _ in pieces], pltpu.with_memory_space_constraint(tiles, pltpu.VMEM), *extra)
+    )(lists, *[array for array, _, _ in pieces], pltpu.with_memory_space_constraint(tiles, pltpu.VMEM), *extra, *after)
 
 
 def local(name, body, out_shape, *operands):
@@ -306,13 +305,13 @@
     return jax.ShapeDtypeStruct((rows, width), dtype)
 
 
-def second_phase(*refs):
-    ins, outs = refs[:8], refs[8:]
-    for k in range(2):
-        kept, one, three, two = ins[4 * k : 4 * k + 4]
-        total = (kept[...] + two[...].astype(F32)) + (one[...].astype(F32) + three[...].astype(F32))
-        for away, out in enumerate(outs[4 * k : 4 * k + 4]):
+def second_phase(half):
+    def kernel(two, one, three, kept, *outs):
+        total = kept[pl.ds(1024 * half, 1024)] + two[...].astype(F32) + (one[...].astype(F32) + three[...].astype(F32))
+        for away, out in enumerate(outs):
             out[...] = total[256 * away : 256 * away + 256].astype(out.dtype)
+
+    return kernel
 
 
 SCALE = math.sqrt(2.0 / math.pi)
@@ -323,7 +322,7 @@
     matrix = weight[...]
     halves = []
     for k in range(2):
-        kept, one, three, two = sums[4 * k : 4 * k + 4]
+        two, one, three, kept = sums[k::2]
         halves.append((kept[...] + two[...].astype(F32)) + (one[...].astype(F32) + three[...].astype(F32)))
     aggregated = jnp.concatenate(halves, 0).astype(BF)
     pre = jnp.dot(aggregated, matrix, preferred_element_type=F32)
@@ -344,7 +343,7 @@
     return (zero.astype(F32) + two.astype(F32)) + (one.astype(F32) + three.astype(F32))
 
 
-def gathered(own, one, three, two, out):
+def gathered(two, three, one, own, out):
     for half in range(2):
         for slot, ref in enumerate((own, one, three, two)):
             out[pl.ds(half * 576 + slot * BLK, BLK)] = ref[pl.ds(192 * half, BLK)]
@@ -362,33 +361,20 @@
             out[pl.ds((2 * k + half) * 64, 64)] = total
 
 
-def last_phase(own, received, grad, grad_received, by_one, by_two, late_two, late_one, kept):
+def last_phase(own, received, grad, grad_received, kept, one, two, three):
     total = own[...] + received[...].astype(F32)
-    by_one[pl.ds(0, 512)] = total[0:512].astype(BF)
-    by_two[pl.ds(0, 512)] = total[512:1024].astype(BF)
-    late_two[...] = total[1024:1280].astype(BF)
-    late_one[...] = total[1280:1536].astype(BF)
-    kept[...] = total[1536:2048]
     both = (grad[...] + grad_received[...]).astype(BF)
-    by_one[pl.ds(512, 256)] = both
-    by_two[pl.ds(512, 256)] = both
-
-
-def last_forward(late_two, by_one, late_one, by_two, out_two, out_one):
-    out_two[pl.ds(0, 256)] = (late_two[...].astype(F32) + by_one[pl.ds(0, 256)].astype(F32)).astype(BF)
-    out_two[pl.ds(256, 128)] = by_one[pl.ds(512, 128)]
-    out_one[pl.ds(0, 256)] = (late_one[...].astype(F32) + by_two[pl.ds(0, 256)].astype(F32)).astype(BF)
-    out_one[pl.ds(256, 128)] = by_two[pl.ds(640, 128)]
-
-
-def last_sum(kept, by_one, by_two, late_two, late_one, own_message, features, weight):
-    first = kept[pl.ds(0, 256)] + (by_one[pl.ds(256, 256)].astype(F32) + late_two[pl.ds(0, 256)].astype(F32))
-    second = kept[pl.ds(256, 256)] + (by_two[pl.ds(256, 256)].astype(F32) + late_one[pl.ds(0, 256)].astype(F32))
-    features[pl.ds(0, 256)] = first.astype(BF)
-    features[pl.ds(256, 256)] = second.astype(BF)
-    for half, late in enumerate((late_two, late_one)):
-        rows = pl.ds(512 + 128 * half, 128)
-        weight[pl.ds(128 * half, 128)] = four(own_message[rows], by_one[rows], late[pl.ds(256, 128)], by_two[rows])
+    kept[...] = total[0:512]
+    for away, out in ((1, one), (2, two), (3, three)):
+        out[pl.ds(0, 512)] = total[512 * away : 512 * away + 512].astype(BF)
+        out[pl.ds(512, 256)] = both
+
+
+def last_sum(two, one, three, kept, own, features, weight):
+    rows, grads = pl.ds(0, 512), pl.ds(512, 256)
+    total = (kept[...] + two[rows].astype(F32)) + (one[rows].astype(F32) + three[rows].astype(F32))
+    features[...] = total.astype(BF)
+    weight[...] = four(own[grads], one[grads], two[grads], three[grads])
 
 
 def per_device(features, weight, cotangent, tile_values, tile_rows, tile_cols, tile_count):
@@ -413,63 +399,61 @@
     def out(*dtypes):
         return [(8 * k, 8, dtype) for k, dtype in enumerate(dtypes)]
 
-    (a_two,) = aggregate("forward_far_a", 0, forward, pieces, held_tiles, out(BF), False)
-    a_two = swap(a_two, "z", FAR)
-    (b_two,) = aggregate("forward_far_b", 1, forward, pieces, held_tiles, out(BF), False)
-    b_two = swap(b_two, "y", FAR)
-    b_one, b_three = aggregate("forward_near_b", 2, forward, pieces, held_tiles, out(BF, BF), False)
+    def forward_part(step, name, outs, *after):
+        return aggregate(name, step, forward, pieces, held_tiles, outs, False, None, after)
+
+    a_two, b_two = far = forward_part(0, "forward_far", out(BF, BF))
+    a_two, b_two = swap(a_two, "z", FAR), swap(b_two, "y", FAR)
+    b_one, b_three = near_b = forward_part(1, "forward_near_b", out(BF, BF), far[0])
     b_one, b_three = swap(b_one, "y", ONE), swap(b_three, "y", TWO)
-    a_one, a_three = aggregate("forward_near_a", 3, forward, pieces, held_tiles, out(BF, BF), False)
+    a_one, a_three = near_a = forward_part(2, "forward_near_a", out(BF, BF), near_b[0])
     a_one, a_three = swap(a_one, "z", ONE), swap(a_three, "z", TWO)
-    a_own, b_own = aggregate("forward_own", 4, forward, pieces, held_tiles, out(F32, F32), False)
-    second_shapes = [shape(256, F32), shape(256), shape(256), shape(256)]
-    a_own, a_one, a_two, a_three, b_own, b_one, b_two, b_three = local(
-        "second_phase", second_phase, second_shapes * 2,
-        a_own, a_one, a_three, a_two, b_own, b_one, b_three, b_two,
-    )
-    a_sums = [a_own, *ways("y", a_one, a_three, a_two)]
-    b_sums = [b_own, *ways("z", b_one, b_three, b_two)]
+    (kept,) = forward_part(3, "forward_own", [(0, 16, F32)], near_a[0], a_two, b_two)
+    shapes = [shape(256, F32), shape(256), shape(256), shape(256)]
+    a_own, a_one, a_two, a_three = local("second_phase_a", second_phase(0), shapes, a_two, a_one, a_three, kept)
+    b_own, b_one, b_two, b_three = local("second_phase_b", second_phase(1), shapes, b_two, b_one, b_three, kept)
+    a_one, a_three, a_two = ways("y", a_one, a_three, a_two)
+    b_one, b_three, b_two = ways("z", b_one, b_three, b_two)
     activated, a_own, b_own = local(
-        "dense", dense, [shape(512), shape(384), shape(384)], *a_sums, *b_sums, cotangent, weight
-    )
-
-    a_held = [a_own, *ways("y", a_own, a_own, a_own)]
-    b_held = [b_own, *ways("z", b_own, b_own, b_own)]
+        "dense", dense, [shape(512), shape(384), shape(384)], a_two, b_two, a_one, b_one, a_three, b_three, a_own, b_own, cotangent, weight
+    )
+
+    def spread(axis, own):
+        two = swap(own, axis, FAR)
+        three = swap(own, axis, TWO)
+        return [two, three, swap(own, axis, ONE), own]
+
+    a_held, b_held = spread("y", a_own), spread("z", b_own)
     (a_own,) = local("gathered_a", gathered, [shape(1152)], *a_held)
     a_one, a_three = swap(a_own, "z", ONE), swap(a_own, "z", TWO)
     (b_own,) = local("gathered_b", gathered, [shape(1152)], *b_held)
     b_one, b_three = swap(b_own, "y", ONE), swap(b_own, "y", TWO)
-    again, loaded = load(tiles, a_own, b_own)
-    a_first, a_second = cut(a_one, a_three, loaded)
-    b_first, b_second = cut(b_one, b_three, loaded)
+    here = [(piece, row, 512) for piece in (a_own, b_own) for row in (0, 576)]
+    (sums,) = aggregate("backward_here", 0, backward, here, held_tiles, [(0, 32, F32)], True)
+    a_first, a_second = cut(a_one, a_three, sums)
+    b_first, b_second = cut(b_one, b_three, sums)
     a_far = swap(a_first, "z", TWO), swap(a_second, "z", ONE)
     b_far = swap(b_first, "y", TWO), swap(b_second, "y", ONE)
 
     near = [
-        (piece, row, 512) for piece in (a_own, a_one, a_three, b_own, b_one, b_three) for row in (0, 576)
+        (piece, row, 512) for piece in (a_one, a_three, b_one, b_three) for row in (0, 576)
     ]
     distant = [(piece, 0, 512) for piece in (*a_far, *b_far)]
-    other_start, own_start = aggregate(
-        "backward_near", 0, backward, near, again, [(0, 16, F32), (16, 16, F32)], True
-    )
-    (other_sum,) = aggregate("backward_other", 1, backward, distant, again, [(0, 16, BF)], True, other_start)
+    (sums,) = aggregate("backward_near", 1, backward, near, held_tiles, [(0, 32, F32)], True, (sums, 0))
+    (other_sum,) = aggregate("backward_other", 2, backward, distant, held_tiles, [(0, 16, BF)], True, (sums, 0))
     received = swap_core(other_sum)
     (grad,) = local(
         "sum_ring", sum_ring, [shape(256, F32)], a_own, a_one, a_three, *a_far, b_own, b_one, b_three, *b_far
     )
     grad_received = swap_core(grad)
-    (own_sum,) = aggregate("backward_own", 2, backward, distant, again, [(0, 16, F32)], True, own_start)
-    by_one, by_two, late_two, late_one, kept = local(
-        "last_phase", last_phase, [shape(768), shape(768), shape(256), shape(256), shape(512, F32)],
+    (own_sum,) = aggregate("backward_own", 3, backward, distant, held_tiles, [(0, 16, F32)], True, (sums, 16))
+    kept, by_one, by_two, by_three = local(
+        "last_phase", last_phase, [shape(512, F32), shape(768), shape(768), shape(768)],
         own_sum, received, grad, grad_received,
     )
-    got_one, got_two = swap(by_one, "x", ONE), swap(by_two, "x", TWO)
-    late_two, late_one = local(
-        "last_forward", last_forward, [shape(384), shape(384)], late_two, got_one, late_one, got_two
-    )
-    late_two, late_one = swap(late_two, "x", TWO), swap(late_one, "x", ONE)
+    one, three, two = ways("x", by_one, by_three, by_two)
     grad_features, grad_weight = local(
-        "last_sum", last_sum, [shape(512), shape(256, F32)], kept, got_one, got_two, late_two, late_one, by_one
+        "last_sum", last_sum, [shape(512), shape(256, F32)], two, one, three, kept, by_one
     )
     return activated, grad_features, grad_weight
 

time: 136 us -> 134 us (0.985); the launches traced: 136 us -> 132 us
  Pallas kernels: 33.5 us -> 30.9 us
  waiting for transfers between devices: 48.7 us -> 46.6 us
    pallas_call x2 -> x1, Pallas kernels: 9.44 us -> 4.74 us  [load(): pl.pallas_call(kernel, in_specs=[pl.BlockSpec(memory_space=pltpu.HBM)] +...]
    ppermute x13, waiting for transfers between devices: 22.1 us -> 19.3 us  [swap(): lax.ppermute(value, 'col', [(a * 4 + z, b * 4 + z) for z in range(4) for...]
    pallas_call x8, Pallas kernels: 19.5 us -> 21.6 us  [aggregate(): pl.pallas_call(kernel, in_specs=[smem] + [vmem] * (n_pieces + 1 + len(ext...]
    ppermute x7 -> x6, starting transfers between devices: 11.5 us -> 9.52 us  [swap(): lax.ppermute(value, 'row', [(a * 2 + k, b * 2 + k) for k in range(2) for...]
    ppermute x13, starting transfers between devices: 17.4 us -> 19 us  [swap(): lax.ppermute(value, 'col', [(a * 4 + z, b * 4 + z) for z in range(4) for...]
    ppermute x7 -> x6, waiting for transfers between devices: 19.7 us -> 20.2 us  [swap(): lax.ppermute(value, 'row', [(a * 2 + k, b * 2 + k) for k in range(2) for...]
  transfers between devices with their start and end apart: 39 -> 38, of which waited for: 18 -> 24; matrix products, arithmetic and copies ran while one was open for 0% -> 0% of each run, Pallas kernels for 20% -> 18%
where the time goes in v3:
time: 134 us; the launch traced here: 132 us
  starting transfers between devices  52.1 us (39%)
  waiting for transfers between devices  46.6 us (35%)
  Pallas kernels  30.9 us (23%)
  between operations  1.52 us (1%)
  local copies, waits for them, and re-layouts  1.38 us (1%)
    ppermute x13, starting transfers between devices, swap(): lax.ppermute(value, 'col', [(y * 4 + a, y * 4 + b) for y in range(4) for...  21.8 us
    pallas_call x8, Pallas kernels, aggregate(): pl.pallas_call(kernel, in_specs=[smem] + [vmem] * (n_pieces + 1 + len(ext...  21.6 us
    ppermute x6, waiting for transfers between devices, swap(): lax.ppermute(value, 'row', [(a * 2 + k, b * 2 + k) for k in range(2) for...  20.2 us
    ppermute x13, waiting for transfers between devices, swap(): lax.ppermute(value, 'col', [(a * 4 + z, b * 4 + z) for z in range(4) for...  19.3 us
    ppermute x13, starting transfers between devices, swap(): lax.ppermute(value, 'col', [(a * 4 + z, b * 4 + z) for z in range(4) for...  19 us
    ppermute x6, starting transfers between devices, swap(): lax.ppermute(value, 'row', [(a * 2 + k, b * 2 + k) for k in range(2) for...  9.52 us
    ppermute x13, waiting for transfers between devices, swap(): lax.ppermute(value, 'col', [(y * 4 + a, y * 4 + b) for y in range(4) for...  4.96 us
    pallas_call x1, Pallas kernels, load(): pl.pallas_call(kernel, in_specs=[pl.BlockSpec(memory_space=pltpu.HBM)] +...  4.74 us
  transfers between devices with their start and end apart: 38, of which 24 were waited for; matrix products, arithmetic and copies ran while one was open for 0% of the time, Pallas kernels for 18%

profile of v3, /device:TPU:32, one launch (start us, length us, event | category | flops | bytes accessed | tf_op | source)
XLA Modules:
  0.0 132.5 jit_solution(13681906719029636207)
XLA Ops:
  0.6 3.1 %collective-permute-start.2 = (bf16[512,256]{1,0:T(8,128)(2,1)}, bf16[512,256]{1,0:T(8,128)(2,1)S(1)}, u32[]{:S(2)}, u32[]{:S(2)}) collective-permute-start(bf16[512,256]{1,0:T(8,128)(2,1)} %refs_0_.1), channel_id=1, source_target_pairs={{0,64},{64,0},{32,96},{96,32},{16,80},{80,16},{48,112},{112,48},{1... | collective-permute-start | bytes 786440 | tf_op jit(solution)/shard_map/ppermute | solution.py:27
  8.2 4.7 %load_tiles.1 = (bf16[384,128,128]{2,1,0:T(8,128)(2,1)S(1)}, s32[8,128]{1,0:T(8,128)S(1)}) custom-call(bf16[384,128,128]{2,1,0:T(8,128)(2,1)} %bitcast.9, s32[4,640]{1,0:T(4,128)S(1)} %get-tuple-element.34.refs_0_.listed, s32[4,640]{1,0:T(4,128)S(1)} %get-tuple-element.35.refs_1_.listed), custom_call_target="tpu_custom_call" | custom-call | bytes 26214400 | tf_op jit(solution)/shard_map/load_tiles/pallas_call | solution.py:146
  13.6 2.6 %collective-permute-done.refs_1_ = bf16[512,256]{1,0:T(8,128)(2,1)S(1)} collective-permute-done((bf16[512,256]{1,0:T(8,128)(2,1)}, bf16[512,256]{1,0:T(8,128)(2,1)S(1)}, u32[]{:S(2)}, u32[]{:S(2)}) %collective-permute-start) | collective-permute-done | bytes 262176 | tf_op jit(solution)/shard_map/ppermute | solution.py:27
  18.3 2.7 %forward_far.1 = (bf16[1024,256]{1,0:T(8,128)(2,1)S(1)}, bf16[1024,256]{1,0:T(8,128)(2,1)S(1)}) custom-call(s32[4,640]{1,0:T(4,128)S(1)} %get-tuple-element.34.refs_0_.listed, bf16[4224,256]{1,0:T(8,128)(2,1)S(1)} %assemble.1.refs_0_, bf16[384,128,128]{2,1,0:T(8,128)(2,1)S(1)} %get-tuple-element.37.refs_1_.refs_4_.refs_8_), custom_call_target="tpu_custom_call" | custom-call | flops 1000000 | bytes 131072 | tf_op jit(solution)/shard_map/forward_far/pallas_call | solution.py:280
  21.0 3.3 %collective-permute-start.10 = (bf16[1024,256]{1,0:T(8,128)(2,1)S(1)}, bf16[1024,256]{1,0:T(8,128)(2,1)S(1)}, u32[]{:S(2)}, u32[]{:S(2)}) collective-permute-start(bf16[1024,256]{1,0:T(8,128)(2,1)S(1)} %get-tuple-element.42), channel_id=1, source_target_pairs={{0,8},{8,0},{4,12},{12,4},{1,9},{9,1},{5,13},{13,5},{2,10},{10,2},... | collective-permute-start | bytes 1572872 | tf_op jit(solution)/shard_map/ppermute | solution.py:26
  24.3 3.6 %collective-permute-start.7 = (bf16[1024,256]{1,0:T(8,128)(2,1)S(1)}, bf16[1024,256]{1,0:T(8,128)(2,1)S(1)}, u32[]{:S(2)}, u32[]{:S(2)}) collective-permute-start(bf16[1024,256]{1,0:T(8,128)(2,1)S(1)} %get-tuple-element.38.refs_2_), channel_id=1, source_target_pairs={{0,2},{2,0},{1,3},{3,1},{4,6},{6,4},{5,7},{7,5},{8,10},{10,8},{9,1... | collective-permute-start | bytes 1572872 | tf_op jit(solution)/shard_map/ppermute | solution.py:24
  27.9 2.4 %forward_near_b.1 = (bf16[1024,256]{1,0:T(8,128)(2,1)S(1)}, bf16[1024,256]{1,0:T(8,128)(2,1)S(1)}) custom-call(s32[4,640]{1,0:T(4,128)S(1)} %get-tuple-element.34.refs_0_.listed, bf16[4224,256]{1,0:T(8,128)(2,1)S(1)} %assemble.1.refs_0_, bf16[384,128,128]{2,1,0:T(8,128)(2,1)S(1)} %get-tuple-element.37.refs_1_.refs_4_.refs_8_, ...), custom_call_target="tpu_custom_call" | custom-call | flops 1000000 | bytes 131072 | tf_op jit(solution)/shard_map/forward_near_b/pallas_call | solution.py:280
  30.3 1.8 %collective-permute-start.12 = (bf16[1024,256]{1,0:T(8,128)(2,1)S(1)}, bf16[1024,256]{1,0:T(8,128)(2,1)S(1)}, u32[]{:S(2)}, u32[]{:S(2)}) collective-permute-start(bf16[1024,256]{1,0:T(8,128)(2,1)S(1)} %get-tuple-element.39.refs_2_), channel_id=1, source_target_pairs={{0,4},{4,0},{8,12},{12,8},{1,5},{5,1},{9,13},{13,9},{2,6},{6,2},{1... | collective-permute-start | bytes 1572872 | tf_op jit(solution)/shard_map/ppermute | solution.py:26
  32.1 2.7 %forward_near_a.1 = (bf16[1024,256]{1,0:T(8,128)(2,1)S(1)}, bf16[1024,256]{1,0:T(8,128)(2,1)S(1)}) custom-call(s32[4,640]{1,0:T(4,128)S(1)} %get-tuple-element.34.refs_0_.listed, bf16[4224,256]{1,0:T(8,128)(2,1)S(1)} %assemble.1.refs_0_, bf16[384,128,128]{2,1,0:T(8,128)(2,1)S(1)} %get-tuple-element.37.refs_1_.refs_4_.refs_8_, ...), custom_call_target="tpu_custom_call" | custom-call | flops 1000000 | bytes 131072 | tf_op jit(solution)/shard_map/forward_near_a/pallas_call | solution.py:280
  34.9 2.5 %collective-permute-done.10.refs_4_.two = bf16[1024,256]{1,0:T(8,128)(2,1)S(1)} collective-permute-done((bf16[1024,256]{1,0:T(8,128)(2,1)S(1)}, bf16[1024,256]{1,0:T(8,128)(2,1)S(1)}, u32[]{:S(2)}, u32[]{:S(2)}) %collective-permute-start.10) | collective-permute-done | bytes 524320 | tf_op jit(solution)/shard_map/ppermute | solution.py:26
  37.4 1.8 %collective-permute-start.9 = (bf16[1024,256]{1,0:T(8,128)(2,1)S(1)}, bf16[1024,256]{1,0:T(8,128)(2,1)S(1)}, u32[]{:S(2)}, u32[]{:S(2)}) collective-permute-start(bf16[1024,256]{1,0:T(8,128)(2,1)S(1)} %get-tuple-element.41), channel_id=1, source_target_pairs={{1,2},{2,1},{3,0},{0,3},{5,6},{6,5},{7,4},{4,7},{9,10},{10,9},{11,... | collective-permute-start | bytes 1572872 | tf_op jit(solution)/shard_map/ppermute | solution.py:24
  40.6 2.5 %forward_own.1.kept = f32[2048,256]{1,0:T(8,128)S(1)} custom-call(s32[4,640]{1,0:T(4,128)S(1)} %get-tuple-element.34.refs_0_.listed, bf16[4224,256]{1,0:T(8,128)(2,1)S(1)} %assemble.1.refs_0_, bf16[384,128,128]{2,1,0:T(8,128)(2,1)S(1)} %get-tuple-element.37.refs_1_.refs_4_.refs_8_, bf16[1024,256]{1,0:T(8,128)(2,1)S(1)} %get-tuple-element.40.refs_2_, ...), custom_call_target="tpu_custom_call" | custom-call | flops 1000000 | bytes 131072 | tf_op jit(solution)/shard_map/forward_own/pallas_call | solution.py:280
  43.2 4.5 %collective-permute-done.12.one = bf16[1024,256]{1,0:T(8,128)(2,1)S(1)} collective-permute-done((bf16[1024,256]{1,0:T(8,128)(2,1)S(1)}, bf16[1024,256]{1,0:T(8,128)(2,1)S(1)}, u32[]{:S(2)}, u32[]{:S(2)}) %collective-permute-start.12) | collective-permute-done | bytes 524320 | tf_op jit(solution)/shard_map/ppermute | solution.py:26
  48.7 3.1 %collective-permute-start.14 = (bf16[256,256]{1,0:T(8,128)(2,1)S(1)}, bf16[256,256]{1,0:T(8,128)(2,1)S(1)}, u32[]{:S(2)}, u32[]{:S(2)}) collective-permute-start(bf16[256,256]{1,0:T(8,128)(2,1)S(1)} %get-tuple-element.45), channel_id=1, source_target_pairs={{0,2},{2,0},{1,3},{3,1},{4,6},{6,4},{5,7},{7,5},{8,10},{10,8},{9,1... | collective-permute-start | bytes 393224 | tf_op jit(solution)/shard_map/ppermute | solution.py:24
  53.1 3.3 %collective-permute-start.11 = (bf16[256,256]{1,0:T(8,128)(2,1)S(1)}, bf16[256,256]{1,0:T(8,128)(2,1)S(1)}, u32[]{:S(2)}, u32[]{:S(2)}) collective-permute-start(bf16[256,256]{1,0:T(8,128)(2,1)S(1)} %get-tuple-element.43), channel_id=1, source_target_pairs={{0,8},{8,0},{4,12},{12,4},{1,9},{9,1},{5,13},{13,5},{2,10},{10,2},... | collective-permute-start | bytes 393224 | tf_op jit(solution)/shard_map/ppermute | solution.py:26
  56.6 1.7 %collective-permute-start.17 = (bf16[256,256]{1,0:T(8,128)(2,1)S(1)}, bf16[256,256]{1,0:T(8,128)(2,1)S(1)}, u32[]{:S(2)}, u32[]{:S(2)}) collective-permute-start(bf16[256,256]{1,0:T(8,128)(2,1)S(1)} %get-tuple-element.48), channel_id=1, source_target_pairs={{4,8},{8,4},{12,0},{0,12},{5,9},{9,5},{13,1},{1,13},{6,10},{10,6},... | collective-permute-start | bytes 393224 | tf_op jit(solution)/shard_map/ppermute | solution.py:26
  58.6 2.2 %collective-permute-done.11.refs_0_ = bf16[256,256]{1,0:T(8,128)(2,1)S(1)} collective-permute-done((bf16[256,256]{1,0:T(8,128)(2,1)S(1)}, bf16[256,256]{1,0:T(8,128)(2,1)S(1)}, u32[]{:S(2)}, u32[]{:S(2)}) %collective-permute-start.11) | collective-permute-done | bytes 131104 | tf_op jit(solution)/shard_map/ppermute | solution.py:26
  64.0 3.1 %collective-permute-start.24 = (bf16[384,256]{1,0:T(8,128)(2,1)S(1)}, bf16[384,256]{1,0:T(8,128)(2,1)S(1)}, u32[]{:S(2)}, u32[]{:S(2)}) collective-permute-start(bf16[384,256]{1,0:T(8,128)(2,1)S(1)} %get-tuple-element.54.own), channel_id=1, source_target_pairs={{0,2},{2,0},{1,3},{3,1},{4,6},{6,4},{5,7},{7,5},{8,10},{10,8},{9,1... | collective-permute-start | bytes 589832 | tf_op jit(solution)/shard_map/ppermute | solution.py:24
  67.1 1.6 %collective-permute-start.26 = (bf16[384,256]{1,0:T(8,128)(2,1)S(1)}, bf16[384,256]{1,0:T(8,128)(2,1)S(1)}, u32[]{:S(2)}, u32[]{:S(2)}) collective-permute-start(bf16[384,256]{1,0:T(8,128)(2,1)S(1)} %get-tuple-element.54.own), channel_id=1, source_target_pairs={{0,1},{1,0},{2,3},{3,2},{4,5},{5,4},{6,7},{7,6},{8,9},{9,8},{10,11... | collective-permute-start | bytes 589832 | tf_op jit(solution)/shard_map/ppermute | solution.py:24
  68.7 2.5 %collective-permute-start.19 = (bf16[384,256]{1,0:T(8,128)(2,1)S(1)}, bf16[384,256]{1,0:T(8,128)(2,1)S(1)}, u32[]{:S(2)}, u32[]{:S(2)}) collective-permute-start(bf16[384,256]{1,0:T(8,128)(2,1)S(1)} %get-tuple-element.53.own), channel_id=1, source_target_pairs={{0,8},{8,0},{4,12},{12,4},{1,9},{9,1},{5,13},{13,5},{2,10},{10,2},... | collective-permute-start | bytes 589832 | tf_op jit(solution)/shard_map/ppermute | solution.py:26
  81.0 3.5 %collective-permute-start.23 = (bf16[1152,256]{1,0:T(8,128)(2,1)S(1)}, bf16[1152,256]{1,0:T(8,128)(2,1)S(1)}, u32[]{:S(2)}, u32[]{:S(2)}) collective-permute-start(bf16[1152,256]{1,0:T(8,128)(2,1)S(1)} %gathered_a.1.refs_0_.refs_1_), channel_id=1, source_target_pairs={{1,2},{2,1},{3,0},{0,3},{5,6},{6,5},{7,4},{4,7},{9,10},{10,9},{11,... | collective-permute-start | bytes 1769480 | tf_op jit(solution)/shard_map/ppermute | solution.py:24
  84.4 3.1 %backward_here.1.refs_0_.refs_9_ = f32[4096,256]{1,0:T(8,128)S(1)} custom-call(s32[4,640]{1,0:T(4,128)S(1)} %get-tuple-element.35.refs_1_.listed, bf16[1152,256]{1,0:T(8,128)(2,1)S(1)} %gathered_a.1.refs_0_.refs_1_, bf16[1152,256]{1,0:T(8,128)(2,1)S(1)} %gathered_a.1.refs_0_.refs_1_, bf16[1152,256]{1,0:T(8,128)(2,1)S(1)} %gathered_b.1.refs_2_.refs_3_.refs_5_, ...), custom_call_target="tpu_custom_call" | custom-call | flops 1000000 | bytes 131072 | tf_op jit(solution)/shard_map/backward_here/pallas_call | solution.py:280
  87.5 4.0 %collective-permute-done.29.one_ref.refs_4_.refs_5_.refs_6_ = bf16[1152,256]{1,0:T(8,128)(2,1)S(1)} collective-permute-done((bf16[1152,256]{1,0:T(8,128)(2,1)S(1)}, bf16[1152,256]{1,0:T(8,128)(2,1)S(1)}, u32[]{:S(2)}, u32[]{:S(2)}) %collective-permute-start.29) | collective-permute-done | bytes 589856 | tf_op jit(solution)/shard_map/ppermute | solution.py:26
  94.4 1.6 %collective-permute-start.27 = (bf16[576,256]{1,0:T(8,128)(2,1)S(1)}, bf16[576,256]{1,0:T(8,128)(2,1)S(1)}, u32[]{:S(2)}, u32[]{:S(2)}) collective-permute-start(bf16[576,256]{1,0:T(8,128)(2,1)S(1)} %get-tuple-element.55), channel_id=1, source_target_pairs={{1,2},{2,1},{3,0},{0,3},{5,6},{6,5},{7,4},{4,7},{9,10},{10,9},{11,... | collective-permute-start | bytes 884744 | tf_op jit(solution)/shard_map/ppermute | solution.py:24
  96.0 2.1 %collective-permute-start.28 = (bf16[576,256]{1,0:T(8,128)(2,1)S(1)}, bf16[576,256]{1,0:T(8,128)(2,1)S(1)}, u32[]{:S(2)}, u32[]{:S(2)}) collective-permute-start(bf16[576,256]{1,0:T(8,128)(2,1)S(1)} %get-tuple-element.56), channel_id=1, source_target_pairs={{0,1},{1,0},{2,3},{3,2},{4,5},{5,4},{6,7},{7,6},{8,9},{9,8},{10,11... | collective-permute-start | bytes 884744 | tf_op jit(solution)/shard_map/ppermute | solution.py:24
  98.0 4.4 %backward_near.1.refs_5_ = f32[4096,256]{1,0:T(8,128)S(1)} custom-call(s32[4,640]{1,0:T(4,128)S(1)} %get-tuple-element.35.refs_1_.listed, bf16[1152,256]{1,0:T(8,128)(2,1)S(1)} %collective-permute-done.22.one_ref.refs_0_.refs_1_, bf16[1152,256]{1,0:T(8,128)(2,1)S(1)} %collective-permute-done.22.one_ref.refs_0_.refs_1_, ...), custom_call_target="tpu_custom_call" | custom-call | flops 1000000 | bytes 131072 | tf_op jit(solution)/shard_map/backward_near/pallas_call | solution.py:280
  103.2 2.2 %backward_other.1 = bf16[2048,256]{1,0:T(8,128)(2,1)S(1)} custom-call(s32[4,640]{1,0:T(4,128)S(1)} %get-tuple-element.35.refs_1_.listed, bf16[576,256]{1,0:T(8,128)(2,1)S(1)} %collective-permute-done.27.refs_0_.refs_3_, bf16[576,256]{1,0:T(8,128)(2,1)S(1)} %collective-permute-done.28.refs_1_.refs_4_, ...), custom_call_target="tpu_custom_call" | custom-call | flops 1000000 | bytes 131072 | tf_op jit(solution)/shard_map/backward_other/pallas_call | solution.py:280
  106.1 1.7 %backward_own.1.own = f32[2048,256]{1,0:T(8,128)S(1)} custom-call(s32[4,640]{1,0:T(4,128)S(1)} %get-tuple-element.35.refs_1_.listed, bf16[576,256]{1,0:T(8,128)(2,1)S(1)} %collective-permute-done.27.refs_0_.refs_3_, bf16[576,256]{1,0:T(8,128)(2,1)S(1)} %collective-permute-done.28.refs_1_.refs_4_, ...), custom_call_target="tpu_custom_call" | custom-call | flops 1000000 | bytes 131072 | tf_op jit(solution)/shard_map/backward_own/pallas_call | solution.py:280
  108.7 1.8 %collective-permute-start.35 = (bf16[768,256]{1,0:T(8,128)(2,1)S(1)}, bf16[768,256]{1,0:T(8,128)(2,1)S(1)}, u32[]{:S(2)}, u32[]{:S(2)}) collective-permute-start(bf16[768,256]{1,0:T(8,128)(2,1)S(1)} %get-tuple-element.59), channel_id=1, source_target_pairs={{0,64},{64,0},{32,96},{96,32},{16,80},{80,16},{48,112},{112,48},{1... | collective-permute-start | bytes 1179656 | tf_op jit(solution)/shard_map/ppermute | solution.py:27
  110.5 3.4 %collective-permute-start.36 = (bf16[768,256]{1,0:T(8,128)(2,1)S(1)}, bf16[768,256]{1,0:T(8,128)(2,1)S(1)}, u32[]{:S(2)}, u32[]{:S(2)}) collective-permute-start(bf16[768,256]{1,0:T(8,128)(2,1)S(1)} %get-tuple-element.60.own), channel_id=1, source_target_pairs={{0,32},{32,0},{64,96},{96,64},{16,48},{48,16},{80,112},{112,80},{1... | collective-permute-start | bytes 1179656 | tf_op jit(solution)/shard_map/ppermute | solution.py:27
  114.0 8.3 %collective-permute-done.35.two = bf16[768,256]{1,0:T(8,128)(2,1)S(1)} collective-permute-done((bf16[768,256]{1,0:T(8,128)(2,1)S(1)}, bf16[768,256]{1,0:T(8,128)(2,1)S(1)}, u32[]{:S(2)}, u32[]{:S(2)}) %collective-permute-start.35) | collective-permute-done | bytes 393248 | tf_op jit(solution)/shard_map/ppermute | solution.py:27
  122.3 9.3 %collective-permute-done.36.one = bf16[768,256]{1,0:T(8,128)(2,1)S(1)} collective-permute-done((bf16[768,256]{1,0:T(8,128)(2,1)S(1)}, bf16[768,256]{1,0:T(8,128)(2,1)S(1)}, u32[]{:S(2)}, u32[]{:S(2)}) %collective-permute-start.36) | collective-permute-done | bytes 393248 | tf_op jit(solution)/shard_map/ppermute | solution.py:27
  (77 shorter events, 29.8 us)
Async XLA Ops:
  0.6 12.4 %collective-permute-start.2 = (bf16[512,256]{1,0:T(8,128)(2,1)}, bf16[512,256]{1,0:T(8,128)(2,1)S(1)}, u32[]{:S(2)}, u32[]{:S(2)}) collective-permute-start(bf16[512,256]{1,0:T(8,128)(2,1)} %refs_0_.1), channel_id=1, source_target_pairs={{0,64},{64,0},{32,96},{96,32},{16,80},{80,16},{48,112},{112,48},{1... | collective-permute-start | bytes 786440 | tf_op jit(solution)/shard_map/ppermute | solution.py:27
  3.7 12.5 %collective-permute-start = (bf16[512,256]{1,0:T(8,128)(2,1)}, bf16[512,256]{1,0:T(8,128)(2,1)S(1)}, u32[]{:S(2)}, u32[]{:S(2)}) collective-permute-start(bf16[512,256]{1,0:T(8,128)(2,1)} %refs_0_.1), channel_id=1, source_target_pairs={{0,32},{32,0},{64,96},{96,64},{16,48},{48,16},{80,112},{112,80},{1... | collective-permute-start | bytes 786440 | tf_op jit(solution)/shard_map/ppermute | solution.py:27
  4.3 11.9 %collective-permute-start.1 = (bf16[512,256]{1,0:T(8,128)(2,1)}, bf16[512,256]{1,0:T(8,128)(2,1)S(1)}, u32[]{:S(2)}, u32[]{:S(2)}) collective-permute-start(bf16[512,256]{1,0:T(8,128)(2,1)} %refs_0_.1), channel_id=1, source_target_pairs={{32,64},{64,32},{96,0},{0,96},{48,80},{80,48},{112,16},{16,112},{3... | collective-permute-start | bytes 786440 | tf_op jit(solution)/shard_map/ppermute | solution.py:27
  4.9 11.9 %collective-permute-start.3 = (bf16[512,256]{1,0:T(8,128)(2,1)}, bf16[512,256]{1,0:T(8,128)(2,1)S(1)}, u32[]{:S(2)}, u32[]{:S(2)}) collective-permute-start(bf16[512,256]{1,0:T(8,128)(2,1)} %refs_0_.1), channel_id=1, source_target_pairs={{0,16},{16,0},{32,48},{48,32},{64,80},{80,64},{96,112},{112,96},{1... | collective-permute-start | bytes 786440 | tf_op jit(solution)/shard_map/ppermute | solution.py:31
  21.0 16.4 %collective-permute-start.10 = (bf16[1024,256]{1,0:T(8,128)(2,1)S(1)}, bf16[1024,256]{1,0:T(8,128)(2,1)S(1)}, u32[]{:S(2)}, u32[]{:S(2)}) collective-permute-start(bf16[1024,256]{1,0:T(8,128)(2,1)S(1)} %get-tuple-element.42), channel_id=1, source_target_pairs={{0,8},{8,0},{4,12},{12,4},{1,9},{9,1},{5,13},{13,5},{2,10},{10,2},... | collective-permute-start | bytes 1572872 | tf_op jit(solution)/shard_map/ppermute | solution.py:26
  24.3 16.4 %collective-permute-start.7 = (bf16[1024,256]{1,0:T(8,128)(2,1)S(1)}, bf16[1024,256]{1,0:T(8,128)(2,1)S(1)}, u32[]{:S(2)}, u32[]{:S(2)}) collective-permute-start(bf16[1024,256]{1,0:T(8,128)(2,1)S(1)} %get-tuple-element.38.refs_2_), channel_id=1, source_target_pairs={{0,2},{2,0},{1,3},{3,1},{4,6},{6,4},{5,7},{7,5},{8,10},{10,8},{9,1... | collective-permute-start | bytes 1572872 | tf_op jit(solution)/shard_map/ppermute | solution.py:24
  30.3 17.4 %collective-permute-start.12 = (bf16[1024,256]{1,0:T(8,128)(2,1)S(1)}, bf16[1024,256]{1,0:T(8,128)(2,1)S(1)}, u32[]{:S(2)}, u32[]{:S(2)}) collective-permute-start(bf16[1024,256]{1,0:T(8,128)(2,1)S(1)} %get-tuple-element.39.refs_2_), channel_id=1, source_target_pairs={{0,4},{4,0},{8,12},{12,8},{1,5},{5,1},{9,13},{13,9},{2,6},{6,2},{1... | collective-permute-start | bytes 1572872 | tf_op jit(solution)/shard_map/ppermute | solution.py:26
  32.1 16.3 %collective-permute-start.13 = (bf16[1024,256]{1,0:T(8,128)(2,1)S(1)}, bf16[1024,256]{1,0:T(8,128)(2,1)S(1)}, u32[]{:S(2)}, u32[]{:S(2)}) collective-permute-start(bf16[1024,256]{1,0:T(8,128)(2,1)S(1)} %get-tuple-element.44), channel_id=1, source_target_pairs={{4,8},{8,4},{12,0},{0,12},{5,9},{9,5},{13,1},{1,13},{6,10},{10,6},... | collective-permute-start | bytes 1572872 | tf_op jit(solution)/shard_map/ppermute | solution.py:26
  34.8 18.1 %collective-permute-start.8 = (bf16[1024,256]{1,0:T(8,128)(2,1)S(1)}, bf16[1024,256]{1,0:T(8,128)(2,1)S(1)}, u32[]{:S(2)}, u32[]{:S(2)}) collective-permute-start(bf16[1024,256]{1,0:T(8,128)(2,1)S(1)} %get-tuple-element.40.refs_2_), channel_id=1, source_target_pairs={{0,1},{1,0},{2,3},{3,2},{4,5},{5,4},{6,7},{7,6},{8,9},{9,8},{10,11... | collective-permute-start | bytes 1572872 | tf_op jit(solution)/shard_map/ppermute | solution.py:24
  37.4 15.4 %collective-permute-start.9 = (bf16[1024,256]{1,0:T(8,128)(2,1)S(1)}, bf16[1024,256]{1,0:T(8,128)(2,1)S(1)}, u32[]{:S(2)}, u32[]{:S(2)}) collective-permute-start(bf16[1024,256]{1,0:T(8,128)(2,1)S(1)} %get-tuple-element.41), channel_id=1, source_target_pairs={{1,2},{2,1},{3,0},{0,3},{5,6},{6,5},{7,4},{4,7},{9,10},{10,9},{11,... | collective-permute-start | bytes 1572872 | tf_op jit(solution)/shard_map/ppermute | solution.py:24
  48.7 7.9 %collective-permute-start.14 = (bf16[256,256]{1,0:T(8,128)(2,1)S(1)}, bf16[256,256]{1,0:T(8,128)(2,1)S(1)}, u32[]{:S(2)}, u32[]{:S(2)}) collective-permute-start(bf16[256,256]{1,0:T(8,128)(2,1)S(1)} %get-tuple-element.45), channel_id=1, source_target_pairs={{0,2},{2,0},{1,3},{3,1},{4,6},{6,4},{5,7},{7,5},{8,10},{10,8},{9,1... | collective-permute-start | bytes 393224 | tf_op jit(solution)/shard_map/ppermute | solution.py:24
  51.7 6.9 %collective-permute-start.16 = (bf16[256,256]{1,0:T(8,128)(2,1)S(1)}, bf16[256,256]{1,0:T(8,128)(2,1)S(1)}, u32[]{:S(2)}, u32[]{:S(2)}) collective-permute-start(bf16[256,256]{1,0:T(8,128)(2,1)S(1)} %get-tuple-element.47), channel_id=1, source_target_pairs={{0,1},{1,0},{2,3},{3,2},{4,5},{5,4},{6,7},{7,6},{8,9},{9,8},{10,11... | collective-permute-start | bytes 393224 | tf_op jit(solution)/shard_map/ppermute | solution.py:24
  52.5 6.1 %collective-permute-start.18 = (bf16[256,256]{1,0:T(8,128)(2,1)S(1)}, bf16[256,256]{1,0:T(8,128)(2,1)S(1)}, u32[]{:S(2)}, u32[]{:S(2)}) collective-permute-start(bf16[256,256]{1,0:T(8,128)(2,1)S(1)} %get-tuple-element.49), channel_id=1, source_target_pairs={{1,2},{2,1},{3,0},{0,3},{5,6},{6,5},{7,4},{4,7},{9,10},{10,9},{11,... | collective-permute-start | bytes 393224 | tf_op jit(solution)/shard_map/ppermute | solution.py:24
  53.1 7.7 %collective-permute-start.11 = (bf16[256,256]{1,0:T(8,128)(2,1)S(1)}, bf16[256,256]{1,0:T(8,128)(2,1)S(1)}, u32[]{:S(2)}, u32[]{:S(2)}) collective-permute-start(bf16[256,256]{1,0:T(8,128)(2,1)S(1)} %get-tuple-element.43), channel_id=1, source_target_pairs={{0,8},{8,0},{4,12},{12,4},{1,9},{9,1},{5,13},{13,5},{2,10},{10,2},... | collective-permute-start | bytes 393224 | tf_op jit(solution)/shard_map/ppermute | solution.py:26
  56.6 6.2 %collective-permute-start.17 = (bf16[256,256]{1,0:T(8,128)(2,1)S(1)}, bf16[256,256]{1,0:T(8,128)(2,1)S(1)}, u32[]{:S(2)}, u32[]{:S(2)}) collective-permute-start(bf16[256,256]{1,0:T(8,128)(2,1)S(1)} %get-tuple-element.48), channel_id=1, source_target_pairs={{4,8},{8,4},{12,0},{0,12},{5,9},{9,5},{13,1},{1,13},{6,10},{10,6},... | collective-permute-start | bytes 393224 | tf_op jit(solution)/shard_map/ppermute | solution.py:26
  64.0 9.1 %collective-permute-start.24 = (bf16[384,256]{1,0:T(8,128)(2,1)S(1)}, bf16[384,256]{1,0:T(8,128)(2,1)S(1)}, u32[]{:S(2)}, u32[]{:S(2)}) collective-permute-start(bf16[384,256]{1,0:T(8,128)(2,1)S(1)} %get-tuple-element.54.own), channel_id=1, source_target_pairs={{0,2},{2,0},{1,3},{3,1},{4,6},{6,4},{5,7},{7,5},{8,10},{10,8},{9,1... | collective-permute-start | bytes 589832 | tf_op jit(solution)/shard_map/ppermute | solution.py:24
  67.1 8.0 %collective-permute-start.25 = (bf16[384,256]{1,0:T(8,128)(2,1)S(1)}, bf16[384,256]{1,0:T(8,128)(2,1)S(1)}, u32[]{:S(2)}, u32[]{:S(2)}) collective-permute-start(bf16[384,256]{1,0:T(8,128)(2,1)S(1)} %get-tuple-element.54.own), channel_id=1, source_target_pairs={{1,2},{2,1},{3,0},{0,3},{5,6},{6,5},{7,4},{4,7},{9,10},{10,9},{11,... | collective-permute-start | bytes 589832 | tf_op jit(solution)/shard_map/ppermute | solution.py:24
  67.1 8.2 %collective-permute-start.26 = (bf16[384,256]{1,0:T(8,128)(2,1)S(1)}, bf16[384,256]{1,0:T(8,128)(2,1)S(1)}, u32[]{:S(2)}, u32[]{:S(2)}) collective-permute-start(bf16[384,256]{1,0:T(8,128)(2,1)S(1)} %get-tuple-element.54.own), channel_id=1, source_target_pairs={{0,1},{1,0},{2,3},{3,2},{4,5},{5,4},{6,7},{7,6},{8,9},{9,8},{10,11... | collective-permute-start | bytes 589832 | tf_op jit(solution)/shard_map/ppermute | solution.py:24
  68.7 9.3 %collective-permute-start.19 = (bf16[384,256]{1,0:T(8,128)(2,1)S(1)}, bf16[384,256]{1,0:T(8,128)(2,1)S(1)}, u32[]{:S(2)}, u32[]{:S(2)}) collective-permute-start(bf16[384,256]{1,0:T(8,128)(2,1)S(1)} %get-tuple-element.53.own), channel_id=1, source_target_pairs={{0,8},{8,0},{4,12},{12,4},{1,9},{9,1},{5,13},{13,5},{2,10},{10,2},... | collective-permute-start | bytes 589832 | tf_op jit(solution)/shard_map/ppermute | solution.py:26
  71.3 7.8 %collective-permute-start.20 = (bf16[384,256]{1,0:T(8,128)(2,1)S(1)}, bf16[384,256]{1,0:T(8,128)(2,1)S(1)}, u32[]{:S(2)}, u32[]{:S(2)}) collective-permute-start(bf16[384,256]{1,0:T(8,128)(2,1)S(1)} %get-tuple-element.53.own), channel_id=1, source_target_pairs={{4,8},{8,4},{12,0},{0,12},{5,9},{9,5},{13,1},{1,13},{6,10},{10,6},... | collective-permute-start | bytes 589832 | tf_op jit(solution)/shard_map/ppermute | solution.py:26
  73.1 7.5 %collective-permute-start.21 = (bf16[384,256]{1,0:T(8,128)(2,1)S(1)}, bf16[384,256]{1,0:T(8,128)(2,1)S(1)}, u32[]{:S(2)}, u32[]{:S(2)}) collective-permute-start(bf16[384,256]{1,0:T(8,128)(2,1)S(1)} %get-tuple-element.53.own), channel_id=1, source_target_pairs={{0,4},{4,0},{8,12},{12,8},{1,5},{5,1},{9,13},{13,9},{2,6},{6,2},{1... | collective-permute-start | bytes 589832 | tf_op jit(solution)/shard_map/ppermute | solution.py:26
  75.3 16.2 %collective-permute-start.29 = (bf16[1152,256]{1,0:T(8,128)(2,1)S(1)}, bf16[1152,256]{1,0:T(8,128)(2,1)S(1)}, u32[]{:S(2)}, u32[]{:S(2)}) collective-permute-start(bf16[1152,256]{1,0:T(8,128)(2,1)S(1)} %gathered_b.1.refs_2_.refs_3_.refs_5_), channel_id=1, source_target_pairs={{0,4},{4,0},{8,12},{12,8},{1,5},{5,1},{9,13},{13,9},{2,6},{6,2},{1... | collective-permute-start | bytes 1769480 | tf_op jit(solution)/shard_map/ppermute | solution.py:26
  76.7 15.6 %collective-permute-start.30 = (bf16[1152,256]{1,0:T(8,128)(2,1)S(1)}, bf16[1152,256]{1,0:T(8,128)(2,1)S(1)}, u32[]{:S(2)}, u32[]{:S(2)}) collective-permute-start(bf16[1152,256]{1,0:T(8,128)(2,1)S(1)} %gathered_b.1.refs_2_.refs_3_.refs_5_), channel_id=1, source_target_pairs={{4,8},{8,4},{12,0},{0,12},{5,9},{9,5},{13,1},{1,13},{6,10},{10,6},... | collective-permute-start | bytes 1769480 | tf_op jit(solution)/shard_map/ppermute | solution.py:26
  80.7 13.1 %collective-permute-start.22 = (bf16[1152,256]{1,0:T(8,128)(2,1)S(1)}, bf16[1152,256]{1,0:T(8,128)(2,1)S(1)}, u32[]{:S(2)}, u32[]{:S(2)}) collective-permute-start(bf16[1152,256]{1,0:T(8,128)(2,1)S(1)} %gathered_a.1.refs_0_.refs_1_), channel_id=1, source_target_pairs={{0,1},{1,0},{2,3},{3,2},{4,5},{5,4},{6,7},{7,6},{8,9},{9,8},{10,11... | collective-permute-start | bytes 1769480 | tf_op jit(solution)/shard_map/ppermute | solution.py:24
  81.0 13.4 %collective-permute-start.23 = (bf16[1152,256]{1,0:T(8,128)(2,1)S(1)}, bf16[1152,256]{1,0:T(8,128)(2,1)S(1)}, u32[]{:S(2)}, u32[]{:S(2)}) collective-permute-start(bf16[1152,256]{1,0:T(8,128)(2,1)S(1)} %gathered_a.1.refs_0_.refs_1_), channel_id=1, source_target_pairs={{1,2},{2,1},{3,0},{0,3},{5,6},{6,5},{7,4},{4,7},{9,10},{10,9},{11,... | collective-permute-start | bytes 1769480 | tf_op jit(solution)/shard_map/ppermute | solution.py:24
  92.3 10.1 %collective-permute-start.31 = (bf16[576,256]{1,0:T(8,128)(2,1)S(1)}, bf16[576,256]{1,0:T(8,128)(2,1)S(1)}, u32[]{:S(2)}, u32[]{:S(2)}) collective-permute-start(bf16[576,256]{1,0:T(8,128)(2,1)S(1)} %get-tuple-element.57), channel_id=1, source_target_pairs={{4,8},{8,4},{12,0},{0,12},{5,9},{9,5},{13,1},{1,13},{6,10},{10,6},... | collective-permute-start | bytes 884744 | tf_op jit(solution)/shard_map/ppermute | solution.py:26
  93.8 8.6 %collective-permute-start.32 = (bf16[576,256]{1,0:T(8,128)(2,1)S(1)}, bf16[576,256]{1,0:T(8,128)(2,1)S(1)}, u32[]{:S(2)}, u32[]{:S(2)}) collective-permute-start(bf16[576,256]{1,0:T(8,128)(2,1)S(1)} %get-tuple-element.58), channel_id=1, source_target_pairs={{0,4},{4,0},{8,12},{12,8},{1,5},{5,1},{9,13},{13,9},{2,6},{6,2},{1... | collective-permute-start | bytes 884744 | tf_op jit(solution)/shard_map/ppermute | solution.py:26
  94.4 8.0 %collective-permute-start.27 = (bf16[576,256]{1,0:T(8,128)(2,1)S(1)}, bf16[576,256]{1,0:T(8,128)(2,1)S(1)}, u32[]{:S(2)}, u32[]{:S(2)}) collective-permute-start(bf16[576,256]{1,0:T(8,128)(2,1)S(1)} %get-tuple-element.55), channel_id=1, source_target_pairs={{1,2},{2,1},{3,0},{0,3},{5,6},{6,5},{7,4},{4,7},{9,10},{10,9},{11,... | collective-permute-start | bytes 884744 | tf_op jit(solution)/shard_map/ppermute | solution.py:24
  96.0 7.2 %collective-permute-start.28 = (bf16[576,256]{1,0:T(8,128)(2,1)S(1)}, bf16[576,256]{1,0:T(8,128)(2,1)S(1)}, u32[]{:S(2)}, u32[]{:S(2)}) collective-permute-start(bf16[576,256]{1,0:T(8,128)(2,1)S(1)} %get-tuple-element.56), channel_id=1, source_target_pairs={{0,1},{1,0},{2,3},{3,2},{4,5},{5,4},{6,7},{7,6},{8,9},{9,8},{10,11... | collective-permute-start | bytes 884744 | tf_op jit(solution)/shard_map/ppermute | solution.py:24
  108.7 13.6 %collective-permute-start.35 = (bf16[768,256]{1,0:T(8,128)(2,1)S(1)}, bf16[768,256]{1,0:T(8,128)(2,1)S(1)}, u32[]{:S(2)}, u32[]{:S(2)}) collective-permute-start(bf16[768,256]{1,0:T(8,128)(2,1)S(1)} %get-tuple-element.59), channel_id=1, source_target_pairs={{0,64},{64,0},{32,96},{96,32},{16,80},{80,16},{48,112},{112,48},{1... | collective-permute-start | bytes 1179656 | tf_op jit(solution)/shard_map/ppermute | solution.py:27
  110.5 21.0 %collective-permute-start.36 = (bf16[768,256]{1,0:T(8,128)(2,1)S(1)}, bf16[768,256]{1,0:T(8,128)(2,1)S(1)}, u32[]{:S(2)}, u32[]{:S(2)}) collective-permute-start(bf16[768,256]{1,0:T(8,128)(2,1)S(1)} %get-tuple-element.60.own), channel_id=1, source_target_pairs={{0,32},{32,0},{64,96},{96,64},{16,48},{48,16},{80,112},{112,80},{1... | collective-permute-start | bytes 1179656 | tf_op jit(solution)/shard_map/ppermute | solution.py:27
  113.9 17.6 %collective-permute-start.37 = (bf16[768,256]{1,0:T(8,128)(2,1)S(1)}, bf16[768,256]{1,0:T(8,128)(2,1)S(1)}, u32[]{:S(2)}, u32[]{:S(2)}) collective-permute-start(bf16[768,256]{1,0:T(8,128)(2,1)S(1)} %get-tuple-element.61), channel_id=1, source_target_pairs={{32,64},{64,32},{96,0},{0,96},{48,80},{80,48},{112,16},{16,112},{3... | collective-permute-start | bytes 1179656 | tf_op jit(solution)/shard_map/ppermute | solution.py:27
  (11 other events, 69.4 us)

commit v4 on v3

--- a/solution.py
+++ b/solution.py
@@ -40,6 +40,9 @@
     for place, entry in enumerate(table):
         found = jnp.where(index == place, entry, found)
     return found
+
+
+ROLE = (6, 1, 0, 4, 7, 5, 2, 3)
 
 
 FORWARD = ((0, 16), (16, 32), (32, 48), (48, 64))
@@ -112,7 +115,8 @@
         inner = ring_two ^ (ring_two >> 1)
         source = jnp.where(near, jnp.where(second, 16, 0) + (ring_one >> 1) * 8, jnp.where(second, 8, 0))
         source += half * 4 + inner
-        keys = jnp.where(far, 64, jnp.where(near, 32, 0)) + (1 - other) * 16 + x_away * 4 + (cols & 3)
+        role = pick(((cols >> 1) & 1) * 4 + x_away, ROLE)
+        keys = jnp.where(far, 64, jnp.where(near, 32, 0)) + (1 - other) * 16 + role * 2 + (cols & 1)
         sort_tiles(backward, keys, source, live, BACKWARD)
 
     smem = pl.BlockSpec(memory_space=pltpu.SMEM)
@@ -361,20 +365,33 @@
             out[pl.ds((2 * k + half) * 64, 64)] = total
 
 
-def last_phase(own, received, grad, grad_received, kept, one, two, three):
+def last_phase(own, received, grad, grad_received, by_one, by_two, late_two, late_one, kept):
     total = own[...] + received[...].astype(F32)
+    by_one[pl.ds(0, 512)] = total[0:512].astype(BF)
+    by_two[pl.ds(0, 512)] = total[512:1024].astype(BF)
+    late_two[...] = total[1024:1280].astype(BF)
+    late_one[...] = total[1280:1536].astype(BF)
+    kept[...] = total[1536:2048]
     both = (grad[...] + grad_received[...]).astype(BF)
-    kept[...] = total[0:512]
-    for away, out in ((1, one), (2, two), (3, three)):
-        out[pl.ds(0, 512)] = total[512 * away : 512 * away + 512].astype(BF)
-        out[pl.ds(512, 256)] = both
-
-
-def last_sum(two, one, three, kept, own, features, weight):
-    rows, grads = pl.ds(0, 512), pl.ds(512, 256)
-    total = (kept[...] + two[rows].astype(F32)) + (one[rows].astype(F32) + three[rows].astype(F32))
-    features[...] = total.astype(BF)
-    weight[...] = four(own[grads], one[grads], two[grads], three[grads])
+    by_one[pl.ds(512, 128)] = both[:128]
+    by_two[pl.ds(512, 128)] = both[128:]
+
+
+def last_forward(late_two, by_one, own_one, late_one, by_two, own_two, out_two, out_one):
+    grads = pl.ds(512, 128)
+    for late, got, own, out in ((late_two, by_one, own_one, out_two), (late_one, by_two, own_two, out_one)):
+        out[pl.ds(0, 256)] = (late[...].astype(F32) + got[pl.ds(0, 256)].astype(F32)).astype(BF)
+        out[pl.ds(256, 128)] = (own[grads].astype(F32) + got[grads].astype(F32)).astype(BF)
+
+
+def last_sum(kept, by_one, by_two, late_two, late_one, own_late_two, own_late_one, features, weight):
+    first = kept[pl.ds(0, 256)] + (by_one[pl.ds(256, 256)].astype(F32) + late_two[pl.ds(0, 256)].astype(F32))
+    second = kept[pl.ds(256, 256)] + (by_two[pl.ds(256, 256)].astype(F32) + late_one[pl.ds(0, 256)].astype(F32))
+    features[pl.ds(0, 256)] = first.astype(BF)
+    features[pl.ds(256, 256)] = second.astype(BF)
+    rows = pl.ds(256, 128)
+    weight[pl.ds(0, 128)] = own_late_two[rows].astype(F32) + late_two[rows].astype(F32)
+    weight[pl.ds(128, 128)] = own_late_one[rows].astype(F32) + late_one[rows].astype(F32)
 
 
 def per_device(features, weight, cotangent, tile_values, tile_rows, tile_cols, tile_count):
@@ -447,13 +464,19 @@
     )
     grad_received = swap_core(grad)
     (own_sum,) = aggregate("backward_own", 3, backward, distant, held_tiles, [(0, 16, F32)], True, (sums, 16))
-    kept, by_one, by_two, by_three = local(
-        "last_phase", last_phase, [shape(512, F32), shape(768), shape(768), shape(768)],
+    by_one, by_two, late_two, late_one, kept = local(
+        "last_phase", last_phase, [shape(640), shape(640), shape(256), shape(256), shape(512, F32)],
         own_sum, received, grad, grad_received,
     )
-    one, three, two = ways("x", by_one, by_three, by_two)
+    got_one, got_two = swap(by_one, "x", ONE), swap(by_two, "x", TWO)
+    own_two, own_one = local(
+        "last_forward", last_forward, [shape(384), shape(384)],
+        late_two, got_one, by_one, late_one, got_two, by_two,
+    )
+    late_two, late_one = swap(own_two, "x", TWO), swap(own_one, "x", ONE)
     grad_features, grad_weight = local(
-        "last_sum", last_sum, [shape(512), shape(256, F32)], two, one, three, kept, by_one
+        "last_sum", last_sum, [shape(512), shape(256, F32)],
+        kept, got_one, got_two, late_two, late_one, own_two, own_one,
     )
     return activated, grad_features, grad_weight
 

time: 134 us -> 133 us (level)
  waiting for transfers between devices: 46.6 us -> 44.7 us
    ppermute x6 -> x7, waiting for transfers between devices: 20.2 us -> 17 us  [swap(): lax.ppermute(value, 'row', [(a * 2 + k, b * 2 + k) for k in range(2) for...]
    ppermute x13, starting transfers between devices: 21.8 us -> 20.4 us  [swap(): lax.ppermute(value, 'col', [(y * 4 + a, y * 4 + b) for y in range(4) for...]
    ppermute x6 -> x7, starting transfers between devices: 9.52 us -> 9.73 us  [swap(): lax.ppermute(value, 'row', [(a * 2 + k, b * 2 + k) for k in range(2) for...]
    pallas_call x8 -> x9, Pallas kernels: 3.05 us -> 3.13 us  [local(): pl.pallas_call(body, in_specs=[vmem] * len(operands), out_specs=[vmem] *...]
  transfers between devices with their start and end apart: 38 -> 39, of which waited for: 24 -> 22; matrix products, arithmetic and copies ran while one was open for 0% -> 0% of each run, Pallas kernels for 18% -> 19%
where the time goes in v4:
time: 133 us; the launch traced here: 131 us
  starting transfers between devices  51.5 us (39%)
  waiting for transfers between devices  44.7 us (34%)
  Pallas kernels  32 us (24%)
  between operations  1.53 us (1%)
  local copies, waits for them, and re-layouts  1.38 us (1%)
    pallas_call x8, Pallas kernels, aggregate(): pl.pallas_call(kernel, in_specs=[smem] + [vmem] * (n_pieces + 1 + len(ext...  22.6 us
    ppermute x13, starting transfers between devices, swap(): lax.ppermute(value, 'col', [(y * 4 + a, y * 4 + b) for y in range(4) for...  20.4 us
    ppermute x13, waiting for transfers between devices, swap(): lax.ppermute(value, 'col', [(a * 4 + z, b * 4 + z) for z in range(4) for...  20 us
    ppermute x13, starting transfers between devices, swap(): lax.ppermute(value, 'col', [(a * 4 + z, b * 4 + z) for z in range(4) for...  19.6 us
    ppermute x7, waiting for transfers between devices, swap(): lax.ppermute(value, 'row', [(a * 2 + k, b * 2 + k) for k in range(2) for...  17 us
    ppermute x7, starting transfers between devices, swap(): lax.ppermute(value, 'row', [(a * 2 + k, b * 2 + k) for k in range(2) for...  9.73 us
    ppermute x13, waiting for transfers between devices, swap(): lax.ppermute(value, 'col', [(y * 4 + a, y * 4 + b) for y in range(4) for...  5.98 us
    pallas_call x1, Pallas kernels, load(): pl.pallas_call(kernel, in_specs=[pl.BlockSpec(memory_space=pltpu.HBM)] +...  4.74 us
  transfers between devices with their start and end apart: 39, of which 22 were waited for; matrix products, arithmetic and copies ran while one was open for 0% of the time, Pallas kernels for 19%

profile of v4, /device:TPU:32, one launch (start us, length us, event | category | flops | bytes accessed | tf_op | source)
XLA Modules:
  0.0 131.2 jit_solution(811745644093332423)
XLA Ops:
  0.6 3.1 %collective-permute-start.2 = (bf16[512,256]{1,0:T(8,128)(2,1)}, bf16[512,256]{1,0:T(8,128)(2,1)S(1)}, u32[]{:S(2)}, u32[]{:S(2)}) collective-permute-start(bf16[512,256]{1,0:T(8,128)(2,1)} %refs_0_.1), channel_id=1, source_target_pairs={{0,64},{64,0},{32,96},{96,32},{16,80},{80,16},{48,112},{112,48},{1... | collective-permute-start | bytes 786440 | tf_op jit(solution)/shard_map/ppermute | solution.py:27
  8.2 4.7 %load_tiles.1 = (bf16[384,128,128]{2,1,0:T(8,128)(2,1)S(1)}, s32[8,128]{1,0:T(8,128)S(1)}) custom-call(bf16[384,128,128]{2,1,0:T(8,128)(2,1)} %bitcast.9, s32[4,640]{1,0:T(4,128)S(1)} %get-tuple-element.37.refs_0_.listed, s32[4,640]{1,0:T(4,128)S(1)} %get-tuple-element.38.refs_1_.listed), custom_call_target="tpu_custom_call" | custom-call | bytes 26214400 | tf_op jit(solution)/shard_map/load_tiles/pallas_call | solution.py:150
  13.6 2.6 %collective-permute-done.refs_1_ = bf16[512,256]{1,0:T(8,128)(2,1)S(1)} collective-permute-done((bf16[512,256]{1,0:T(8,128)(2,1)}, bf16[512,256]{1,0:T(8,128)(2,1)S(1)}, u32[]{:S(2)}, u32[]{:S(2)}) %collective-permute-start) | collective-permute-done | bytes 262176 | tf_op jit(solution)/shard_map/ppermute | solution.py:27
  18.3 2.7 %forward_far.1 = (bf16[1024,256]{1,0:T(8,128)(2,1)S(1)}, bf16[1024,256]{1,0:T(8,128)(2,1)S(1)}) custom-call(s32[4,640]{1,0:T(4,128)S(1)} %get-tuple-element.37.refs_0_.listed, bf16[4224,256]{1,0:T(8,128)(2,1)S(1)} %assemble.1.refs_0_, bf16[384,128,128]{2,1,0:T(8,128)(2,1)S(1)} %get-tuple-element.40.refs_1_.refs_4_.refs_8_), custom_call_target="tpu_custom_call" | custom-call | flops 1000000 | bytes 131072 | tf_op jit(solution)/shard_map/forward_far/pallas_call | solution.py:284
  21.0 2.9 %collective-permute-start.10 = (bf16[1024,256]{1,0:T(8,128)(2,1)S(1)}, bf16[1024,256]{1,0:T(8,128)(2,1)S(1)}, u32[]{:S(2)}, u32[]{:S(2)}) collective-permute-start(bf16[1024,256]{1,0:T(8,128)(2,1)S(1)} %get-tuple-element.45), channel_id=1, source_target_pairs={{0,8},{8,0},{4,12},{12,4},{1,9},{9,1},{5,13},{13,5},{2,10},{10,2},... | collective-permute-start | bytes 1572872 | tf_op jit(solution)/shard_map/ppermute | solution.py:26
  23.9 3.6 %collective-permute-start.7 = (bf16[1024,256]{1,0:T(8,128)(2,1)S(1)}, bf16[1024,256]{1,0:T(8,128)(2,1)S(1)}, u32[]{:S(2)}, u32[]{:S(2)}) collective-permute-start(bf16[1024,256]{1,0:T(8,128)(2,1)S(1)} %get-tuple-element.41.refs_2_), channel_id=1, source_target_pairs={{0,2},{2,0},{1,3},{3,1},{4,6},{6,4},{5,7},{7,5},{8,10},{10,8},{9,1... | collective-permute-start | bytes 1572872 | tf_op jit(solution)/shard_map/ppermute | solution.py:24
  27.6 2.7 %forward_near_b.1 = (bf16[1024,256]{1,0:T(8,128)(2,1)S(1)}, bf16[1024,256]{1,0:T(8,128)(2,1)S(1)}) custom-call(s32[4,640]{1,0:T(4,128)S(1)} %get-tuple-element.37.refs_0_.listed, bf16[4224,256]{1,0:T(8,128)(2,1)S(1)} %assemble.1.refs_0_, bf16[384,128,128]{2,1,0:T(8,128)(2,1)S(1)} %get-tuple-element.40.refs_1_.refs_4_.refs_8_, ...), custom_call_target="tpu_custom_call" | custom-call | flops 1000000 | bytes 131072 | tf_op jit(solution)/shard_map/forward_near_b/pallas_call | solution.py:284
  30.7 2.7 %forward_near_a.1 = (bf16[1024,256]{1,0:T(8,128)(2,1)S(1)}, bf16[1024,256]{1,0:T(8,128)(2,1)S(1)}) custom-call(s32[4,640]{1,0:T(4,128)S(1)} %get-tuple-element.37.refs_0_.listed, bf16[4224,256]{1,0:T(8,128)(2,1)S(1)} %assemble.1.refs_0_, bf16[384,128,128]{2,1,0:T(8,128)(2,1)S(1)} %get-tuple-element.40.refs_1_.refs_4_.refs_8_, ...), custom_call_target="tpu_custom_call" | custom-call | flops 1000000 | bytes 131072 | tf_op jit(solution)/shard_map/forward_near_a/pallas_call | solution.py:284
  33.4 1.9 %collective-permute-start.8 = (bf16[1024,256]{1,0:T(8,128)(2,1)S(1)}, bf16[1024,256]{1,0:T(8,128)(2,1)S(1)}, u32[]{:S(2)}, u32[]{:S(2)}) collective-permute-start(bf16[1024,256]{1,0:T(8,128)(2,1)S(1)} %get-tuple-element.43.refs_2_), channel_id=1, source_target_pairs={{0,1},{1,0},{2,3},{3,2},{4,5},{5,4},{6,7},{7,6},{8,9},{9,8},{10,11... | collective-permute-start | bytes 1572872 | tf_op jit(solution)/shard_map/ppermute | solution.py:24
  35.3 2.1 %collective-permute-done.10.refs_4_.two = bf16[1024,256]{1,0:T(8,128)(2,1)S(1)} collective-permute-done((bf16[1024,256]{1,0:T(8,128)(2,1)S(1)}, bf16[1024,256]{1,0:T(8,128)(2,1)S(1)}, u32[]{:S(2)}, u32[]{:S(2)}) %collective-permute-start.10) | collective-permute-done | bytes 524320 | tf_op jit(solution)/shard_map/ppermute | solution.py:26
  40.3 2.5 %forward_own.1.kept = f32[2048,256]{1,0:T(8,128)S(1)} custom-call(s32[4,640]{1,0:T(4,128)S(1)} %get-tuple-element.37.refs_0_.listed, bf16[4224,256]{1,0:T(8,128)(2,1)S(1)} %assemble.1.refs_0_, bf16[384,128,128]{2,1,0:T(8,128)(2,1)S(1)} %get-tuple-element.40.refs_1_.refs_4_.refs_8_, bf16[1024,256]{1,0:T(8,128)(2,1)S(1)} %get-tuple-element.43.refs_2_, ...), custom_call_target="tpu_custom_call" | custom-call | flops 1000000 | bytes 131072 | tf_op jit(solution)/shard_map/forward_own/pallas_call | solution.py:284
  42.9 5.4 %collective-permute-done.12.one = bf16[1024,256]{1,0:T(8,128)(2,1)S(1)} collective-permute-done((bf16[1024,256]{1,0:T(8,128)(2,1)S(1)}, bf16[1024,256]{1,0:T(8,128)(2,1)S(1)}, u32[]{:S(2)}, u32[]{:S(2)}) %collective-permute-start.12) | collective-permute-done | bytes 524320 | tf_op jit(solution)/shard_map/ppermute | solution.py:26
  48.5 3.0 %collective-permute-start.14 = (bf16[256,256]{1,0:T(8,128)(2,1)S(1)}, bf16[256,256]{1,0:T(8,128)(2,1)S(1)}, u32[]{:S(2)}, u32[]{:S(2)}) collective-permute-start(bf16[256,256]{1,0:T(8,128)(2,1)S(1)} %get-tuple-element.48), channel_id=1, source_target_pairs={{0,2},{2,0},{1,3},{3,1},{4,6},{6,4},{5,7},{7,5},{8,10},{10,8},{9,1... | collective-permute-start | bytes 393224 | tf_op jit(solution)/shard_map/ppermute | solution.py:24
  52.9 2.8 %collective-permute-start.11 = (bf16[256,256]{1,0:T(8,128)(2,1)S(1)}, bf16[256,256]{1,0:T(8,128)(2,1)S(1)}, u32[]{:S(2)}, u32[]{:S(2)}) collective-permute-start(bf16[256,256]{1,0:T(8,128)(2,1)S(1)} %get-tuple-element.46), channel_id=1, source_target_pairs={{0,8},{8,0},{4,12},{12,4},{1,9},{9,1},{5,13},{13,5},{2,10},{10,2},... | collective-permute-start | bytes 393224 | tf_op jit(solution)/shard_map/ppermute | solution.py:26
  56.9 2.5 %collective-permute-start.17 = (bf16[256,256]{1,0:T(8,128)(2,1)S(1)}, bf16[256,256]{1,0:T(8,128)(2,1)S(1)}, u32[]{:S(2)}, u32[]{:S(2)}) collective-permute-start(bf16[256,256]{1,0:T(8,128)(2,1)S(1)} %get-tuple-element.51), channel_id=1, source_target_pairs={{4,8},{8,4},{12,0},{0,12},{5,9},{9,5},{13,1},{1,13},{6,10},{10,6},... | collective-permute-start | bytes 393224 | tf_op jit(solution)/shard_map/ppermute | solution.py:26
  64.4 2.6 %collective-permute-start.24 = (bf16[384,256]{1,0:T(8,128)(2,1)S(1)}, bf16[384,256]{1,0:T(8,128)(2,1)S(1)}, u32[]{:S(2)}, u32[]{:S(2)}) collective-permute-start(bf16[384,256]{1,0:T(8,128)(2,1)S(1)} %get-tuple-element.57.own), channel_id=1, source_target_pairs={{0,2},{2,0},{1,3},{3,1},{4,6},{6,4},{5,7},{7,5},{8,10},{10,8},{9,1... | collective-permute-start | bytes 589832 | tf_op jit(solution)/shard_map/ppermute | solution.py:24
  67.0 2.2 %collective-permute-start.25 = (bf16[384,256]{1,0:T(8,128)(2,1)S(1)}, bf16[384,256]{1,0:T(8,128)(2,1)S(1)}, u32[]{:S(2)}, u32[]{:S(2)}) collective-permute-start(bf16[384,256]{1,0:T(8,128)(2,1)S(1)} %get-tuple-element.57.own), channel_id=1, source_target_pairs={{1,2},{2,1},{3,0},{0,3},{5,6},{6,5},{7,4},{4,7},{9,10},{10,9},{11,... | collective-permute-start | bytes 589832 | tf_op jit(solution)/shard_map/ppermute | solution.py:24
  76.6 2.5 %collective-permute-start.30 = (bf16[1152,256]{1,0:T(8,128)(2,1)S(1)}, bf16[1152,256]{1,0:T(8,128)(2,1)S(1)}, u32[]{:S(2)}, u32[]{:S(2)}) collective-permute-start(bf16[1152,256]{1,0:T(8,128)(2,1)S(1)} %gathered_b.1.refs_2_.refs_3_.refs_5_), channel_id=1, source_target_pairs={{4,8},{8,4},{12,0},{0,12},{5,9},{9,5},{13,1},{1,13},{6,10},{10,6},... | collective-permute-start | bytes 1769480 | tf_op jit(solution)/shard_map/ppermute | solution.py:26
  79.5 3.0 %collective-permute-done.21.one = bf16[384,256]{1,0:T(8,128)(2,1)S(1)} collective-permute-done((bf16[384,256]{1,0:T(8,128)(2,1)S(1)}, bf16[384,256]{1,0:T(8,128)(2,1)S(1)}, u32[]{:S(2)}, u32[]{:S(2)}) %collective-permute-start.21) | collective-permute-done | bytes 196640 | tf_op jit(solution)/shard_map/ppermute | solution.py:26
  82.6 1.8 %collective-permute-start.22 = (bf16[1152,256]{1,0:T(8,128)(2,1)S(1)}, bf16[1152,256]{1,0:T(8,128)(2,1)S(1)}, u32[]{:S(2)}, u32[]{:S(2)}) collective-permute-start(bf16[1152,256]{1,0:T(8,128)(2,1)S(1)} %gathered_a.1.refs_0_.refs_1_), channel_id=1, source_target_pairs={{0,1},{1,0},{2,3},{3,2},{4,5},{5,4},{6,7},{7,6},{8,9},{9,8},{10,11... | collective-permute-start | bytes 1769480 | tf_op jit(solution)/shard_map/ppermute | solution.py:24
  84.4 3.1 %backward_here.1.refs_0_.refs_9_ = f32[4096,256]{1,0:T(8,128)S(1)} custom-call(s32[4,640]{1,0:T(4,128)S(1)} %get-tuple-element.38.refs_1_.listed, bf16[1152,256]{1,0:T(8,128)(2,1)S(1)} %gathered_a.1.refs_0_.refs_1_, bf16[1152,256]{1,0:T(8,128)(2,1)S(1)} %gathered_a.1.refs_0_.refs_1_, bf16[1152,256]{1,0:T(8,128)(2,1)S(1)} %gathered_b.1.refs_2_.refs_3_.refs_5_, ...), custom_call_target="tpu_custom_call" | custom-call | flops 1000000 | bytes 131072 | tf_op jit(solution)/shard_map/backward_here/pallas_call | solution.py:284
  87.5 5.5 %collective-permute-done.29.one_ref.refs_4_.refs_5_.refs_6_ = bf16[1152,256]{1,0:T(8,128)(2,1)S(1)} collective-permute-done((bf16[1152,256]{1,0:T(8,128)(2,1)S(1)}, bf16[1152,256]{1,0:T(8,128)(2,1)S(1)}, u32[]{:S(2)}, u32[]{:S(2)}) %collective-permute-start.29) | collective-permute-done | bytes 589856 | tf_op jit(solution)/shard_map/ppermute | solution.py:26
  93.1 2.4 %collective-permute-start.31 = (bf16[576,256]{1,0:T(8,128)(2,1)S(1)}, bf16[576,256]{1,0:T(8,128)(2,1)S(1)}, u32[]{:S(2)}, u32[]{:S(2)}) collective-permute-start(bf16[576,256]{1,0:T(8,128)(2,1)S(1)} %get-tuple-element.60), channel_id=1, source_target_pairs={{4,8},{8,4},{12,0},{0,12},{5,9},{9,5},{13,1},{1,13},{6,10},{10,6},... | collective-permute-start | bytes 884744 | tf_op jit(solution)/shard_map/ppermute | solution.py:26
  97.3 2.1 %collective-permute-start.28 = (bf16[576,256]{1,0:T(8,128)(2,1)S(1)}, bf16[576,256]{1,0:T(8,128)(2,1)S(1)}, u32[]{:S(2)}, u32[]{:S(2)}) collective-permute-start(bf16[576,256]{1,0:T(8,128)(2,1)S(1)} %get-tuple-element.59), channel_id=1, source_target_pairs={{0,1},{1,0},{2,3},{3,2},{4,5},{5,4},{6,7},{7,6},{8,9},{9,8},{10,11... | collective-permute-start | bytes 884744 | tf_op jit(solution)/shard_map/ppermute | solution.py:24
  99.4 4.7 %backward_near.1.refs_5_ = f32[4096,256]{1,0:T(8,128)S(1)} custom-call(s32[4,640]{1,0:T(4,128)S(1)} %get-tuple-element.38.refs_1_.listed, bf16[1152,256]{1,0:T(8,128)(2,1)S(1)} %collective-permute-done.22.one_ref.refs_0_.refs_1_, bf16[1152,256]{1,0:T(8,128)(2,1)S(1)} %collective-permute-done.22.one_ref.refs_0_.refs_1_, ...), custom_call_target="tpu_custom_call" | custom-call | flops 1000000 | bytes 131072 | tf_op jit(solution)/shard_map/backward_near/pallas_call | solution.py:284
  104.8 2.2 %backward_other.1 = bf16[2048,256]{1,0:T(8,128)(2,1)S(1)} custom-call(s32[4,640]{1,0:T(4,128)S(1)} %get-tuple-element.38.refs_1_.listed, bf16[576,256]{1,0:T(8,128)(2,1)S(1)} %collective-permute-done.27.refs_0_.refs_3_, bf16[576,256]{1,0:T(8,128)(2,1)S(1)} %collective-permute-done.28.refs_1_.refs_4_, ...), custom_call_target="tpu_custom_call" | custom-call | flops 1000000 | bytes 131072 | tf_op jit(solution)/shard_map/backward_other/pallas_call | solution.py:284
  107.7 2.0 %backward_own.1.own = f32[2048,256]{1,0:T(8,128)S(1)} custom-call(s32[4,640]{1,0:T(4,128)S(1)} %get-tuple-element.38.refs_1_.listed, bf16[576,256]{1,0:T(8,128)(2,1)S(1)} %collective-permute-done.27.refs_0_.refs_3_, bf16[576,256]{1,0:T(8,128)(2,1)S(1)} %collective-permute-done.28.refs_1_.refs_4_, ...), custom_call_target="tpu_custom_call" | custom-call | flops 1000000 | bytes 131072 | tf_op jit(solution)/shard_map/backward_own/pallas_call | solution.py:284
  111.9 1.9 %collective-permute-start.36 = (bf16[640,256]{1,0:T(8,128)(2,1)S(1)}, bf16[640,256]{1,0:T(8,128)(2,1)S(1)}, u32[]{:S(2)}, u32[]{:S(2)}) collective-permute-start(bf16[640,256]{1,0:T(8,128)(2,1)S(1)} %get-tuple-element.64.own_two), channel_id=1, source_target_pairs={{32,64},{64,32},{96,0},{0,96},{48,80},{80,48},{112,16},{16,112},{3... | collective-permute-start | bytes 983048 | tf_op jit(solution)/shard_map/ppermute | solution.py:27
  113.8 6.3 %collective-permute-done.35.by_one = bf16[640,256]{1,0:T(8,128)(2,1)S(1)} collective-permute-done((bf16[640,256]{1,0:T(8,128)(2,1)S(1)}, bf16[640,256]{1,0:T(8,128)(2,1)S(1)}, u32[]{:S(2)}, u32[]{:S(2)}) %collective-permute-start.35) | collective-permute-done | bytes 327712 | tf_op jit(solution)/shard_map/ppermute | solution.py:27
  120.1 2.4 %collective-permute-done.36.by_two = bf16[640,256]{1,0:T(8,128)(2,1)S(1)} collective-permute-done((bf16[640,256]{1,0:T(8,128)(2,1)S(1)}, bf16[640,256]{1,0:T(8,128)(2,1)S(1)}, u32[]{:S(2)}, u32[]{:S(2)}) %collective-permute-start.36) | collective-permute-done | bytes 327712 | tf_op jit(solution)/shard_map/ppermute | solution.py:27
  122.7 2.0 %collective-permute-start.37 = (bf16[384,256]{1,0:T(8,128)(2,1)S(1)}, bf16[384,256]{1,0:T(8,128)(2,1)S(1)}, u32[]{:S(2)}, u32[]{:S(2)}) collective-permute-start(bf16[384,256]{1,0:T(8,128)(2,1)S(1)} %get-tuple-element.67.own_late_two), channel_id=1, source_target_pairs={{32,64},{64,32},{96,0},{0,96},{48,80},{80,48},{112,16},{16,112},{3... | collective-permute-start | bytes 589832 | tf_op jit(solution)/shard_map/ppermute | solution.py:27
  124.7 5.1 %collective-permute-done.37.late_two = bf16[384,256]{1,0:T(8,128)(2,1)S(1)} collective-permute-done((bf16[384,256]{1,0:T(8,128)(2,1)S(1)}, bf16[384,256]{1,0:T(8,128)(2,1)S(1)}, u32[]{:S(2)}, u32[]{:S(2)}) %collective-permute-start.37) | collective-permute-done | bytes 196640 | tf_op jit(solution)/shard_map/ppermute | solution.py:27
  (80 shorter events, 32.4 us)
Async XLA Ops:
  0.6 12.4 %collective-permute-start.2 = (bf16[512,256]{1,0:T(8,128)(2,1)}, bf16[512,256]{1,0:T(8,128)(2,1)S(1)}, u32[]{:S(2)}, u32[]{:S(2)}) collective-permute-start(bf16[512,256]{1,0:T(8,128)(2,1)} %refs_0_.1), channel_id=1, source_target_pairs={{0,64},{64,0},{32,96},{96,32},{16,80},{80,16},{48,112},{112,48},{1... | collective-permute-start | bytes 786440 | tf_op jit(solution)/shard_map/ppermute | solution.py:27
  3.7 12.5 %collective-permute-start = (bf16[512,256]{1,0:T(8,128)(2,1)}, bf16[512,256]{1,0:T(8,128)(2,1)S(1)}, u32[]{:S(2)}, u32[]{:S(2)}) collective-permute-start(bf16[512,256]{1,0:T(8,128)(2,1)} %refs_0_.1), channel_id=1, source_target_pairs={{0,32},{32,0},{64,96},{96,64},{16,48},{48,16},{80,112},{112,80},{1... | collective-permute-start | bytes 786440 | tf_op jit(solution)/shard_map/ppermute | solution.py:27
  4.3 11.9 %collective-permute-start.1 = (bf16[512,256]{1,0:T(8,128)(2,1)}, bf16[512,256]{1,0:T(8,128)(2,1)S(1)}, u32[]{:S(2)}, u32[]{:S(2)}) collective-permute-start(bf16[512,256]{1,0:T(8,128)(2,1)} %refs_0_.1), channel_id=1, source_target_pairs={{32,64},{64,32},{96,0},{0,96},{48,80},{80,48},{112,16},{16,112},{3... | collective-permute-start | bytes 786440 | tf_op jit(solution)/shard_map/ppermute | solution.py:27
  4.9 11.9 %collective-permute-start.3 = (bf16[512,256]{1,0:T(8,128)(2,1)}, bf16[512,256]{1,0:T(8,128)(2,1)S(1)}, u32[]{:S(2)}, u32[]{:S(2)}) collective-permute-start(bf16[512,256]{1,0:T(8,128)(2,1)} %refs_0_.1), channel_id=1, source_target_pairs={{0,16},{16,0},{32,48},{48,32},{64,80},{80,64},{96,112},{112,96},{1... | collective-permute-start | bytes 786440 | tf_op jit(solution)/shard_map/ppermute | solution.py:31
  21.0 16.4 %collective-permute-start.10 = (bf16[1024,256]{1,0:T(8,128)(2,1)S(1)}, bf16[1024,256]{1,0:T(8,128)(2,1)S(1)}, u32[]{:S(2)}, u32[]{:S(2)}) collective-permute-start(bf16[1024,256]{1,0:T(8,128)(2,1)S(1)} %get-tuple-element.45), channel_id=1, source_target_pairs={{0,8},{8,0},{4,12},{12,4},{1,9},{9,1},{5,13},{13,5},{2,10},{10,2},... | collective-permute-start | bytes 1572872 | tf_op jit(solution)/shard_map/ppermute | solution.py:26
  23.9 16.4 %collective-permute-start.7 = (bf16[1024,256]{1,0:T(8,128)(2,1)S(1)}, bf16[1024,256]{1,0:T(8,128)(2,1)S(1)}, u32[]{:S(2)}, u32[]{:S(2)}) collective-permute-start(bf16[1024,256]{1,0:T(8,128)(2,1)S(1)} %get-tuple-element.41.refs_2_), channel_id=1, source_target_pairs={{0,2},{2,0},{1,3},{3,1},{4,6},{6,4},{5,7},{7,5},{8,10},{10,8},{9,1... | collective-permute-start | bytes 1572872 | tf_op jit(solution)/shard_map/ppermute | solution.py:24
  30.3 17.9 %collective-permute-start.12 = (bf16[1024,256]{1,0:T(8,128)(2,1)S(1)}, bf16[1024,256]{1,0:T(8,128)(2,1)S(1)}, u32[]{:S(2)}, u32[]{:S(2)}) collective-permute-start(bf16[1024,256]{1,0:T(8,128)(2,1)S(1)} %get-tuple-element.42.refs_2_), channel_id=1, source_target_pairs={{0,4},{4,0},{8,12},{12,8},{1,5},{5,1},{9,13},{13,9},{2,6},{6,2},{1... | collective-permute-start | bytes 1572872 | tf_op jit(solution)/shard_map/ppermute | solution.py:26
  30.4 17.8 %collective-permute-start.13 = (bf16[1024,256]{1,0:T(8,128)(2,1)S(1)}, bf16[1024,256]{1,0:T(8,128)(2,1)S(1)}, u32[]{:S(2)}, u32[]{:S(2)}) collective-permute-start(bf16[1024,256]{1,0:T(8,128)(2,1)S(1)} %get-tuple-element.47), channel_id=1, source_target_pairs={{4,8},{8,4},{12,0},{0,12},{5,9},{9,5},{13,1},{1,13},{6,10},{10,6},... | collective-permute-start | bytes 1572872 | tf_op jit(solution)/shard_map/ppermute | solution.py:26
  33.4 19.2 %collective-permute-start.8 = (bf16[1024,256]{1,0:T(8,128)(2,1)S(1)}, bf16[1024,256]{1,0:T(8,128)(2,1)S(1)}, u32[]{:S(2)}, u32[]{:S(2)}) collective-permute-start(bf16[1024,256]{1,0:T(8,128)(2,1)S(1)} %get-tuple-element.43.refs_2_), channel_id=1, source_target_pairs={{0,1},{1,0},{2,3},{3,2},{4,5},{5,4},{6,7},{7,6},{8,9},{9,8},{10,11... | collective-permute-start | bytes 1572872 | tf_op jit(solution)/shard_map/ppermute | solution.py:24
  37.4 15.3 %collective-permute-start.9 = (bf16[1024,256]{1,0:T(8,128)(2,1)S(1)}, bf16[1024,256]{1,0:T(8,128)(2,1)S(1)}, u32[]{:S(2)}, u32[]{:S(2)}) collective-permute-start(bf16[1024,256]{1,0:T(8,128)(2,1)S(1)} %get-tuple-element.44), channel_id=1, source_target_pairs={{1,2},{2,1},{3,0},{0,3},{5,6},{6,5},{7,4},{4,7},{9,10},{10,9},{11,... | collective-permute-start | bytes 1572872 | tf_op jit(solution)/shard_map/ppermute | solution.py:24
  48.5 8.4 %collective-permute-start.14 = (bf16[256,256]{1,0:T(8,128)(2,1)S(1)}, bf16[256,256]{1,0:T(8,128)(2,1)S(1)}, u32[]{:S(2)}, u32[]{:S(2)}) collective-permute-start(bf16[256,256]{1,0:T(8,128)(2,1)S(1)} %get-tuple-element.48), channel_id=1, source_target_pairs={{0,2},{2,0},{1,3},{3,1},{4,6},{6,4},{5,7},{7,5},{8,10},{10,8},{9,1... | collective-permute-start | bytes 393224 | tf_op jit(solution)/shard_map/ppermute | solution.py:24
  51.5 8.0 %collective-permute-start.16 = (bf16[256,256]{1,0:T(8,128)(2,1)S(1)}, bf16[256,256]{1,0:T(8,128)(2,1)S(1)}, u32[]{:S(2)}, u32[]{:S(2)}) collective-permute-start(bf16[256,256]{1,0:T(8,128)(2,1)S(1)} %get-tuple-element.50), channel_id=1, source_target_pairs={{0,1},{1,0},{2,3},{3,2},{4,5},{5,4},{6,7},{7,6},{8,9},{9,8},{10,11... | collective-permute-start | bytes 393224 | tf_op jit(solution)/shard_map/ppermute | solution.py:24
  51.5 8.0 %collective-permute-start.18 = (bf16[256,256]{1,0:T(8,128)(2,1)S(1)}, bf16[256,256]{1,0:T(8,128)(2,1)S(1)}, u32[]{:S(2)}, u32[]{:S(2)}) collective-permute-start(bf16[256,256]{1,0:T(8,128)(2,1)S(1)} %get-tuple-element.52), channel_id=1, source_target_pairs={{1,2},{2,1},{3,0},{0,3},{5,6},{6,5},{7,4},{4,7},{9,10},{10,9},{11,... | collective-permute-start | bytes 393224 | tf_op jit(solution)/shard_map/ppermute | solution.py:24
  52.9 8.0 %collective-permute-start.11 = (bf16[256,256]{1,0:T(8,128)(2,1)S(1)}, bf16[256,256]{1,0:T(8,128)(2,1)S(1)}, u32[]{:S(2)}, u32[]{:S(2)}) collective-permute-start(bf16[256,256]{1,0:T(8,128)(2,1)S(1)} %get-tuple-element.46), channel_id=1, source_target_pairs={{0,8},{8,0},{4,12},{12,4},{1,9},{9,1},{5,13},{13,5},{2,10},{10,2},... | collective-permute-start | bytes 393224 | tf_op jit(solution)/shard_map/ppermute | solution.py:26
  55.8 6.6 %collective-permute-start.15 = (bf16[256,256]{1,0:T(8,128)(2,1)S(1)}, bf16[256,256]{1,0:T(8,128)(2,1)S(1)}, u32[]{:S(2)}, u32[]{:S(2)}) collective-permute-start(bf16[256,256]{1,0:T(8,128)(2,1)S(1)} %get-tuple-element.49), channel_id=1, source_target_pairs={{0,4},{4,0},{8,12},{12,8},{1,5},{5,1},{9,13},{13,9},{2,6},{6,2},{1... | collective-permute-start | bytes 393224 | tf_op jit(solution)/shard_map/ppermute | solution.py:26
  64.4 8.9 %collective-permute-start.24 = (bf16[384,256]{1,0:T(8,128)(2,1)S(1)}, bf16[384,256]{1,0:T(8,128)(2,1)S(1)}, u32[]{:S(2)}, u32[]{:S(2)}) collective-permute-start(bf16[384,256]{1,0:T(8,128)(2,1)S(1)} %get-tuple-element.57.own), channel_id=1, source_target_pairs={{0,2},{2,0},{1,3},{3,1},{4,6},{6,4},{5,7},{7,5},{8,10},{10,8},{9,1... | collective-permute-start | bytes 589832 | tf_op jit(solution)/shard_map/ppermute | solution.py:24
  67.0 8.3 %collective-permute-start.25 = (bf16[384,256]{1,0:T(8,128)(2,1)S(1)}, bf16[384,256]{1,0:T(8,128)(2,1)S(1)}, u32[]{:S(2)}, u32[]{:S(2)}) collective-permute-start(bf16[384,256]{1,0:T(8,128)(2,1)S(1)} %get-tuple-element.57.own), channel_id=1, source_target_pairs={{1,2},{2,1},{3,0},{0,3},{5,6},{6,5},{7,4},{4,7},{9,10},{10,9},{11,... | collective-permute-start | bytes 589832 | tf_op jit(solution)/shard_map/ppermute | solution.py:24
  69.2 6.3 %collective-permute-start.26 = (bf16[384,256]{1,0:T(8,128)(2,1)S(1)}, bf16[384,256]{1,0:T(8,128)(2,1)S(1)}, u32[]{:S(2)}, u32[]{:S(2)}) collective-permute-start(bf16[384,256]{1,0:T(8,128)(2,1)S(1)} %get-tuple-element.57.own), channel_id=1, source_target_pairs={{0,1},{1,0},{2,3},{3,2},{4,5},{5,4},{6,7},{7,6},{8,9},{9,8},{10,11... | collective-permute-start | bytes 589832 | tf_op jit(solution)/shard_map/ppermute | solution.py:24
  69.2 9.9 %collective-permute-start.19 = (bf16[384,256]{1,0:T(8,128)(2,1)S(1)}, bf16[384,256]{1,0:T(8,128)(2,1)S(1)}, u32[]{:S(2)}, u32[]{:S(2)}) collective-permute-start(bf16[384,256]{1,0:T(8,128)(2,1)S(1)} %get-tuple-element.56.own), channel_id=1, source_target_pairs={{0,8},{8,0},{4,12},{12,4},{1,9},{9,1},{5,13},{13,5},{2,10},{10,2},... | collective-permute-start | bytes 589832 | tf_op jit(solution)/shard_map/ppermute | solution.py:26
  70.7 8.9 %collective-permute-start.20 = (bf16[384,256]{1,0:T(8,128)(2,1)S(1)}, bf16[384,256]{1,0:T(8,128)(2,1)S(1)}, u32[]{:S(2)}, u32[]{:S(2)}) collective-permute-start(bf16[384,256]{1,0:T(8,128)(2,1)S(1)} %get-tuple-element.56.own), channel_id=1, source_target_pairs={{4,8},{8,4},{12,0},{0,12},{5,9},{9,5},{13,1},{1,13},{6,10},{10,6},... | collective-permute-start | bytes 589832 | tf_op jit(solution)/shard_map/ppermute | solution.py:26
  73.3 9.2 %collective-permute-start.21 = (bf16[384,256]{1,0:T(8,128)(2,1)S(1)}, bf16[384,256]{1,0:T(8,128)(2,1)S(1)}, u32[]{:S(2)}, u32[]{:S(2)}) collective-permute-start(bf16[384,256]{1,0:T(8,128)(2,1)S(1)} %get-tuple-element.56.own), channel_id=1, source_target_pairs={{0,4},{4,0},{8,12},{12,8},{1,5},{5,1},{9,13},{13,9},{2,6},{6,2},{1... | collective-permute-start | bytes 589832 | tf_op jit(solution)/shard_map/ppermute | solution.py:26
  75.6 17.4 %collective-permute-start.29 = (bf16[1152,256]{1,0:T(8,128)(2,1)S(1)}, bf16[1152,256]{1,0:T(8,128)(2,1)S(1)}, u32[]{:S(2)}, u32[]{:S(2)}) collective-permute-start(bf16[1152,256]{1,0:T(8,128)(2,1)S(1)} %gathered_b.1.refs_2_.refs_3_.refs_5_), channel_id=1, source_target_pairs={{0,4},{4,0},{8,12},{12,8},{1,5},{5,1},{9,13},{13,9},{2,6},{6,2},{1... | collective-permute-start | bytes 1769480 | tf_op jit(solution)/shard_map/ppermute | solution.py:26
  76.6 16.4 %collective-permute-start.30 = (bf16[1152,256]{1,0:T(8,128)(2,1)S(1)}, bf16[1152,256]{1,0:T(8,128)(2,1)S(1)}, u32[]{:S(2)}, u32[]{:S(2)}) collective-permute-start(bf16[1152,256]{1,0:T(8,128)(2,1)S(1)} %gathered_b.1.refs_2_.refs_3_.refs_5_), channel_id=1, source_target_pairs={{4,8},{8,4},{12,0},{0,12},{5,9},{9,5},{13,1},{1,13},{6,10},{10,6},... | collective-permute-start | bytes 1769480 | tf_op jit(solution)/shard_map/ppermute | solution.py:26
  82.6 12.9 %collective-permute-start.22 = (bf16[1152,256]{1,0:T(8,128)(2,1)S(1)}, bf16[1152,256]{1,0:T(8,128)(2,1)S(1)}, u32[]{:S(2)}, u32[]{:S(2)}) collective-permute-start(bf16[1152,256]{1,0:T(8,128)(2,1)S(1)} %gathered_a.1.refs_0_.refs_1_), channel_id=1, source_target_pairs={{0,1},{1,0},{2,3},{3,2},{4,5},{5,4},{6,7},{7,6},{8,9},{9,8},{10,11... | collective-permute-start | bytes 1769480 | tf_op jit(solution)/shard_map/ppermute | solution.py:24
  84.4 12.1 %collective-permute-start.23 = (bf16[1152,256]{1,0:T(8,128)(2,1)S(1)}, bf16[1152,256]{1,0:T(8,128)(2,1)S(1)}, u32[]{:S(2)}, u32[]{:S(2)}) collective-permute-start(bf16[1152,256]{1,0:T(8,128)(2,1)S(1)} %gathered_a.1.refs_0_.refs_1_), channel_id=1, source_target_pairs={{1,2},{2,1},{3,0},{0,3},{5,6},{6,5},{7,4},{4,7},{9,10},{10,9},{11,... | collective-permute-start | bytes 1769480 | tf_op jit(solution)/shard_map/ppermute | solution.py:24
  93.1 11.0 %collective-permute-start.31 = (bf16[576,256]{1,0:T(8,128)(2,1)S(1)}, bf16[576,256]{1,0:T(8,128)(2,1)S(1)}, u32[]{:S(2)}, u32[]{:S(2)}) collective-permute-start(bf16[576,256]{1,0:T(8,128)(2,1)S(1)} %get-tuple-element.60), channel_id=1, source_target_pairs={{4,8},{8,4},{12,0},{0,12},{5,9},{9,5},{13,1},{1,13},{6,10},{10,6},... | collective-permute-start | bytes 884744 | tf_op jit(solution)/shard_map/ppermute | solution.py:26
  95.5 8.6 %collective-permute-start.32 = (bf16[576,256]{1,0:T(8,128)(2,1)S(1)}, bf16[576,256]{1,0:T(8,128)(2,1)S(1)}, u32[]{:S(2)}, u32[]{:S(2)}) collective-permute-start(bf16[576,256]{1,0:T(8,128)(2,1)S(1)} %get-tuple-element.61), channel_id=1, source_target_pairs={{0,4},{4,0},{8,12},{12,8},{1,5},{5,1},{9,13},{13,9},{2,6},{6,2},{1... | collective-permute-start | bytes 884744 | tf_op jit(solution)/shard_map/ppermute | solution.py:26
  96.6 7.5 %collective-permute-start.27 = (bf16[576,256]{1,0:T(8,128)(2,1)S(1)}, bf16[576,256]{1,0:T(8,128)(2,1)S(1)}, u32[]{:S(2)}, u32[]{:S(2)}) collective-permute-start(bf16[576,256]{1,0:T(8,128)(2,1)S(1)} %get-tuple-element.58), channel_id=1, source_target_pairs={{1,2},{2,1},{3,0},{0,3},{5,6},{6,5},{7,4},{4,7},{9,10},{10,9},{11,... | collective-permute-start | bytes 884744 | tf_op jit(solution)/shard_map/ppermute | solution.py:24
  97.3 7.5 %collective-permute-start.28 = (bf16[576,256]{1,0:T(8,128)(2,1)S(1)}, bf16[576,256]{1,0:T(8,128)(2,1)S(1)}, u32[]{:S(2)}, u32[]{:S(2)}) collective-permute-start(bf16[576,256]{1,0:T(8,128)(2,1)S(1)} %get-tuple-element.59), channel_id=1, source_target_pairs={{0,1},{1,0},{2,3},{3,2},{4,5},{5,4},{6,7},{7,6},{8,9},{9,8},{10,11... | collective-permute-start | bytes 884744 | tf_op jit(solution)/shard_map/ppermute | solution.py:24
  110.3 9.8 %collective-permute-start.35 = (bf16[640,256]{1,0:T(8,128)(2,1)S(1)}, bf16[640,256]{1,0:T(8,128)(2,1)S(1)}, u32[]{:S(2)}, u32[]{:S(2)}) collective-permute-start(bf16[640,256]{1,0:T(8,128)(2,1)S(1)} %get-tuple-element.63.own_one), channel_id=1, source_target_pairs={{0,32},{32,0},{64,96},{96,64},{16,48},{48,16},{80,112},{112,80},{1... | collective-permute-start | bytes 983048 | tf_op jit(solution)/shard_map/ppermute | solution.py:27
  111.9 10.7 %collective-permute-start.36 = (bf16[640,256]{1,0:T(8,128)(2,1)S(1)}, bf16[640,256]{1,0:T(8,128)(2,1)S(1)}, u32[]{:S(2)}, u32[]{:S(2)}) collective-permute-start(bf16[640,256]{1,0:T(8,128)(2,1)S(1)} %get-tuple-element.64.own_two), channel_id=1, source_target_pairs={{32,64},{64,32},{96,0},{0,96},{48,80},{80,48},{112,16},{16,112},{3... | collective-permute-start | bytes 983048 | tf_op jit(solution)/shard_map/ppermute | solution.py:27
  122.7 7.1 %collective-permute-start.37 = (bf16[384,256]{1,0:T(8,128)(2,1)S(1)}, bf16[384,256]{1,0:T(8,128)(2,1)S(1)}, u32[]{:S(2)}, u32[]{:S(2)}) collective-permute-start(bf16[384,256]{1,0:T(8,128)(2,1)S(1)} %get-tuple-element.67.own_late_two), channel_id=1, source_target_pairs={{32,64},{64,32},{96,0},{0,96},{48,80},{80,48},{112,16},{16,112},{3... | collective-permute-start | bytes 589832 | tf_op jit(solution)/shard_map/ppermute | solution.py:27
  (12 other events, 76.8 us)

commit v5 on v4

--- a/solution.py
+++ b/solution.py
@@ -45,7 +45,7 @@
 ROLE = (6, 1, 0, 4, 7, 5, 2, 3)
 
 
-FORWARD = ((0, 16), (16, 32), (32, 48), (48, 64))
+FORWARD = ((0, 16), (16, 48), (48, 64))
 BACKWARD = ((0, 32), (32, 64), (64, 80), (80, 96))
 ROOM = 640
 
@@ -421,11 +421,10 @@
 
     a_two, b_two = far = forward_part(0, "forward_far", out(BF, BF))
     a_two, b_two = swap(a_two, "z", FAR), swap(b_two, "y", FAR)
-    b_one, b_three = near_b = forward_part(1, "forward_near_b", out(BF, BF), far[0])
-    b_one, b_three = swap(b_one, "y", ONE), swap(b_three, "y", TWO)
-    a_one, a_three = near_a = forward_part(2, "forward_near_a", out(BF, BF), near_b[0])
-    a_one, a_three = swap(a_one, "z", ONE), swap(a_three, "z", TWO)
-    (kept,) = forward_part(3, "forward_own", [(0, 16, F32)], near_a[0], a_two, b_two)
+    near = forward_part(1, "forward_near", out(BF, BF, BF, BF), far[0])
+    b_one, b_three = swap(near[0], "y", ONE), swap(near[1], "y", TWO)
+    a_one, a_three = swap(near[2], "z", ONE), swap(near[3], "z", TWO)
+    (kept,) = forward_part(2, "forward_own", [(0, 16, F32)], near[0], a_two, b_two)
     shapes = [shape(256, F32), shape(256), shape(256), shape(256)]
     a_own, a_one, a_two, a_three = local("second_phase_a", second_phase(0), shapes, a_two, a_one, a_three, kept)
     b_own, b_one, b_two, b_three = local("second_phase_b", second_phase(1), shapes, b_two, b_one, b_three, kept)

time: 133 us -> 134 us (level)
  Pallas kernels: 32 us -> 24.9 us
  starting transfers between devices: 51.5 us -> 58 us
    pallas_call x8 -> x7, Pallas kernels: 22.6 us -> 15.4 us  [aggregate(): pl.pallas_call(kernel, in_specs=[smem] + [vmem] * (n_pieces + 1 + len(ext...]
    ppermute x13, starting transfers between devices: 19.6 us -> 23.9 us  [swap(): lax.ppermute(value, 'col', [(a * 4 + z, b * 4 + z) for z in range(4) for...]
    ppermute x7, starting transfers between devices: 9.73 us -> 13.1 us  [swap(): lax.ppermute(value, 'row', [(a * 2 + k, b * 2 + k) for k in range(2) for...]
    ppermute x13, waiting for transfers between devices: 20 us -> 22.3 us  [swap(): lax.ppermute(value, 'col', [(a * 4 + z, b * 4 + z) for z in range(4) for...]
  transfers between devices with their start and end apart: 39 -> 39, of which waited for: 22 -> 27; matrix products, arithmetic and copies ran while one was open for 0% -> 0% of each run, Pallas kernels for 19% -> 14%
where the time goes in v5:
time: 134 us; the launch traced here: 132 us
  starting transfers between devices  58 us (43%)
  waiting for transfers between devices  45.9 us (34%)
  Pallas kernels  24.9 us (19%)
  between operations  1.5 us (1%)
  local copies, waits for them, and re-layouts  1.38 us (1%)
    ppermute x13, starting transfers between devices, swap(): lax.ppermute(value, 'col', [(a * 4 + z, b * 4 + z) for z in range(4) for...  23.9 us
    ppermute x13, waiting for transfers between devices, swap(): lax.ppermute(value, 'col', [(a * 4 + z, b * 4 + z) for z in range(4) for...  22.3 us
    ppermute x13, starting transfers between devices, swap(): lax.ppermute(value, 'col', [(y * 4 + a, y * 4 + b) for y in range(4) for...  19.2 us
    ppermute x7, waiting for transfers between devices, swap(): lax.ppermute(value, 'row', [(a * 2 + k, b * 2 + k) for k in range(2) for...  16.4 us
    pallas_call x7, Pallas kernels, aggregate(): pl.pallas_call(kernel, in_specs=[smem] + [vmem] * (n_pieces + 1 + len(ext...  15.4 us
    ppermute x7, starting transfers between devices, swap(): lax.ppermute(value, 'row', [(a * 2 + k, b * 2 + k) for k in range(2) for...  13.1 us
    ppermute x13, waiting for transfers between devices, swap(): lax.ppermute(value, 'col', [(y * 4 + a, y * 4 + b) for y in range(4) for...  4.79 us
    pallas_call x1, Pallas kernels, load(): pl.pallas_call(kernel, in_specs=[pl.BlockSpec(memory_space=pltpu.HBM)] +...  4.74 us
  transfers between devices with their start and end apart: 39, of which 27 were waited for; matrix products, arithmetic and copies ran while one was open for 0% of the time, Pallas kernels for 14%

profile of v5, /device:TPU:32, one launch (start us, length us, event | category | flops | bytes accessed | tf_op | source)
XLA Modules:
  0.0 131.7 jit_solution(5135285912979605350)
XLA Ops:
  0.6 3.1 %collective-permute-start.2 = (bf16[512,256]{1,0:T(8,128)(2,1)}, bf16[512,256]{1,0:T(8,128)(2,1)S(1)}, u32[]{:S(2)}, u32[]{:S(2)}) collective-permute-start(bf16[512,256]{1,0:T(8,128)(2,1)} %refs_0_.1), channel_id=1, source_target_pairs={{0,64},{64,0},{32,96},{96,32},{16,80},{80,16},{48,112},{112,48},{1... | collective-permute-start | bytes 786440 | tf_op jit(solution)/shard_map/ppermute | solution.py:27
  8.3 4.7 %load_tiles.1 = (bf16[384,128,128]{2,1,0:T(8,128)(2,1)S(1)}, s32[8,128]{1,0:T(8,128)S(1)}) custom-call(bf16[384,128,128]{2,1,0:T(8,128)(2,1)} %bitcast.9, s32[4,640]{1,0:T(4,128)S(1)} %get-tuple-element.37.refs_0_.listed, s32[4,640]{1,0:T(4,128)S(1)} %get-tuple-element.38.refs_1_.listed), custom_call_target="tpu_custom_call" | custom-call | bytes 26214400 | tf_op jit(solution)/shard_map/load_tiles/pallas_call | solution.py:150
  13.7 2.5 %collective-permute-done.refs_1_ = bf16[512,256]{1,0:T(8,128)(2,1)S(1)} collective-permute-done((bf16[512,256]{1,0:T(8,128)(2,1)}, bf16[512,256]{1,0:T(8,128)(2,1)S(1)}, u32[]{:S(2)}, u32[]{:S(2)}) %collective-permute-start) | collective-permute-done | bytes 262176 | tf_op jit(solution)/shard_map/ppermute | solution.py:27
  18.3 2.0 %forward_far.1 = (bf16[1024,256]{1,0:T(8,128)(2,1)S(1)}, bf16[1024,256]{1,0:T(8,128)(2,1)S(1)}) custom-call(s32[4,640]{1,0:T(4,128)S(1)} %get-tuple-element.37.refs_0_.listed, bf16[4224,256]{1,0:T(8,128)(2,1)S(1)} %assemble.1.refs_0_, bf16[384,128,128]{2,1,0:T(8,128)(2,1)S(1)} %get-tuple-element.40.refs_1_.refs_4_.refs_8_), custom_call_target="tpu_custom_call" | custom-call | flops 1000000 | bytes 131072 | tf_op jit(solution)/shard_map/forward_far/pallas_call | solution.py:284
  20.3 4.3 %collective-permute-start.10 = (bf16[1024,256]{1,0:T(8,128)(2,1)S(1)}, bf16[1024,256]{1,0:T(8,128)(2,1)S(1)}, u32[]{:S(2)}, u32[]{:S(2)}) collective-permute-start(bf16[1024,256]{1,0:T(8,128)(2,1)S(1)} %get-tuple-element.45), channel_id=1, source_target_pairs={{0,8},{8,0},{4,12},{12,4},{1,9},{9,1},{5,13},{13,5},{2,10},{10,2},... | collective-permute-start | bytes 1572872 | tf_op jit(solution)/shard_map/ppermute | solution.py:26
  24.6 1.6 %collective-permute-start.7 = (bf16[1024,256]{1,0:T(8,128)(2,1)S(1)}, bf16[1024,256]{1,0:T(8,128)(2,1)S(1)}, u32[]{:S(2)}, u32[]{:S(2)}) collective-permute-start(bf16[1024,256]{1,0:T(8,128)(2,1)S(1)} %get-tuple-element.41.refs_2_), channel_id=1, source_target_pairs={{0,2},{2,0},{1,3},{3,1},{4,6},{6,4},{5,7},{7,5},{8,10},{10,8},{9,1... | collective-permute-start | bytes 1572872 | tf_op jit(solution)/shard_map/ppermute | solution.py:24
  26.3 3.4 %forward_near.1 = (bf16[1024,256]{1,0:T(8,128)(2,1)S(1)}, bf16[1024,256]{1,0:T(8,128)(2,1)S(1)}, bf16[1024,256]{1,0:T(8,128)(2,1)S(1)}, bf16[1024,256]{1,0:T(8,128)(2,1)S(1)}) custom-call(s32[4,640]{1,0:T(4,128)S(1)} %get-tuple-element.37.refs_0_.listed, bf16[4224,256]{1,0:T(8,128)(2,1)S(1)} %assemble.1.refs_0_, ...), custom_call_target="tpu_custom_call" | custom-call | flops 1000000 | bytes 131072 | tf_op jit(solution)/shard_map/forward_near/pallas_call | solution.py:284
  29.7 3.7 %collective-permute-start.12 = (bf16[1024,256]{1,0:T(8,128)(2,1)S(1)}, bf16[1024,256]{1,0:T(8,128)(2,1)S(1)}, u32[]{:S(2)}, u32[]{:S(2)}) collective-permute-start(bf16[1024,256]{1,0:T(8,128)(2,1)S(1)} %get-tuple-element.44.refs_2_), channel_id=1, source_target_pairs={{0,4},{4,0},{8,12},{12,8},{1,5},{5,1},{9,13},{13,9},{2,6},{6,2},{1... | collective-permute-start | bytes 1572872 | tf_op jit(solution)/shard_map/ppermute | solution.py:26
  34.4 3.0 %collective-permute-done.10.refs_4_.two = bf16[1024,256]{1,0:T(8,128)(2,1)S(1)} collective-permute-done((bf16[1024,256]{1,0:T(8,128)(2,1)S(1)}, bf16[1024,256]{1,0:T(8,128)(2,1)S(1)}, u32[]{:S(2)}, u32[]{:S(2)}) %collective-permute-start.10) | collective-permute-done | bytes 524320 | tf_op jit(solution)/shard_map/ppermute | solution.py:26
  39.0 2.0 %collective-permute-done.7.refs_3_.two = bf16[1024,256]{1,0:T(8,128)(2,1)S(1)} collective-permute-done((bf16[1024,256]{1,0:T(8,128)(2,1)S(1)}, bf16[1024,256]{1,0:T(8,128)(2,1)S(1)}, u32[]{:S(2)}, u32[]{:S(2)}) %collective-permute-start.7) | collective-permute-done | bytes 524320 | tf_op jit(solution)/shard_map/ppermute | solution.py:24
  42.5 5.3 %collective-permute-done.12.one = bf16[1024,256]{1,0:T(8,128)(2,1)S(1)} collective-permute-done((bf16[1024,256]{1,0:T(8,128)(2,1)S(1)}, bf16[1024,256]{1,0:T(8,128)(2,1)S(1)}, u32[]{:S(2)}, u32[]{:S(2)}) %collective-permute-start.12) | collective-permute-done | bytes 524320 | tf_op jit(solution)/shard_map/ppermute | solution.py:26
  48.7 2.4 %collective-permute-start.14 = (bf16[256,256]{1,0:T(8,128)(2,1)S(1)}, bf16[256,256]{1,0:T(8,128)(2,1)S(1)}, u32[]{:S(2)}, u32[]{:S(2)}) collective-permute-start(bf16[256,256]{1,0:T(8,128)(2,1)S(1)} %get-tuple-element.48), channel_id=1, source_target_pairs={{0,2},{2,0},{1,3},{3,1},{4,6},{6,4},{5,7},{7,5},{8,10},{10,8},{9,1... | collective-permute-start | bytes 393224 | tf_op jit(solution)/shard_map/ppermute | solution.py:24
  53.2 2.8 %collective-permute-start.11 = (bf16[256,256]{1,0:T(8,128)(2,1)S(1)}, bf16[256,256]{1,0:T(8,128)(2,1)S(1)}, u32[]{:S(2)}, u32[]{:S(2)}) collective-permute-start(bf16[256,256]{1,0:T(8,128)(2,1)S(1)} %get-tuple-element.46), channel_id=1, source_target_pairs={{0,8},{8,0},{4,12},{12,4},{1,9},{9,1},{5,13},{13,5},{2,10},{10,2},... | collective-permute-start | bytes 393224 | tf_op jit(solution)/shard_map/ppermute | solution.py:26
  56.3 2.4 %collective-permute-start.17 = (bf16[256,256]{1,0:T(8,128)(2,1)S(1)}, bf16[256,256]{1,0:T(8,128)(2,1)S(1)}, u32[]{:S(2)}, u32[]{:S(2)}) collective-permute-start(bf16[256,256]{1,0:T(8,128)(2,1)S(1)} %get-tuple-element.51), channel_id=1, source_target_pairs={{4,8},{8,4},{12,0},{0,12},{5,9},{9,5},{13,1},{1,13},{6,10},{10,6},... | collective-permute-start | bytes 393224 | tf_op jit(solution)/shard_map/ppermute | solution.py:26
  58.7 2.3 %collective-permute-done.11.refs_0_ = bf16[256,256]{1,0:T(8,128)(2,1)S(1)} collective-permute-done((bf16[256,256]{1,0:T(8,128)(2,1)S(1)}, bf16[256,256]{1,0:T(8,128)(2,1)S(1)}, u32[]{:S(2)}, u32[]{:S(2)}) %collective-permute-start.11) | collective-permute-done | bytes 131104 | tf_op jit(solution)/shard_map/ppermute | solution.py:26
  64.1 2.3 %collective-permute-start.24 = (bf16[384,256]{1,0:T(8,128)(2,1)S(1)}, bf16[384,256]{1,0:T(8,128)(2,1)S(1)}, u32[]{:S(2)}, u32[]{:S(2)}) collective-permute-start(bf16[384,256]{1,0:T(8,128)(2,1)S(1)} %get-tuple-element.57.own), channel_id=1, source_target_pairs={{0,2},{2,0},{1,3},{3,1},{4,6},{6,4},{5,7},{7,5},{8,10},{10,8},{9,1... | collective-permute-start | bytes 589832 | tf_op jit(solution)/shard_map/ppermute | solution.py:24
  66.4 2.4 %collective-permute-start.26 = (bf16[384,256]{1,0:T(8,128)(2,1)S(1)}, bf16[384,256]{1,0:T(8,128)(2,1)S(1)}, u32[]{:S(2)}, u32[]{:S(2)}) collective-permute-start(bf16[384,256]{1,0:T(8,128)(2,1)S(1)} %get-tuple-element.57.own), channel_id=1, source_target_pairs={{0,1},{1,0},{2,3},{3,2},{4,5},{5,4},{6,7},{7,6},{8,9},{9,8},{10,11... | collective-permute-start | bytes 589832 | tf_op jit(solution)/shard_map/ppermute | solution.py:24
  68.8 2.3 %collective-permute-start.19 = (bf16[384,256]{1,0:T(8,128)(2,1)S(1)}, bf16[384,256]{1,0:T(8,128)(2,1)S(1)}, u32[]{:S(2)}, u32[]{:S(2)}) collective-permute-start(bf16[384,256]{1,0:T(8,128)(2,1)S(1)} %get-tuple-element.56.own), channel_id=1, source_target_pairs={{0,8},{8,0},{4,12},{12,4},{1,9},{9,1},{5,13},{13,5},{2,10},{10,2},... | collective-permute-start | bytes 589832 | tf_op jit(solution)/shard_map/ppermute | solution.py:26
  76.9 2.1 %collective-permute-start.30 = (bf16[1152,256]{1,0:T(8,128)(2,1)S(1)}, bf16[1152,256]{1,0:T(8,128)(2,1)S(1)}, u32[]{:S(2)}, u32[]{:S(2)}) collective-permute-start(bf16[1152,256]{1,0:T(8,128)(2,1)S(1)} %gathered_b.1.refs_2_.refs_3_.refs_5_), channel_id=1, source_target_pairs={{4,8},{8,4},{12,0},{0,12},{5,9},{9,5},{13,1},{1,13},{6,10},{10,6},... | collective-permute-start | bytes 1769480 | tf_op jit(solution)/shard_map/ppermute | solution.py:26
  80.5 3.5 %collective-permute-start.23 = (bf16[1152,256]{1,0:T(8,128)(2,1)S(1)}, bf16[1152,256]{1,0:T(8,128)(2,1)S(1)}, u32[]{:S(2)}, u32[]{:S(2)}) collective-permute-start(bf16[1152,256]{1,0:T(8,128)(2,1)S(1)} %gathered_a.1.refs_0_.refs_1_), channel_id=1, source_target_pairs={{1,2},{2,1},{3,0},{0,3},{5,6},{6,5},{7,4},{4,7},{9,10},{10,9},{11,... | collective-permute-start | bytes 1769480 | tf_op jit(solution)/shard_map/ppermute | solution.py:24
  84.0 2.0 %backward_here.1.refs_0_.refs_9_ = f32[4096,256]{1,0:T(8,128)S(1)} custom-call(s32[4,640]{1,0:T(4,128)S(1)} %get-tuple-element.38.refs_1_.listed, bf16[1152,256]{1,0:T(8,128)(2,1)S(1)} %gathered_a.1.refs_0_.refs_1_, bf16[1152,256]{1,0:T(8,128)(2,1)S(1)} %gathered_a.1.refs_0_.refs_1_, bf16[1152,256]{1,0:T(8,128)(2,1)S(1)} %gathered_b.1.refs_2_.refs_3_.refs_5_, ...), custom_call_target="tpu_custom_call" | custom-call | flops 1000000 | bytes 131072 | tf_op jit(solution)/shard_map/backward_here/pallas_call | solution.py:284
  86.0 5.7 %collective-permute-done.29.one_ref.refs_4_.refs_5_.refs_6_ = bf16[1152,256]{1,0:T(8,128)(2,1)S(1)} collective-permute-done((bf16[1152,256]{1,0:T(8,128)(2,1)S(1)}, bf16[1152,256]{1,0:T(8,128)(2,1)S(1)}, u32[]{:S(2)}, u32[]{:S(2)}) %collective-permute-start.29) | collective-permute-done | bytes 589856 | tf_op jit(solution)/shard_map/ppermute | solution.py:26
  92.4 2.9 %collective-permute-start.31 = (bf16[576,256]{1,0:T(8,128)(2,1)S(1)}, bf16[576,256]{1,0:T(8,128)(2,1)S(1)}, u32[]{:S(2)}, u32[]{:S(2)}) collective-permute-start(bf16[576,256]{1,0:T(8,128)(2,1)S(1)} %get-tuple-element.60), channel_id=1, source_target_pairs={{4,8},{8,4},{12,0},{0,12},{5,9},{9,5},{13,1},{1,13},{6,10},{10,6},... | collective-permute-start | bytes 884744 | tf_op jit(solution)/shard_map/ppermute | solution.py:26
  95.6 2.2 %collective-permute-start.28 = (bf16[576,256]{1,0:T(8,128)(2,1)S(1)}, bf16[576,256]{1,0:T(8,128)(2,1)S(1)}, u32[]{:S(2)}, u32[]{:S(2)}) collective-permute-start(bf16[576,256]{1,0:T(8,128)(2,1)S(1)} %get-tuple-element.59), channel_id=1, source_target_pairs={{0,1},{1,0},{2,3},{3,2},{4,5},{5,4},{6,7},{7,6},{8,9},{9,8},{10,11... | collective-permute-start | bytes 884744 | tf_op jit(solution)/shard_map/ppermute | solution.py:24
  97.9 3.3 %backward_near.1.refs_5_ = f32[4096,256]{1,0:T(8,128)S(1)} custom-call(s32[4,640]{1,0:T(4,128)S(1)} %get-tuple-element.38.refs_1_.listed, bf16[1152,256]{1,0:T(8,128)(2,1)S(1)} %collective-permute-done.22.one_ref.refs_0_.refs_1_, bf16[1152,256]{1,0:T(8,128)(2,1)S(1)} %collective-permute-done.22.one_ref.refs_0_.refs_1_, ...), custom_call_target="tpu_custom_call" | custom-call | flops 1000000 | bytes 131072 | tf_op jit(solution)/shard_map/backward_near/pallas_call | solution.py:284
  102.9 1.8 %backward_other.1 = bf16[2048,256]{1,0:T(8,128)(2,1)S(1)} custom-call(s32[4,640]{1,0:T(4,128)S(1)} %get-tuple-element.38.refs_1_.listed, bf16[576,256]{1,0:T(8,128)(2,1)S(1)} %collective-permute-done.27.refs_0_.refs_3_, bf16[576,256]{1,0:T(8,128)(2,1)S(1)} %collective-permute-done.28.refs_1_.refs_4_, ...), custom_call_target="tpu_custom_call" | custom-call | flops 1000000 | bytes 131072 | tf_op jit(solution)/shard_map/backward_other/pallas_call | solution.py:284
  108.1 1.7 %collective-permute-start.35 = (bf16[640,256]{1,0:T(8,128)(2,1)S(1)}, bf16[640,256]{1,0:T(8,128)(2,1)S(1)}, u32[]{:S(2)}, u32[]{:S(2)}) collective-permute-start(bf16[640,256]{1,0:T(8,128)(2,1)S(1)} %get-tuple-element.63.own_one), channel_id=1, source_target_pairs={{0,32},{32,0},{64,96},{96,64},{16,48},{48,16},{80,112},{112,80},{1... | collective-permute-start | bytes 983048 | tf_op jit(solution)/shard_map/ppermute | solution.py:27
  109.8 4.0 %collective-permute-start.36 = (bf16[640,256]{1,0:T(8,128)(2,1)S(1)}, bf16[640,256]{1,0:T(8,128)(2,1)S(1)}, u32[]{:S(2)}, u32[]{:S(2)}) collective-permute-start(bf16[640,256]{1,0:T(8,128)(2,1)S(1)} %get-tuple-element.64.own_two), channel_id=1, source_target_pairs={{32,64},{64,32},{96,0},{0,96},{48,80},{80,48},{112,16},{16,112},{3... | collective-permute-start | bytes 983048 | tf_op jit(solution)/shard_map/ppermute | solution.py:27
  113.9 4.0 %collective-permute-done.35.by_one = bf16[640,256]{1,0:T(8,128)(2,1)S(1)} collective-permute-done((bf16[640,256]{1,0:T(8,128)(2,1)S(1)}, bf16[640,256]{1,0:T(8,128)(2,1)S(1)}, u32[]{:S(2)}, u32[]{:S(2)}) %collective-permute-start.35) | collective-permute-done | bytes 327712 | tf_op jit(solution)/shard_map/ppermute | solution.py:27
  117.9 4.0 %collective-permute-done.36.by_two = bf16[640,256]{1,0:T(8,128)(2,1)S(1)} collective-permute-done((bf16[640,256]{1,0:T(8,128)(2,1)S(1)}, bf16[640,256]{1,0:T(8,128)(2,1)S(1)}, u32[]{:S(2)}, u32[]{:S(2)}) %collective-permute-start.36) | collective-permute-done | bytes 327712 | tf_op jit(solution)/shard_map/ppermute | solution.py:27
  122.0 3.0 %collective-permute-start.37 = (bf16[384,256]{1,0:T(8,128)(2,1)S(1)}, bf16[384,256]{1,0:T(8,128)(2,1)S(1)}, u32[]{:S(2)}, u32[]{:S(2)}) collective-permute-start(bf16[384,256]{1,0:T(8,128)(2,1)S(1)} %get-tuple-element.67.own_late_two), channel_id=1, source_target_pairs={{32,64},{64,32},{96,0},{0,96},{48,80},{80,48},{112,16},{16,112},{3... | collective-permute-start | bytes 589832 | tf_op jit(solution)/shard_map/ppermute | solution.py:27
  125.0 4.7 %collective-permute-done.37.late_two = bf16[384,256]{1,0:T(8,128)(2,1)S(1)} collective-permute-done((bf16[384,256]{1,0:T(8,128)(2,1)S(1)}, bf16[384,256]{1,0:T(8,128)(2,1)S(1)}, u32[]{:S(2)}, u32[]{:S(2)}) %collective-permute-start.37) | collective-permute-done | bytes 196640 | tf_op jit(solution)/shard_map/ppermute | solution.py:27
  (79 shorter events, 32.5 us)
Async XLA Ops:
  0.6 12.4 %collective-permute-start.2 = (bf16[512,256]{1,0:T(8,128)(2,1)}, bf16[512,256]{1,0:T(8,128)(2,1)S(1)}, u32[]{:S(2)}, u32[]{:S(2)}) collective-permute-start(bf16[512,256]{1,0:T(8,128)(2,1)} %refs_0_.1), channel_id=1, source_target_pairs={{0,64},{64,0},{32,96},{96,32},{16,80},{80,16},{48,112},{112,48},{1... | collective-permute-start | bytes 786440 | tf_op jit(solution)/shard_map/ppermute | solution.py:27
  3.7 12.5 %collective-permute-start = (bf16[512,256]{1,0:T(8,128)(2,1)}, bf16[512,256]{1,0:T(8,128)(2,1)S(1)}, u32[]{:S(2)}, u32[]{:S(2)}) collective-permute-start(bf16[512,256]{1,0:T(8,128)(2,1)} %refs_0_.1), channel_id=1, source_target_pairs={{0,32},{32,0},{64,96},{96,64},{16,48},{48,16},{80,112},{112,80},{1... | collective-permute-start | bytes 786440 | tf_op jit(solution)/shard_map/ppermute | solution.py:27
  4.3 11.9 %collective-permute-start.1 = (bf16[512,256]{1,0:T(8,128)(2,1)}, bf16[512,256]{1,0:T(8,128)(2,1)S(1)}, u32[]{:S(2)}, u32[]{:S(2)}) collective-permute-start(bf16[512,256]{1,0:T(8,128)(2,1)} %refs_0_.1), channel_id=1, source_target_pairs={{32,64},{64,32},{96,0},{0,96},{48,80},{80,48},{112,16},{16,112},{3... | collective-permute-start | bytes 786440 | tf_op jit(solution)/shard_map/ppermute | solution.py:27
  4.9 11.9 %collective-permute-start.3 = (bf16[512,256]{1,0:T(8,128)(2,1)}, bf16[512,256]{1,0:T(8,128)(2,1)S(1)}, u32[]{:S(2)}, u32[]{:S(2)}) collective-permute-start(bf16[512,256]{1,0:T(8,128)(2,1)} %refs_0_.1), channel_id=1, source_target_pairs={{0,16},{16,0},{32,48},{48,32},{64,80},{80,64},{96,112},{112,96},{1... | collective-permute-start | bytes 786440 | tf_op jit(solution)/shard_map/ppermute | solution.py:31
  20.3 17.1 %collective-permute-start.10 = (bf16[1024,256]{1,0:T(8,128)(2,1)S(1)}, bf16[1024,256]{1,0:T(8,128)(2,1)S(1)}, u32[]{:S(2)}, u32[]{:S(2)}) collective-permute-start(bf16[1024,256]{1,0:T(8,128)(2,1)S(1)} %get-tuple-element.45), channel_id=1, source_target_pairs={{0,8},{8,0},{4,12},{12,4},{1,9},{9,1},{5,13},{13,5},{2,10},{10,2},... | collective-permute-start | bytes 1572872 | tf_op jit(solution)/shard_map/ppermute | solution.py:26
  24.6 16.4 %collective-permute-start.7 = (bf16[1024,256]{1,0:T(8,128)(2,1)S(1)}, bf16[1024,256]{1,0:T(8,128)(2,1)S(1)}, u32[]{:S(2)}, u32[]{:S(2)}) collective-permute-start(bf16[1024,256]{1,0:T(8,128)(2,1)S(1)} %get-tuple-element.41.refs_2_), channel_id=1, source_target_pairs={{0,2},{2,0},{1,3},{3,1},{4,6},{6,4},{5,7},{7,5},{8,10},{10,8},{9,1... | collective-permute-start | bytes 1572872 | tf_op jit(solution)/shard_map/ppermute | solution.py:24
  29.7 18.1 %collective-permute-start.12 = (bf16[1024,256]{1,0:T(8,128)(2,1)S(1)}, bf16[1024,256]{1,0:T(8,128)(2,1)S(1)}, u32[]{:S(2)}, u32[]{:S(2)}) collective-permute-start(bf16[1024,256]{1,0:T(8,128)(2,1)S(1)} %get-tuple-element.44.refs_2_), channel_id=1, source_target_pairs={{0,4},{4,0},{8,12},{12,8},{1,5},{5,1},{9,13},{13,9},{2,6},{6,2},{1... | collective-permute-start | bytes 1572872 | tf_op jit(solution)/shard_map/ppermute | solution.py:26
  33.4 15.0 %collective-permute-start.13 = (bf16[1024,256]{1,0:T(8,128)(2,1)S(1)}, bf16[1024,256]{1,0:T(8,128)(2,1)S(1)}, u32[]{:S(2)}, u32[]{:S(2)}) collective-permute-start(bf16[1024,256]{1,0:T(8,128)(2,1)S(1)} %get-tuple-element.47), channel_id=1, source_target_pairs={{4,8},{8,4},{12,0},{0,12},{5,9},{9,5},{13,1},{1,13},{6,10},{10,6},... | collective-permute-start | bytes 1572872 | tf_op jit(solution)/shard_map/ppermute | solution.py:26
  33.4 19.5 %collective-permute-start.8 = (bf16[1024,256]{1,0:T(8,128)(2,1)S(1)}, bf16[1024,256]{1,0:T(8,128)(2,1)S(1)}, u32[]{:S(2)}, u32[]{:S(2)}) collective-permute-start(bf16[1024,256]{1,0:T(8,128)(2,1)S(1)} %get-tuple-element.42), channel_id=1, source_target_pairs={{0,1},{1,0},{2,3},{3,2},{4,5},{5,4},{6,7},{7,6},{8,9},{9,8},{10,11... | collective-permute-start | bytes 1572872 | tf_op jit(solution)/shard_map/ppermute | solution.py:24
  37.4 15.5 %collective-permute-start.9 = (bf16[1024,256]{1,0:T(8,128)(2,1)S(1)}, bf16[1024,256]{1,0:T(8,128)(2,1)S(1)}, u32[]{:S(2)}, u32[]{:S(2)}) collective-permute-start(bf16[1024,256]{1,0:T(8,128)(2,1)S(1)} %get-tuple-element.43), channel_id=1, source_target_pairs={{1,2},{2,1},{3,0},{0,3},{5,6},{6,5},{7,4},{4,7},{9,10},{10,9},{11,... | collective-permute-start | bytes 1572872 | tf_op jit(solution)/shard_map/ppermute | solution.py:24
  48.7 7.6 %collective-permute-start.14 = (bf16[256,256]{1,0:T(8,128)(2,1)S(1)}, bf16[256,256]{1,0:T(8,128)(2,1)S(1)}, u32[]{:S(2)}, u32[]{:S(2)}) collective-permute-start(bf16[256,256]{1,0:T(8,128)(2,1)S(1)} %get-tuple-element.48), channel_id=1, source_target_pairs={{0,2},{2,0},{1,3},{3,1},{4,6},{6,4},{5,7},{7,5},{8,10},{10,8},{9,1... | collective-permute-start | bytes 393224 | tf_op jit(solution)/shard_map/ppermute | solution.py:24
  51.1 7.6 %collective-permute-start.16 = (bf16[256,256]{1,0:T(8,128)(2,1)S(1)}, bf16[256,256]{1,0:T(8,128)(2,1)S(1)}, u32[]{:S(2)}, u32[]{:S(2)}) collective-permute-start(bf16[256,256]{1,0:T(8,128)(2,1)S(1)} %get-tuple-element.50), channel_id=1, source_target_pairs={{0,1},{1,0},{2,3},{3,2},{4,5},{5,4},{6,7},{7,6},{8,9},{9,8},{10,11... | collective-permute-start | bytes 393224 | tf_op jit(solution)/shard_map/ppermute | solution.py:24
  52.4 6.3 %collective-permute-start.18 = (bf16[256,256]{1,0:T(8,128)(2,1)S(1)}, bf16[256,256]{1,0:T(8,128)(2,1)S(1)}, u32[]{:S(2)}, u32[]{:S(2)}) collective-permute-start(bf16[256,256]{1,0:T(8,128)(2,1)S(1)} %get-tuple-element.52), channel_id=1, source_target_pairs={{1,2},{2,1},{3,0},{0,3},{5,6},{6,5},{7,4},{4,7},{9,10},{10,9},{11,... | collective-permute-start | bytes 393224 | tf_op jit(solution)/shard_map/ppermute | solution.py:24
  53.2 7.9 %collective-permute-start.11 = (bf16[256,256]{1,0:T(8,128)(2,1)S(1)}, bf16[256,256]{1,0:T(8,128)(2,1)S(1)}, u32[]{:S(2)}, u32[]{:S(2)}) collective-permute-start(bf16[256,256]{1,0:T(8,128)(2,1)S(1)} %get-tuple-element.46), channel_id=1, source_target_pairs={{0,8},{8,0},{4,12},{12,4},{1,9},{9,1},{5,13},{13,5},{2,10},{10,2},... | collective-permute-start | bytes 393224 | tf_op jit(solution)/shard_map/ppermute | solution.py:26
  56.3 6.6 %collective-permute-start.17 = (bf16[256,256]{1,0:T(8,128)(2,1)S(1)}, bf16[256,256]{1,0:T(8,128)(2,1)S(1)}, u32[]{:S(2)}, u32[]{:S(2)}) collective-permute-start(bf16[256,256]{1,0:T(8,128)(2,1)S(1)} %get-tuple-element.51), channel_id=1, source_target_pairs={{4,8},{8,4},{12,0},{0,12},{5,9},{9,5},{13,1},{1,13},{6,10},{10,6},... | collective-permute-start | bytes 393224 | tf_op jit(solution)/shard_map/ppermute | solution.py:26
  64.1 9.3 %collective-permute-start.24 = (bf16[384,256]{1,0:T(8,128)(2,1)S(1)}, bf16[384,256]{1,0:T(8,128)(2,1)S(1)}, u32[]{:S(2)}, u32[]{:S(2)}) collective-permute-start(bf16[384,256]{1,0:T(8,128)(2,1)S(1)} %get-tuple-element.57.own), channel_id=1, source_target_pairs={{0,2},{2,0},{1,3},{3,1},{4,6},{6,4},{5,7},{7,5},{8,10},{10,8},{9,1... | collective-permute-start | bytes 589832 | tf_op jit(solution)/shard_map/ppermute | solution.py:24
  66.4 9.1 %collective-permute-start.25 = (bf16[384,256]{1,0:T(8,128)(2,1)S(1)}, bf16[384,256]{1,0:T(8,128)(2,1)S(1)}, u32[]{:S(2)}, u32[]{:S(2)}) collective-permute-start(bf16[384,256]{1,0:T(8,128)(2,1)S(1)} %get-tuple-element.57.own), channel_id=1, source_target_pairs={{1,2},{2,1},{3,0},{0,3},{5,6},{6,5},{7,4},{4,7},{9,10},{10,9},{11,... | collective-permute-start | bytes 589832 | tf_op jit(solution)/shard_map/ppermute | solution.py:24
  66.4 9.2 %collective-permute-start.26 = (bf16[384,256]{1,0:T(8,128)(2,1)S(1)}, bf16[384,256]{1,0:T(8,128)(2,1)S(1)}, u32[]{:S(2)}, u32[]{:S(2)}) collective-permute-start(bf16[384,256]{1,0:T(8,128)(2,1)S(1)} %get-tuple-element.57.own), channel_id=1, source_target_pairs={{0,1},{1,0},{2,3},{3,2},{4,5},{5,4},{6,7},{7,6},{8,9},{9,8},{10,11... | collective-permute-start | bytes 589832 | tf_op jit(solution)/shard_map/ppermute | solution.py:24
  68.8 10.2 %collective-permute-start.19 = (bf16[384,256]{1,0:T(8,128)(2,1)S(1)}, bf16[384,256]{1,0:T(8,128)(2,1)S(1)}, u32[]{:S(2)}, u32[]{:S(2)}) collective-permute-start(bf16[384,256]{1,0:T(8,128)(2,1)S(1)} %get-tuple-element.56.own), channel_id=1, source_target_pairs={{0,8},{8,0},{4,12},{12,4},{1,9},{9,1},{5,13},{13,5},{2,10},{10,2},... | collective-permute-start | bytes 589832 | tf_op jit(solution)/shard_map/ppermute | solution.py:26
  71.1 8.4 %collective-permute-start.20 = (bf16[384,256]{1,0:T(8,128)(2,1)S(1)}, bf16[384,256]{1,0:T(8,128)(2,1)S(1)}, u32[]{:S(2)}, u32[]{:S(2)}) collective-permute-start(bf16[384,256]{1,0:T(8,128)(2,1)S(1)} %get-tuple-element.56.own), channel_id=1, source_target_pairs={{4,8},{8,4},{12,0},{0,12},{5,9},{9,5},{13,1},{1,13},{6,10},{10,6},... | collective-permute-start | bytes 589832 | tf_op jit(solution)/shard_map/ppermute | solution.py:26
  73.4 6.9 %collective-permute-start.21 = (bf16[384,256]{1,0:T(8,128)(2,1)S(1)}, bf16[384,256]{1,0:T(8,128)(2,1)S(1)}, u32[]{:S(2)}, u32[]{:S(2)}) collective-permute-start(bf16[384,256]{1,0:T(8,128)(2,1)S(1)} %get-tuple-element.56.own), channel_id=1, source_target_pairs={{0,4},{4,0},{8,12},{12,8},{1,5},{5,1},{9,13},{13,9},{2,6},{6,2},{1... | collective-permute-start | bytes 589832 | tf_op jit(solution)/shard_map/ppermute | solution.py:26
  75.7 16.1 %collective-permute-start.29 = (bf16[1152,256]{1,0:T(8,128)(2,1)S(1)}, bf16[1152,256]{1,0:T(8,128)(2,1)S(1)}, u32[]{:S(2)}, u32[]{:S(2)}) collective-permute-start(bf16[1152,256]{1,0:T(8,128)(2,1)S(1)} %gathered_b.1.refs_2_.refs_3_.refs_5_), channel_id=1, source_target_pairs={{0,4},{4,0},{8,12},{12,8},{1,5},{5,1},{9,13},{13,9},{2,6},{6,2},{1... | collective-permute-start | bytes 1769480 | tf_op jit(solution)/shard_map/ppermute | solution.py:26
  76.9 15.5 %collective-permute-start.30 = (bf16[1152,256]{1,0:T(8,128)(2,1)S(1)}, bf16[1152,256]{1,0:T(8,128)(2,1)S(1)}, u32[]{:S(2)}, u32[]{:S(2)}) collective-permute-start(bf16[1152,256]{1,0:T(8,128)(2,1)S(1)} %gathered_b.1.refs_2_.refs_3_.refs_5_), channel_id=1, source_target_pairs={{4,8},{8,4},{12,0},{0,12},{5,9},{9,5},{13,1},{1,13},{6,10},{10,6},... | collective-permute-start | bytes 1769480 | tf_op jit(solution)/shard_map/ppermute | solution.py:26
  80.4 14.8 %collective-permute-start.22 = (bf16[1152,256]{1,0:T(8,128)(2,1)S(1)}, bf16[1152,256]{1,0:T(8,128)(2,1)S(1)}, u32[]{:S(2)}, u32[]{:S(2)}) collective-permute-start(bf16[1152,256]{1,0:T(8,128)(2,1)S(1)} %gathered_a.1.refs_0_.refs_1_), channel_id=1, source_target_pairs={{0,1},{1,0},{2,3},{3,2},{4,5},{5,4},{6,7},{7,6},{8,9},{9,8},{10,11... | collective-permute-start | bytes 1769480 | tf_op jit(solution)/shard_map/ppermute | solution.py:24
  80.5 14.7 %collective-permute-start.23 = (bf16[1152,256]{1,0:T(8,128)(2,1)S(1)}, bf16[1152,256]{1,0:T(8,128)(2,1)S(1)}, u32[]{:S(2)}, u32[]{:S(2)}) collective-permute-start(bf16[1152,256]{1,0:T(8,128)(2,1)S(1)} %gathered_a.1.refs_0_.refs_1_), channel_id=1, source_target_pairs={{1,2},{2,1},{3,0},{0,3},{5,6},{6,5},{7,4},{4,7},{9,10},{10,9},{11,... | collective-permute-start | bytes 1769480 | tf_op jit(solution)/shard_map/ppermute | solution.py:24
  92.4 8.9 %collective-permute-start.31 = (bf16[576,256]{1,0:T(8,128)(2,1)S(1)}, bf16[576,256]{1,0:T(8,128)(2,1)S(1)}, u32[]{:S(2)}, u32[]{:S(2)}) collective-permute-start(bf16[576,256]{1,0:T(8,128)(2,1)S(1)} %get-tuple-element.60), channel_id=1, source_target_pairs={{4,8},{8,4},{12,0},{0,12},{5,9},{9,5},{13,1},{1,13},{6,10},{10,6},... | collective-permute-start | bytes 884744 | tf_op jit(solution)/shard_map/ppermute | solution.py:26
  95.2 7.5 %collective-permute-start.32 = (bf16[576,256]{1,0:T(8,128)(2,1)S(1)}, bf16[576,256]{1,0:T(8,128)(2,1)S(1)}, u32[]{:S(2)}, u32[]{:S(2)}) collective-permute-start(bf16[576,256]{1,0:T(8,128)(2,1)S(1)} %get-tuple-element.61), channel_id=1, source_target_pairs={{0,4},{4,0},{8,12},{12,8},{1,5},{5,1},{9,13},{13,9},{2,6},{6,2},{1... | collective-permute-start | bytes 884744 | tf_op jit(solution)/shard_map/ppermute | solution.py:26
  95.3 7.5 %collective-permute-start.27 = (bf16[576,256]{1,0:T(8,128)(2,1)S(1)}, bf16[576,256]{1,0:T(8,128)(2,1)S(1)}, u32[]{:S(2)}, u32[]{:S(2)}) collective-permute-start(bf16[576,256]{1,0:T(8,128)(2,1)S(1)} %get-tuple-element.58), channel_id=1, source_target_pairs={{1,2},{2,1},{3,0},{0,3},{5,6},{6,5},{7,4},{4,7},{9,10},{10,9},{11,... | collective-permute-start | bytes 884744 | tf_op jit(solution)/shard_map/ppermute | solution.py:24
  95.6 7.3 %collective-permute-start.28 = (bf16[576,256]{1,0:T(8,128)(2,1)S(1)}, bf16[576,256]{1,0:T(8,128)(2,1)S(1)}, u32[]{:S(2)}, u32[]{:S(2)}) collective-permute-start(bf16[576,256]{1,0:T(8,128)(2,1)S(1)} %get-tuple-element.59), channel_id=1, source_target_pairs={{0,1},{1,0},{2,3},{3,2},{4,5},{5,4},{6,7},{7,6},{8,9},{9,8},{10,11... | collective-permute-start | bytes 884744 | tf_op jit(solution)/shard_map/ppermute | solution.py:24
  108.1 9.8 %collective-permute-start.35 = (bf16[640,256]{1,0:T(8,128)(2,1)S(1)}, bf16[640,256]{1,0:T(8,128)(2,1)S(1)}, u32[]{:S(2)}, u32[]{:S(2)}) collective-permute-start(bf16[640,256]{1,0:T(8,128)(2,1)S(1)} %get-tuple-element.63.own_one), channel_id=1, source_target_pairs={{0,32},{32,0},{64,96},{96,64},{16,48},{48,16},{80,112},{112,80},{1... | collective-permute-start | bytes 983048 | tf_op jit(solution)/shard_map/ppermute | solution.py:27
  109.8 12.1 %collective-permute-start.36 = (bf16[640,256]{1,0:T(8,128)(2,1)S(1)}, bf16[640,256]{1,0:T(8,128)(2,1)S(1)}, u32[]{:S(2)}, u32[]{:S(2)}) collective-permute-start(bf16[640,256]{1,0:T(8,128)(2,1)S(1)} %get-tuple-element.64.own_two), channel_id=1, source_target_pairs={{32,64},{64,32},{96,0},{0,96},{48,80},{80,48},{112,16},{16,112},{3... | collective-permute-start | bytes 983048 | tf_op jit(solution)/shard_map/ppermute | solution.py:27
  122.0 7.7 %collective-permute-start.37 = (bf16[384,256]{1,0:T(8,128)(2,1)S(1)}, bf16[384,256]{1,0:T(8,128)(2,1)S(1)}, u32[]{:S(2)}, u32[]{:S(2)}) collective-permute-start(bf16[384,256]{1,0:T(8,128)(2,1)S(1)} %get-tuple-element.67.own_late_two), channel_id=1, source_target_pairs={{32,64},{64,32},{96,0},{0,96},{48,80},{80,48},{112,16},{16,112},{3... | collective-permute-start | bytes 589832 | tf_op jit(solution)/shard_map/ppermute | solution.py:27
  (12 other events, 76.7 us)
